TPU v7x, 32 devices: a whole 2x2x4 slice. The times are simulated.
32 devices in a mesh: grp: 2 (over x), gx: 16 (over z, y, core).
Axes of the slice: x: 2, y: 2, z: 4, core: 2. Of those that a mesh axis runs over, the one named last changes fastest.
Arguments:
- wave_state: float32 [4, 256, 96, 128], P('grp', 'gx'), parts along dimension 0, may hold values from -6 to 6
- layer_fields: float32 [8, 256, 96, 128], P('grp', 'gx'), parts along dimension 0, may hold values from -6 to 6
- source: float32 [512, 96, 128], P(('grp', 'gx')), parts along dimension 0, may hold values from -24 to 24
- filtered: float32 [512, 96, 128], P(('grp', 'gx')), parts along dimension 0, may hold values from -12 to 12
- frequency: float32 [2], P('grp'), parts along dimension 0, may hold values from 0.5 to 1.5
- start_time: float32 [2], P('grp'), parts along dimension 0, may hold values from 0 to 20
- speed_table: float32 [16], replicated, may hold values from 1.4 to 1.8
- speed_index: int32 [32, 12, 16], P('gx'), may hold values from 0 to 15
- pml_mask: int32 [32, 12, 16], P('gx'), may hold values from 0 to 7, as said below
Outputs:
- next_state: float32 [4, 256, 96, 128], P('grp', 'gx'), parts along dimension 0
- next_layer: float32 [8, 256, 96, 128], P('grp', 'gx'), parts along dimension 0
- next_filtered: float32 [512, 96, 128], P(('grp', 'gx')), parts along dimension 0
- filter_norm: float32 [2], P('grp'), parts along dimension 0
There are 2 independent parts, one for each index of `grp`. A program takes and returns all parts, laid end to end along the dimension named above; an argument that names none is the same for every part. Nothing has to cross between parts.
Inputs may be any that keep to these rules, and one draw needn't show every extreme that they name: `pml_mask`: bit d of a block's value is 1 exactly where the block lies in the absorbing layer of a grid face normal to dimension d; the layer at each of the six faces is 2 to 4 blocks thick.
All inputs are finite; a program needn't handle non-finite values.
Results may differ from a plain program's by a relative error of at most 0.000068.
Values sent between devices are 32-bit elements; how exact they have to be, the bound alone decides.
No kernel may reach another device: no remote copies, remote signals or barrier semaphores. Data moves between devices by JAX's collectives and lax.ppermute only.
A program may use at most 64 MiB of HBM per device.

v0:
```python
import math

import jax
import jax.numpy as jnp
from jax import lax
from jax.sharding import PartitionSpec as P

BLK = 8
STEPS = 3


TIME_STEP = 0.25
DAMP_PEAK = 1.5
STENCIL = (-205.0 / 72.0, 8.0 / 5.0, -1.0 / 5.0, 8.0 / 315.0, -1.0 / 560.0)


def with_halo(cells, sides, width):
    for axis, dim in sides:
        count = lax.axis_size(axis)
        ends = count - 1
        head = lax.slice_in_dim(cells, 0, width, axis=dim)
        tail = lax.slice_in_dim(cells, cells.shape[dim] - width, cells.shape[dim], axis=dim)
        cells = jnp.concatenate(
            [
                lax.ppermute(tail, axis, [(i, (i + 1) % count) for i in range(ends)]),
                cells,
                lax.ppermute(head, axis, [((i + 1) % count, i) for i in range(ends)]),
            ],
            axis=dim,
        )
    return cells


def expand(blocks, factor):
    first_len, second_len, third_len = blocks.shape
    wide_len = third_len * factor
    cell_block = jnp.arange(wide_len, dtype=jnp.int32) // factor
    block_ids = jnp.arange(third_len, dtype=jnp.int32)
    spread = (block_ids[:, None] == cell_block[None, :]).astype(jnp.float32)
    flat = blocks.reshape(first_len * second_len, third_len)
    widened_last = jnp.dot(
        flat, spread, precision=lax.Precision.HIGHEST, preferred_element_type=jnp.float32
    )
    widened_last = widened_last.reshape(first_len, second_len, wide_len)
    widened = jnp.broadcast_to(
        widened_last[:, None, :, None, :], (first_len, factor, second_len, factor, wide_len)
    )
    return widened.reshape(first_len * factor, second_len * factor, wide_len)


def speed_squares(speed_index, speed_table):
    levels = jnp.arange(speed_table.shape[0], dtype=jnp.int32)
    picked = jnp.where(speed_index[..., None] == levels, speed_table, jnp.zeros_like(speed_table))
    speeds = jnp.sum(picked, axis=-1)
    return speeds * speeds


def layer_bits(pml_mask):
    return [
        expand((pml_mask // 2**direction % 2).astype(jnp.float32), BLK) for direction in range(3)
    ]


def layer_terms(bits):
    damp_rates = [DAMP_PEAK * bit_field for bit_field in bits]
    damping = damp_rates[0] + damp_rates[1] + damp_rates[2]
    pairing = (
        damp_rates[0] * damp_rates[1]
        + damp_rates[1] * damp_rates[2]
        + damp_rates[2] * damp_rates[0]
    )
    retention = [jnp.exp(-TIME_STEP * rate_field) for rate_field in damp_rates]
    decay_factor = jnp.exp(-TIME_STEP * damping)
    return (damping, pairing, retention, decay_factor)


def pad_along(field, dimension):
    widths = [(0, 0), (0, 0), (0, 0)]
    widths[dimension] = (4, 4)
    return jnp.pad(field, widths)


def along_axis(padded, center_count, dimension):
    accumulated = STENCIL[0] * lax.slice_in_dim(padded, 4, 4 + center_count, axis=dimension)
    for offset in range(1, 5):
        upper = lax.slice_in_dim(padded, 4 + offset, 4 + offset + center_count, axis=dimension)
        lower = lax.slice_in_dim(padded, 4 - offset, 4 - offset + center_count, axis=dimension)
        accumulated = accumulated + STENCIL[offset] * (upper + lower)
    return accumulated


def advance(
    second_diffs,
    displace,
    previous,
    memory,
    stiff_memory,
    source,
    speed_square,
    bits,
    layer_consts,
    forcing_phase,
):
    damping, pairing, retention, decay_factor = layer_consts
    memory = [
        retention[direction] * memory[direction]
        + (1.0 - retention[direction]) * second_diffs[direction]
        for direction in range(3)
    ]
    stiff_memory = decay_factor * stiff_memory + TIME_STEP * pairing * displace
    layered = bits[0] * memory[0] + bits[1] * memory[1] + bits[2] * memory[2]
    acceleration = (
        speed_square * (second_diffs[0] + second_diffs[1] + second_diffs[2] - layered)
        - pairing * displace
        - damping * stiff_memory
        - source * forcing_phase
    )
    half_damp = 0.5 * TIME_STEP * damping
    updated = (
        2.0 * displace - (1.0 - half_damp) * previous + TIME_STEP * TIME_STEP * acceleration
    ) / (1.0 + half_damp)
    return (updated, memory, stiff_memory)


def filter_weight(angular, start_clock, count):
    return (
        TIME_STEP
        * angular
        / math.pi
        * (jnp.cos(angular * (start_clock + count * TIME_STEP)) - 0.25)
    )


def side_diffs(padded, displace):
    row_count = padded.shape[0] - 8
    return [
        along_axis(padded, row_count, 0),
        along_axis(pad_along(displace, 1), displace.shape[1], 1),
        along_axis(pad_along(displace, 2), displace.shape[2], 2),
    ]


def body(
    wave_state,
    layer_fields,
    source,
    filtered,
    frequency,
    start_time,
    speed_table,
    speed_index,
    pml_mask,
):
    angular = frequency[0]
    start_clock = start_time[0]
    bits = layer_bits(pml_mask)
    speed_square = expand(speed_squares(speed_index, speed_table), BLK)
    layer_consts = layer_terms(bits)
    displace = wave_state[0]
    previous = wave_state[1]
    memory = [layer_fields[0], layer_fields[1], layer_fields[2]]
    stiff_memory = layer_fields[3]
    for step_number in range(STEPS):
        padded = with_halo(displace, (("gx", 0),), 4)
        second_diffs = side_diffs(padded, displace)
        forcing_phase = jnp.cos(angular * (start_clock + step_number * TIME_STEP))
        updated, memory, stiff_memory = advance(
            second_diffs,
            displace,
            previous,
            memory,
            stiff_memory,
            source,
            speed_square,
            bits,
            layer_consts,
            forcing_phase,
        )
        previous = displace
        displace = updated
        filtered = filtered + filter_weight(angular, start_clock, step_number + 1) * displace
    local_sum = jnp.sum(filtered * filtered)
    total_sum = lax.psum(local_sum, "gx")
    filter_norm = jnp.sqrt(total_sum / (filtered.size * lax.axis_size("gx")) + 1e-06)
    return (
        jnp.stack([displace, previous]),
        jnp.stack(memory + [stiff_memory]),
        filtered,
        filter_norm.reshape(1),
    )


def solution(mesh):
    placed = (
        P("grp", "gx", None, None),
        P("grp", "gx", None, None),
        P(("grp", "gx"), None, None),
        P(("grp", "gx"), None, None),
        P("grp"),
        P("grp"),
        P(),
        P("gx", None, None),
        P("gx", None, None),
    )
    return jax.shard_map(
        body,
        mesh=mesh,
        in_specs=placed,
        out_specs=(
            P("grp", "gx", None, None),
            P("grp", "gx", None, None),
            P(("grp", "gx"), None, None),
            P("grp"),
        ),
        check_vma=False,
    )
```

profile of v0, /device:TPU:0, one launch (start us, length us, event | category | flops | bytes accessed | tf_op | source)
XLA Modules:
  0.0 135.8 jit_solution(5158814040780560594)
XLA Ops:
  0.6 1.2 slice_bitcast_fusion.2
  1.8 1.3 collective-permute-start
  3.1 3.7 %collective-permute-start.1 = (f32[4,96,128]{2,1,0:T(8,128)S(1)}, f32[4,96,128]{2,1,0:T(8,128)}, u32[]{:S(2)}, u32[]{:S(2)}) collective-permute-start(f32[4,96,128]{2,1,0:T(8,128)S(1)} %get-tuple-element.23), channel_id=1, source_target_pairs={{0,1},{1,2},{2,3},{3,4},{4,5},{5,6},{6,7},{7,8},{8,9},{9,10},{10,1... | collective-permute-start | bytes 589832 | tf_op jit(solution)/shard_map/ppermute | solution.py:25
  6.9 2.1 %slice_bitcast_fusion = f32[16,96,128]{2,1,0:T(8,128)} fusion(f32[2,16,96,128]{3,2,1,0:T(8,128)} %param.9), kind=kLoop, calls=%fused_computation.209 | loop fusion | bytes 1572864 | tf_op jit(solution)/shard_map/squeeze | solution.py:159
  10.3 0.9 copy.20
  11.2 0.8 fusion.119
  12.0 0.9 select_reduce_fusion
  13.8 16.7 %fusion.96 = (f32[16,96,128]{2,1,0:T(8,128)S(1)}, f32[16,96,128]{2,1,0:T(8,128)}, f32[16,96,128]{2,1,0:T(8,128)}, f32[16,96,128]{2,1,0:T(8,128)}) fusion(f32[16,96,128]{2,1,0:T(8,128)S(1)} %copy-done.12, f32[16,96,128]{2,1,0:T(8,128)S(1)} %bitcast.124, f32[16,96,128]{2,1,0:T(8,128)S(1)} %bitcast.112, f32[16,96,128]{2,1,0:T(8,128)S(1)} %bitcast.116, ...), kind=kLoop, calls=%fused_computation.169 | loop fusion | flops 19267584 | bytes 12976132 | tf_op jit(solution)/shard_map/div | solution.py:119
  30.6 0.9 copy-done.10
  31.5 0.8 fusion.140
  32.3 1.3 collective-permute-start.2
  33.6 4.5 %collective-permute-start.3 = (f32[4,96,128]{2,1,0:T(8,128)}, f32[4,96,128]{2,1,0:T(8,128)S(1)}, u32[]{:S(2)}, u32[]{:S(2)}) collective-permute-start(f32[4,96,128]{2,1,0:T(8,128)} %get-tuple-element.27), channel_id=1, source_target_pairs={{0,1},{1,2},{2,3},{3,4},{4,5},{5,6},{6,7},{7,8},{8,9},{9,10},{10,1... | collective-permute-start | bytes 589832 | tf_op jit(solution)/shard_map/ppermute | solution.py:25
  38.1 1.2 collective-permute-done.3
  39.3 18.8 %fusion.110 = (f32[1,16,96,128]{3,2,1,0:T(8,128)}, f32[16,96,128]{2,1,0:T(8,128)S(1)}, f32[16,96,128]{2,1,0:T(8,128)}, f32[16,96,128]{2,1,0:T(8,128)}, f32[16,96,128]{2,1,0:T(8,128)}) fusion(f32[16,96,128]{2,1,0:T(8,128)} %copy-done.10, f32[4,16,96,128]{3,2,1,0:T(8,128)S(1)} %copy-done, f32[16,96,128]{2,1,0:T(8,128)} %bitcast.117, ...), kind=kLoop, calls=%fused_computation.216 | loop fusion | flops 22216704 | bytes 15335428 | tf_op jit(solution)/shard_map/stack | solution.py:187
  58.1 0.9 copy-done.11
  59.0 0.8 fusion.139
  59.7 1.3 collective-permute-start.4
  61.0 7.9 %collective-permute-start.5 = (f32[4,96,128]{2,1,0:T(8,128)}, f32[4,96,128]{2,1,0:T(8,128)S(1)}, u32[]{:S(2)}, u32[]{:S(2)}) collective-permute-start(f32[4,96,128]{2,1,0:T(8,128)} %get-tuple-element.25), channel_id=1, source_target_pairs={{0,1},{1,2},{2,3},{3,4},{4,5},{5,6},{6,7},{7,8},{8,9},{9,10},{10,1... | collective-permute-start | bytes 589832 | tf_op jit(solution)/shard_map/ppermute | solution.py:25
  69.1 1.1 collective-permute-done.5
  70.2 19.7 %multiply_reduce_fusion = (f32[]{:T(128)}, f32[16,96,128]{2,1,0:T(8,128)}, f32[16,96,128]{2,1,0:T(8,128)}, f32[16,96,128]{2,1,0:T(8,128)}, f32[16,96,128]{2,1,0:T(8,128)}, /*index=5*/f32[16,96,128]{2,1,0:T(8,128)}) fusion(f32[]{:T(128)S(6)} %mul.509, f32[16,96,128]{2,1,0:T(8,128)} %copy-done.11, f32[]{:T(128)S(6)} %mul.505, f32[16,96,128]{2,1,0:T(8,128)} %param.12, ...), kind=kLoop, calls=%fused_computation.171 | loop fusion | flops 25559040 | bytes 19267604 | tf_op jit(solution)/shard_map/reduce_sum | solution.py:182
  89.9 35.0 %psum.7 = f32[]{:T(128)} all-reduce(f32[]{:T(128)} %get-tuple-element.4), channel_id=1, replica_groups=mesh['grp'=2,'gx'=16] {'gx'}, use_global_device_ids=true, to_apply=%region_2.3 | all-reduce | flops 1 | bytes 8 | tf_op jit(solution)/shard_map/psum | solution.py:183
  125.6 2.8 %pad_maximum_fusion.1 = f32[2,16,96,128]{3,2,1,0:T(8,128)} fusion(f32[1,16,96,128]{3,2,1,0:T(8,128)} %bitcast.127, f32[1,16,96,128]{3,2,1,0:T(8,128)} %bitcast.128), kind=kLoop, calls=%fused_computation.43 | loop fusion | flops 393216 | bytes 3145728 | tf_op jit(solution)/shard_map/stack | solution.py:186
  128.4 4.2 %fusion.109 = (f32[1,16,96,128]{3,2,1,0:T(8,128)S(1)}, f32[1,16,96,128]{3,2,1,0:T(8,128)S(1)}, f32[1,16,96,128]{3,2,1,0:T(8,128)S(1)}) fusion(f32[16,96,128]{2,1,0:T(8,128)} %get-tuple-element.8, f32[16,96,128]{2,1,0:T(8,128)} %get-tuple-element.13, f32[16,96,128]{2,1,0:T(8,128)S(1)} %bitcast.123, f32[16,96,128]{2,1,0:T(8,128)} %get-tuple-element.17, ...), kind=kLoop, calls=%fused_computation.215 | loop fusion | flops 6488064 | bytes 14155776 | tf_op jit(solution)/shard_map/stack | solution.py:187
  132.7 2.0 %pad_maximum_fusion = f32[4,16,96,128]{3,2,1,0:T(8,128)} fusion(f32[1,16,96,128]{3,2,1,0:T(8,128)S(1)} %copy-done.13, f32[1,16,96,128]{3,2,1,0:T(8,128)S(1)} %get-tuple-element.21, f32[1,16,96,128]{3,2,1,0:T(8,128)S(1)} %get-tuple-element.20, f32[1,16,96,128]{3,2,1,0:T(8,128)S(1)} %get-tuple-element.19), kind=kLoop, calls=%fused_computation.24 | loop fusion | flops 2359296 | bytes 6291456 | tf_op jit(solution)/shard_map/stack | solution.py:187
  (39 shorter events, 0.9 us)
Async XLA Ops:
  0.6 13.2 %copy-start = (f32[4,16,96,128]{3,2,1,0:T(8,128)S(1)}, f32[4,16,96,128]{3,2,1,0:T(8,128)}, u32[]{:S(2)}) copy-start(f32[4,16,96,128]{3,2,1,0:T(8,128)} %param.10) | copy-start | bytes 9437188
  1.8 11.6 %collective-permute-start = (f32[4,96,128]{2,1,0:T(8,128)S(1)}, f32[4,96,128]{2,1,0:T(8,128)}, u32[]{:S(2)}, u32[]{:S(2)}) collective-permute-start(f32[4,96,128]{2,1,0:T(8,128)S(1)} %get-tuple-element.22), channel_id=1, source_target_pairs={{1,0},{2,1},{3,2},{4,3},{5,4},{6,5},{7,6},{8,7},{9,8},{10,9},{11,1... | collective-permute-start | bytes 589832 | tf_op jit(solution)/shard_map/ppermute | solution.py:27
  3.1 10.3 %collective-permute-start.1 = (f32[4,96,128]{2,1,0:T(8,128)S(1)}, f32[4,96,128]{2,1,0:T(8,128)}, u32[]{:S(2)}, u32[]{:S(2)}) collective-permute-start(f32[4,96,128]{2,1,0:T(8,128)S(1)} %get-tuple-element.23), channel_id=1, source_target_pairs={{0,1},{1,2},{2,3},{3,4},{4,5},{5,6},{6,7},{7,8},{8,9},{9,10},{10,1... | collective-permute-start | bytes 589832 | tf_op jit(solution)/shard_map/ppermute | solution.py:25
  10.3 3.5 %copy-start.9 = (f32[2,16,96,128]{3,2,1,0:T(8,128)S(1)}, f32[2,16,96,128]{3,2,1,0:T(8,128)}, u32[]{:S(2)}) copy-start(f32[2,16,96,128]{3,2,1,0:T(8,128)} %param.9) | copy-start | bytes 4718596
  10.3 3.5 %copy-start.12 = (f32[16,96,128]{2,1,0:T(8,128)S(1)}, f32[16,96,128]{2,1,0:T(8,128)}, u32[]{:S(2)}) copy-start(f32[16,96,128]{2,1,0:T(8,128)} %param.11) | copy-start | bytes 2359300
  13.5 17.0 %copy-start.1 = (f32[2,8,12,8,128]{4,3,2,1,0:T(8,128)}, f32[2,8,12,8,128]{4,3,2,1,0:T(8,128)S(1)}, u32[]{:S(2)}) copy-start(f32[2,8,12,8,128]{4,3,2,1,0:T(8,128)S(1)} %broadcast_in_dim.16) | copy-start | bytes 2359300
  13.6 17.0 %copy-start.3 = (f32[2,8,12,8,128]{4,3,2,1,0:T(8,128)}, f32[2,8,12,8,128]{4,3,2,1,0:T(8,128)S(1)}, u32[]{:S(2)}) copy-start(f32[2,8,12,8,128]{4,3,2,1,0:T(8,128)S(1)} %broadcast_in_dim.15) | copy-start | bytes 2359300
  13.7 16.9 %copy-start.5 = (f32[2,8,12,8,128]{4,3,2,1,0:T(8,128)}, f32[2,8,12,8,128]{4,3,2,1,0:T(8,128)S(1)}, u32[]{:S(2)}) copy-start(f32[2,8,12,8,128]{4,3,2,1,0:T(8,128)S(1)} %broadcast_in_dim.14) | copy-start | bytes 2359300
  13.8 16.8 %copy-start.8 = (f32[2,8,12,8,128]{4,3,2,1,0:T(8,128)}, f32[2,8,12,8,128]{4,3,2,1,0:T(8,128)S(1)}, u32[]{:S(2)}) copy-start(f32[2,8,12,8,128]{4,3,2,1,0:T(8,128)S(1)} %broadcast_in_dim.21) | copy-start | bytes 2359300
  30.6 0.9 copy-start.10
  32.3 5.9 %collective-permute-start.2 = (f32[4,96,128]{2,1,0:T(8,128)}, f32[4,96,128]{2,1,0:T(8,128)S(1)}, u32[]{:S(2)}, u32[]{:S(2)}) collective-permute-start(f32[4,96,128]{2,1,0:T(8,128)} %get-tuple-element.26), channel_id=1, source_target_pairs={{1,0},{2,1},{3,2},{4,3},{5,4},{6,5},{7,6},{8,7},{9,8},{10,9},{11,1... | collective-permute-start | bytes 589832 | tf_op jit(solution)/shard_map/ppermute | solution.py:27
  33.6 5.7 %collective-permute-start.3 = (f32[4,96,128]{2,1,0:T(8,128)}, f32[4,96,128]{2,1,0:T(8,128)S(1)}, u32[]{:S(2)}, u32[]{:S(2)}) collective-permute-start(f32[4,96,128]{2,1,0:T(8,128)} %get-tuple-element.27), channel_id=1, source_target_pairs={{0,1},{1,2},{2,3},{3,4},{4,5},{5,6},{6,7},{7,8},{8,9},{9,10},{10,1... | collective-permute-start | bytes 589832 | tf_op jit(solution)/shard_map/ppermute | solution.py:25
  58.1 0.9 copy-start.11
  59.7 9.4 %collective-permute-start.4 = (f32[4,96,128]{2,1,0:T(8,128)}, f32[4,96,128]{2,1,0:T(8,128)S(1)}, u32[]{:S(2)}, u32[]{:S(2)}) collective-permute-start(f32[4,96,128]{2,1,0:T(8,128)} %get-tuple-element.24), channel_id=1, source_target_pairs={{1,0},{2,1},{3,2},{4,3},{5,4},{6,5},{7,6},{8,7},{9,8},{10,9},{11,1... | collective-permute-start | bytes 589832 | tf_op jit(solution)/shard_map/ppermute | solution.py:27
  61.0 9.2 %collective-permute-start.5 = (f32[4,96,128]{2,1,0:T(8,128)}, f32[4,96,128]{2,1,0:T(8,128)S(1)}, u32[]{:S(2)}, u32[]{:S(2)}) collective-permute-start(f32[4,96,128]{2,1,0:T(8,128)} %get-tuple-element.25), channel_id=1, source_target_pairs={{0,1},{1,2},{2,3},{3,4},{4,5},{5,6},{6,7},{7,8},{8,9},{9,10},{10,1... | collective-permute-start | bytes 589832 | tf_op jit(solution)/shard_map/ppermute | solution.py:25
  125.6 2.8 %copy-start.2 = (f32[2,8,12,8,128]{4,3,2,1,0:T(8,128)S(1)}, f32[2,8,12,8,128]{4,3,2,1,0:T(8,128)}, u32[]{:S(2)}) copy-start(f32[2,8,12,8,128]{4,3,2,1,0:T(8,128)} %copy-done.1) | copy-start | bytes 2359300
  125.6 2.8 %copy-start.4 = (f32[2,8,12,8,128]{4,3,2,1,0:T(8,128)S(1)}, f32[2,8,12,8,128]{4,3,2,1,0:T(8,128)}, u32[]{:S(2)}) copy-start(f32[2,8,12,8,128]{4,3,2,1,0:T(8,128)} %copy-done.3) | copy-start | bytes 2359300
  125.6 2.8 %copy-start.6 = (f32[2,8,12,8,128]{4,3,2,1,0:T(8,128)S(1)}, f32[2,8,12,8,128]{4,3,2,1,0:T(8,128)}, u32[]{:S(2)}) copy-start(f32[2,8,12,8,128]{4,3,2,1,0:T(8,128)} %copy-done.5) | copy-start | bytes 2359300
  125.6 2.8 %copy-start.7 = (f32[16,96,128]{2,1,0:T(8,128)S(1)}, f32[16,96,128]{2,1,0:T(8,128)}, u32[]{:S(2)}) copy-start(f32[16,96,128]{2,1,0:T(8,128)} %get-tuple-element.16) | copy-start | bytes 2359300
  128.4 4.2 %copy-start.13 = (f32[1,16,96,128]{3,2,1,0:T(8,128)S(1)}, f32[1,16,96,128]{3,2,1,0:T(8,128)}, u32[]{:S(2)}) copy-start(f32[1,16,96,128]{3,2,1,0:T(8,128)} %get-tuple-element.10) | copy-start | bytes 2359300
where the time goes:
time: 136 us
  other arithmetic  65.9 us (48%)
  blocking collectives  35 us (26%)
  starting transfers between devices  20 us (15%)
  local copies, waits for them, and re-layouts  7.74 us (6%)
  between operations  4.41 us (3%)
  waiting for transfers between devices  2.25 us (2%)
    psum x1, blocking collectives, body(): total_sum = lax.psum(local_sum, 'gx')  35 us
    another operation x3, other arithmetic, body(): jnp.stack(memory + [stiff_memory])  25 us
    reduce_sum x1, other arithmetic, body(): local_sum = jnp.sum(filtered * filtered)  19.7 us
    div x1, other arithmetic, advance(): (2.0 * displace - (1.0 - half_damp) * previous + TIME_STEP * TIME_STEP *...  16.7 us
    ppermute x3, starting transfers between devices, with_halo(): lax.ppermute(tail, axis, [(i, (i + 1) % count) for i in range(ends)])  16.1 us
    ppermute x3, starting transfers between devices, with_halo(): lax.ppermute(head, axis, [((i + 1) % count, i) for i in range(ends)])  3.85 us
    another operation x1, other arithmetic, body(): jnp.stack([displace, previous])  2.77 us
    slice x3, local copies, waits for them, and re-layouts, with_halo(): head = lax.slice_in_dim(cells, 0, width, axis=dim)  2.74 us
  transfers between devices with their start and end apart: 6, of which 2 were waited for; matrix products, arithmetic and copies ran while one was open for 4% of the time, Pallas kernels for 0%

commit v1 on v0

v1 whole, which is shorter than its diff:
```python
import functools
import math

import jax
import jax.numpy as jnp
from jax import lax
from jax.experimental import pallas as pl
from jax.experimental.pallas import tpu as pltpu
from jax.sharding import PartitionSpec as P

F32 = jnp.float32
BF16 = jnp.bfloat16
STEPS = 3
BLK = 8
REACH = 4
TIME_STEP = 0.25
DAMP_PEAK = 1.5
STENCIL = (-205.0 / 72.0, 8.0 / 5.0, -1.0 / 5.0, 8.0 / 315.0, -1.0 / 560.0)
SCALE = 5040.0
WHOLE = (-14336.0, 8064.0, -1008.0, 128.0, -9.0)
CENTRE_REST = 14.0 / SCALE
TAG_ROWS = 16
KAPPA, KAPPA_R, Q0, Q1, Q2, B0, B1, B2, DECAY, PAIR, AMP, BACK, STIFF, FORCE = range(14)
N_COEF = 14
VMEM_LIMIT = 30 * 1024 * 1024


def band(rows, cols, row_period, col_period):
    row = lax.broadcasted_iota(jnp.int32, (rows, cols), 0) % row_period
    col = lax.broadcasted_iota(jnp.int32, (rows, cols), 1) % col_period
    apart = jnp.abs(row - col)
    out = jnp.zeros((rows, cols), F32)
    for offset, value in enumerate(WHOLE):
        out = jnp.where(apart == offset, value, out)
    return out.astype(BF16)


def pieces(cells):
    high = cells.astype(BF16)
    return high, (cells - high.astype(F32)).astype(BF16)


def cross_diffs(planes, read, write_y, write_z, ny, nz):
    mat_y = band(ny, 2 * ny, ny, ny)
    mat_z = band(2 * nz, nz, nz, nz)
    for one, two in zip(planes[0::2], planes[1::2]):
        high_one, low_one = pieces(read(one))
        high_two, low_two = pieces(read(two))
        upper = jnp.concatenate([high_one, high_two], axis=1)
        lower = jnp.concatenate([low_one, low_two], axis=1)
        diff_y = jnp.dot(
            mat_y, jnp.concatenate([upper, lower], axis=0), preferred_element_type=F32
        )
        write_y(one, diff_y[:, :nz])
        write_y(two, diff_y[:, nz:])
        left = jnp.concatenate([high_one, low_one], axis=1)
        right = jnp.concatenate([high_two, low_two], axis=1)
        diff_z = jnp.dot(
            jnp.concatenate([left, right], axis=0), mat_z, preferred_element_type=F32
        )
        write_z(one, diff_z[:ny])
        write_z(two, diff_z[ny:])


def first_diff(cells, at):
    total = STENCIL[0] * cells[at]
    for offset in range(1, REACH + 1):
        above, below = cells.get(at + offset), cells.get(at - offset)
        if above is not None and below is not None:
            total = total + STENCIL[offset] * (above + below)
        elif above is not None:
            total = total + STENCIL[offset] * above
        elif below is not None:
            total = total + STENCIL[offset] * below
    return total


def outer_part(cells, at, positions):
    total = None
    for position in positions:
        offset = abs(position - at)
        if offset <= REACH:
            term = STENCIL[offset] * cells[position]
            total = term if total is None else total + term
    return total


def advance(cells, previous, memory, stiff, forcing, diffs, co, phase):
    rest = CENTRE_REST * cells
    diffs = [diffs[0], diffs[1] * (1.0 / SCALE) - rest, diffs[2] * (1.0 / SCALE) - rest]
    memory = [m + co(Q0 + d) * (diffs[d] - m) for d, m in enumerate(memory)]
    inner = sum(diffs[d] - co(B0 + d) * memory[d] for d in range(3))
    stiff = co(DECAY) * stiff + co(PAIR) * cells
    new = (
        co(AMP) * cells
        - co(BACK) * previous
        + co(KAPPA) * inner
        - co(STIFF) * stiff
        - (co(FORCE) * phase) * forcing
    )
    return new, memory, stiff


def coefficients(speed_square, bits):
    rates = [DAMP_PEAK * bit for bit in bits]
    damping = rates[0] + rates[1] + rates[2]
    pairing = rates[0] * rates[1] + rates[1] * rates[2] + rates[2] * rates[0]
    retention = [jnp.exp(-TIME_STEP * rate) for rate in rates]
    half = 0.5 * TIME_STEP * damping
    inverse = 1.0 / (1.0 + half)
    square = TIME_STEP * TIME_STEP
    kappa = square * speed_square * inverse
    return (
        kappa,
        kappa * retention[0],
        1.0 - retention[0],
        1.0 - retention[1],
        1.0 - retention[2],
        bits[0],
        bits[1],
        bits[2],
        jnp.exp(-TIME_STEP * damping),
        TIME_STEP * pairing,
        (2.0 - square * pairing) * inverse,
        (1.0 - half) * inverse,
        square * damping * inverse,
        square * inverse,
    )


def spread(tile, ny, nz):
    row = lax.broadcasted_iota(jnp.int32, (ny, TAG_ROWS), 0) // BLK
    col = lax.broadcasted_iota(jnp.int32, (ny, TAG_ROWS), 1)
    down = (row == col).astype(F32).astype(BF16)
    row = lax.broadcasted_iota(jnp.int32, (nz, nz), 0)
    col = lax.broadcasted_iota(jnp.int32, (nz, nz), 1) // BLK
    along = (row == col).astype(F32).astype(BF16)
    wide = jnp.dot(tile.astype(BF16), along, preferred_element_type=F32)
    return jnp.dot(down, wide.astype(BF16), preferred_element_type=F32)


def medium(index_tile, mask_tile, table, ny, nz):
    index = spread(index_tile, ny, nz)
    mask = spread(mask_tile, ny, nz).astype(jnp.int32)
    speed = jnp.zeros((ny, nz), F32)
    for entry in range(table.shape[0]):
        speed = jnp.where(index == float(entry), table[entry], speed)
    bits = [((mask >> direction) & 1).astype(F32) for direction in range(3)]
    return speed * speed, bits


def phase_at(freq, start, count):
    angle = freq[0] * (start[0] + count * TIME_STEP)
    return jnp.cos(jnp.full((BLK, 128), angle, F32))


def weight_at(freq, start, count):
    return (TIME_STEP * freq[0] / math.pi) * (phase_at(freq, start, count) - 0.25)


def over_rows(ny, step):
    def one(block, carry):
        step(pl.multiple_of(block * BLK, BLK))
        return carry

    lax.fori_loop(0, ny // BLK, one, 0)


def is_even():
    return lax.axis_index("gx") % 2 == 0


def send_kernel(
    wave, layer, source, freq, start, table, index, mask,
    inside, across, coef,
    u0, strips, diff_y, diff_z, tags, sems,
):
    nx, ny, nz = u0.shape
    n_block = nx // BLK
    edges = (0, nx - REACH)
    copies = [pltpu.make_async_copy(wave.at[0], u0, sems.at[0])]
    for side in range(2):
        at = pl.ds(edges[side], REACH)
        copies += [
            pltpu.make_async_copy(wave.at[1, at], strips.at[side, 0], sems.at[1 + 3 * side]),
            pltpu.make_async_copy(
                layer.at[:, at], strips.at[side, pl.ds(1, 4)], sems.at[2 + 3 * side]
            ),
            pltpu.make_async_copy(source.at[at], strips.at[side, 5], sems.at[3 + 3 * side]),
        ]
    for copy in copies:
        copy.start()
    even = is_even()
    tags[...] = jnp.zeros_like(tags)
    for block in range(n_block):
        tags[block, 0, : index.shape[1], : index.shape[2]] = index[block].astype(F32)
        tags[block, 1, : mask.shape[1], : mask.shape[2]] = mask[block].astype(F32)
    for block in range(n_block):
        square, bits = medium(tags[block, 0], tags[block, 1], table, ny, nz)
        for entry, value in enumerate(coefficients(square, bits)):
            coef[entry, block] = value
    phase = phase_at(freq, start, 0)
    copies[0].wait()
    edge_planes = [*range(REACH), *range(nx - REACH, nx)]
    slot = {plane: number for number, plane in enumerate(edge_planes)}

    def put_y(plane, value):
        diff_y[slot[plane]] = value

    def put_z(plane, value):
        diff_z[slot[plane]] = value

    cross_diffs(edge_planes, lambda plane: u0[plane], put_y, put_z, ny, nz)
    for copy in copies[1:]:
        copy.wait()

    def step(rows):
        at = pl.ds(rows, BLK)
        sides = []
        for side in range(2):
            block = side * (n_block - 1)
            reach = range(2 * REACH) if side == 0 else range(nx - 2 * REACH, nx)
            cells = {plane: u0[plane, at] for plane in reach}
            co = {}

            def get(entry):
                if entry not in co:
                    co[entry] = coef[entry, block, at]
                return co[entry]

            values = []
            for number in range(REACH):
                plane = edges[side] + number
                new, _, _ = advance(
                    cells[plane],
                    strips[side, 0, number, at],
                    [strips[side, 1 + d, number, at] for d in range(3)],
                    strips[side, 4, number, at],
                    strips[side, 5, number, at],
                    [
                        first_diff(cells, plane),
                        diff_y[slot[plane], at],
                        diff_z[slot[plane], at],
                    ],
                    get,
                    phase,
                )
                values.append((cells[plane], new))
            sides.append(values)
        for number in range(REACH):
            for part in range(2):
                to = pl.ds(pl.multiple_of((part * REACH + number) * ny + rows, BLK), BLK)
                left, right = sides[0][number][part], sides[1][number][part]
                inside[to] = jnp.where(even, right, left)
                across[to] = jnp.where(even, left, right)

    over_rows(ny, step)
    for part in range(2):
        to = pl.ds(2 * REACH * ny + part * TAG_ROWS, TAG_ROWS)
        left, right = tags[0, part], tags[n_block - 1, part]
        inside[to] = jnp.where(even, right, left)
        across[to] = jnp.where(even, left, right)


def local_kernel(
    wave, layer, source, filtered, freq, start, coef,
    inside, across, u0, forcing, running, state, memory, stiff,
    prev, mem_in, diff_y, diff_z, sems,
):
    nx, ny, nz = u0.shape
    copies = [
        pltpu.make_async_copy(wave.at[0], u0, sems.at[0]),
        pltpu.make_async_copy(wave.at[1], prev, sems.at[1]),
        pltpu.make_async_copy(layer, mem_in, sems.at[2]),
        pltpu.make_async_copy(source, forcing, sems.at[3]),
        pltpu.make_async_copy(filtered, running, sems.at[4]),
    ]
    for copy in copies:
        copy.start()
    even = is_even()
    phases = [phase_at(freq, start, count) for count in range(2)]
    copies[0].wait()

    def put_y(plane, value):
        diff_y[plane] = value

    def put_z(plane, value):
        diff_z[plane] = value

    cross_diffs(range(nx), lambda plane: u0[plane], put_y, put_z, ny, nz)
    for copy in copies[1:]:
        copy.wait()

    def first(rows):
        at = pl.ds(rows, BLK)
        cells = {plane: u0[plane, at] for plane in range(nx)}
        for plane in range(nx):
            new, mem, sti = advance(
                cells[plane],
                prev[plane, at],
                [mem_in[d, plane, at] for d in range(3)],
                mem_in[3, plane, at],
                forcing[plane, at],
                [first_diff(cells, plane), diff_y[plane, at], diff_z[plane, at]],
                lambda entry, block=plane // BLK: coef[entry, block, at],
                phases[0],
            )
            state[plane, at] = new
            for d in range(3):
                memory[d, plane, at] = mem[d]
            stiff[plane, at] = sti

    over_rows(ny, first)
    edge_planes = [*range(REACH), *range(nx - REACH, nx)]
    cross_diffs(edge_planes, lambda plane: state[plane], put_y, put_z, ny, nz)

    def second(rows):
        at = pl.ds(rows, BLK)
        cells = {plane: state[plane, at] for plane in range(nx)}
        values = {}
        for plane in edge_planes:
            values[plane], _, _ = advance(
                cells[plane],
                u0[plane, at],
                [memory[d, plane, at] for d in range(3)],
                stiff[plane, at],
                forcing[plane, at],
                [first_diff(cells, plane), diff_y[plane, at], diff_z[plane, at]],
                lambda entry, block=plane // BLK: coef[entry, block, at],
                phases[1],
            )
        for number in range(REACH):
            left, right = values[number], values[nx - REACH + number]
            inside[number, at] = jnp.where(even, right, left)
            across[number, at] = jnp.where(even, left, right)

    over_rows(ny, second)


def joint_kernel(
    freq, start, table, coef, inside, across, u0, forcing, running, state, memory, stiff,
    out_state, out_layer, out_filtered, edge_new, edge_memory, edge_running, ghost, partial,
    ext, bump, push, new, field, tail, ghost_coef, diff_y, diff_z, bump_y, bump_z, sems,
):
    nx, ny, nz = u0.shape
    count = lax.axis_size("gx")
    place = lax.axis_index("gx")
    even = is_even()
    n_block = nx // BLK
    present = (
        jnp.where(place > 0, 1.0, 0.0).astype(F32),
        jnp.where(place < count - 1, 1.0, 0.0).astype(F32),
    )
    phases = [phase_at(freq, start, number) for number in range(STEPS)]
    weights = [weight_at(freq, start, number + 1) for number in range(STEPS)]

    def received(to):
        one, two = inside[to], across[to]
        return jnp.where(even, two, one), jnp.where(even, one, two)

    tag_at = 2 * REACH * ny
    tiles = [received(pl.ds(tag_at + part * TAG_ROWS, TAG_ROWS)) for part in range(2)]
    for side in range(2):
        square, bits = medium(tiles[0][side], tiles[1][side], table, ny, nz)
        values = coefficients(square * present[side], bits)
        pairing, damping = values[PAIR] * (1.0 / TIME_STEP), DAMP_PEAK * (bits[0] + bits[1] + bits[2])
        inverse = values[FORCE] * (1.0 / (TIME_STEP * TIME_STEP))
        grown = (
            2.0 - TIME_STEP * TIME_STEP * pairing * (1.0 + TIME_STEP * damping)
        ) * inverse
        kappa = values[KAPPA]
        for entry, value in enumerate(
            (
                values[KAPPA_R],
                values[Q0],
                kappa * (1.0 - values[Q1]),
                kappa * (1.0 - values[Q2]),
                grown,
            )
        ):
            ghost_coef[side, entry] = value

    ghosts = (range(-REACH, 0), range(nx, nx + REACH))
    owned = (range(REACH), range(nx - REACH, nx))

    def exchange(rows):
        at = pl.ds(rows, BLK)
        halo = {}
        sent = {}
        for number in range(REACH):
            to = pl.ds(pl.multiple_of(number * ny + rows, BLK), BLK)
            halo[-REACH + number], halo[nx + number] = received(to)
            to = pl.ds(pl.multiple_of((REACH + number) * ny + rows, BLK), BLK)
            sent[-REACH + number], sent[nx + number] = received(to)
        for side in range(2):
            block = side * (n_block - 1)
            mine = {plane: u0[plane, at] for plane in owned[side]}
            kappa_r, q0 = coef[KAPPA_R, block, at], coef[Q0, block, at]
            for plane in owned[side]:
                outer = outer_part(halo, plane, ghosts[side])
                ext[plane + REACH, at] = state[plane, at] + kappa_r * outer
                number = plane - owned[side][0]
                edge_memory[side, number, at] = memory[0, plane, at] + q0 * outer
            kappa_r = ghost_coef[side, 0, at]
            for position in ghosts[side]:
                outer = outer_part(mine, position, owned[side])
                added = kappa_r * outer
                number = position - ghosts[side][0]
                bump[side * REACH + number, at] = added
                push[side, number, at] = outer
                ext[position + REACH, at] = sent[position] + added
        for plane in range(REACH, nx - REACH):
            ext[plane + REACH, at] = state[plane, at]

    over_rows(ny, exchange)

    def put_y(plane, value):
        diff_y[plane] = value

    def put_z(plane, value):
        diff_z[plane] = value

    cross_diffs(range(nx), lambda plane: ext[plane + REACH], put_y, put_z, ny, nz)

    def put_bump_y(plane, value):
        bump_y[plane] = value

    def put_bump_z(plane, value):
        bump_z[plane] = value

    cross_diffs(range(2 * REACH), lambda plane: bump[plane], put_bump_y, put_bump_z, ny, nz)

    def second(rows):
        at = pl.ds(rows, BLK)
        cells = {plane: ext[plane + REACH, at] for plane in range(-REACH, nx + REACH)}
        for plane in range(nx):
            if plane < REACH:
                mem0 = edge_memory[0, plane, at]
            elif plane >= nx - REACH:
                mem0 = edge_memory[1, plane - nx + REACH, at]
            else:
                mem0 = memory[0, plane, at]
            value, mem, sti = advance(
                cells[plane],
                u0[plane, at],
                [mem0, memory[1, plane, at], memory[2, plane, at]],
                stiff[plane, at],
                forcing[plane, at],
                [first_diff(cells, plane), diff_y[plane, at], diff_z[plane, at]],
                lambda entry, block=plane // BLK: coef[entry, block, at],
                phases[1],
            )
            new[plane, at] = value
            for d in range(3):
                field[d, plane, at] = mem[d]
            field[3, plane, at] = sti
            tail[plane, at] = running[plane, at] + weights[0] * cells[plane] + weights[1] * value
        for side in range(2):
            kappa_r, q0, kappa_1, kappa_2, grown = [
                ghost_coef[side, entry, at] for entry in range(5)
            ]
            added = {
                position: bump[side * REACH + position - ghosts[side][0], at]
                for position in ghosts[side]
            }
            for position in ghosts[side]:
                number = position - ghosts[side][0]
                value = added[position]
                rest = CENTRE_REST * value
                along = first_diff(added, position) + outer_part(cells, position, owned[side])
                side_y = bump_y[side * REACH + number, at] * (1.0 / SCALE) - rest
                side_z = bump_z[side * REACH + number, at] * (1.0 / SCALE) - rest
                ghost[side * REACH + number, at] = (
                    grown * value
                    + kappa_r * (along - q0 * push[side, number, at])
                    + kappa_1 * side_y
                    + kappa_2 * side_z
                )

    over_rows(ny, second)
    inner = pl.ds(REACH, nx - 2 * REACH)
    writes = [pltpu.make_async_copy(new, out_state.at[1], sems.at[0])]
    writes[0].start()
    cross_diffs(range(nx), lambda plane: new[plane], put_y, put_z, ny, nz)
    partial[...] = jnp.zeros_like(partial)

    def third(rows):
        at = pl.ds(rows, BLK)
        cells = {plane: new[plane, at] for plane in range(nx)}
        total = partial[...]
        for plane in range(nx):
            value, mem, sti = advance(
                cells[plane],
                ext[plane + REACH, at],
                [field[d, plane, at] for d in range(3)],
                field[3, plane, at],
                forcing[plane, at],
                [first_diff(cells, plane), diff_y[plane, at], diff_z[plane, at]],
                lambda entry, block=plane // BLK: coef[entry, block, at],
                phases[2],
            )
            done = tail[plane, at] + weights[2] * value
            for d in range(1, 3):
                field[d, plane, at] = mem[d]
            field[3, plane, at] = sti
            if REACH <= plane < nx - REACH:
                field[0, plane, at] = mem[0]
                bump_plane = plane
                ext[bump_plane + REACH, at] = value
                tail[plane, at] = done
                total = total + done * done
            else:
                side = 0 if plane < REACH else 1
                number = plane if side == 0 else plane - nx + REACH
                edge_new[side, number, at] = value
                edge_memory[side, number, at] = mem[0]
                edge_running[side, number, at] = done
        partial[...] = total

    over_rows(ny, third)
    own = pl.ds(2 * REACH, nx - 2 * REACH)
    writes += [
        pltpu.make_async_copy(ext.at[own], out_state.at[0, inner], sems.at[1]),
        pltpu.make_async_copy(field.at[0, inner], out_layer.at[0, inner], sems.at[2]),
        pltpu.make_async_copy(field.at[pl.ds(1, 3)], out_layer.at[pl.ds(1, 3)], sems.at[3]),
        pltpu.make_async_copy(tail.at[inner], out_filtered.at[inner], sems.at[4]),
    ]
    for write in writes[1:]:
        write.start()
    for write in writes:
        write.wait()


def finish_kernel(
    freq, start, coef, inside, across, edge_new, edge_memory, edge_running, ghost, partial,
    state_in, layer_in, filtered_in,
    out_state, out_layer, out_filtered, total_out,
    last, layer_last, tail, sems,
):
    del state_in, layer_in, filtered_in
    nx = out_state.shape[1]
    ny = out_state.shape[2]
    n_block = nx // BLK
    even = is_even()
    weight = weight_at(freq, start, STEPS)
    total_out[...] = partial[...]
    ghosts = (range(-REACH, 0), range(nx, nx + REACH))
    owned = (range(REACH), range(nx - REACH, nx))

    def step(rows):
        at = pl.ds(rows, BLK)
        halo = {}
        for number in range(REACH):
            one, two = inside[number, at], across[number, at]
            halo[-REACH + number] = jnp.where(even, two, one) + ghost[number, at]
            halo[nx + number] = jnp.where(even, one, two) + ghost[REACH + number, at]
        total = total_out[...]
        for side in range(2):
            block = side * (n_block - 1)
            kappa_r, q0 = coef[KAPPA_R, block, at], coef[Q0, block, at]
            for number, plane in enumerate(owned[side]):
                outer = outer_part(halo, plane, ghosts[side])
                added = kappa_r * outer
                last[side, number, at] = edge_new[side, number, at] + added
                layer_last[side, number, at] = edge_memory[side, number, at] + q0 * outer
                done = edge_running[side, number, at] + weight * added
                tail[side, number, at] = done
                total = total + done * done
        total_out[...] = total

    over_rows(ny, step)
    writes = []
    for side in range(2):
        at = pl.ds(owned[side][0], REACH)
        writes += [
            pltpu.make_async_copy(last.at[side], out_state.at[0, at], sems.at[3 * side]),
            pltpu.make_async_copy(layer_last.at[side], out_layer.at[0, at], sems.at[3 * side + 1]),
            pltpu.make_async_copy(tail.at[side], out_filtered.at[at], sems.at[3 * side + 2]),
        ]
    for write in writes:
        write.start()
    for write in writes:
        write.wait()


ANY = pl.BlockSpec(memory_space=pl.ANY)
VEC = pl.BlockSpec(memory_space=pltpu.VMEM)
SCALAR = pl.BlockSpec(memory_space=pltpu.SMEM)


def held(*shape):
    return pltpu.VMEM(shape, F32)


def in_vmem(*arrays):
    return [pltpu.with_memory_space_constraint(array, pltpu.VMEM) for array in arrays]


def call(kernel, name, in_specs, out_shape, out_specs, scratch, operands, micros, aliases=None):
    return pl.pallas_call(
        kernel,
        name=name,
        in_specs=in_specs,
        out_shape=out_shape,
        out_specs=out_specs,
        scratch_shapes=scratch,
        input_output_aliases=aliases or {},
        compiler_params=pltpu.CompilerParams(vmem_limit_bytes=VMEM_LIMIT),
        cost_estimate=pl.CostEstimate(
            flops=0, bytes_accessed=int(micros * 3.6e6), transcendentals=0
        ),
    )(*operands)


def swap_pairs(count):
    inside = [(i, i ^ 1) for i in range(count)]
    across = []
    for i in range(1, count - 1, 2):
        across += [(i, i + 1), (i + 1, i)]
    return inside, across


def total_over(values, axis):
    count = lax.axis_size(axis)
    if count & (count - 1):
        return lax.psum(values, axis)
    hop = 1
    while hop < count:
        values = values + lax.ppermute(values, axis, [(i, i ^ hop) for i in range(count)])
        hop *= 2
    return values


def body(
    wave_state, layer_fields, source, filtered, frequency, start_time, speed_table, speed_index,
    pml_mask,
):
    _, nx, ny, nz = wave_state.shape
    n_block = nx // BLK
    count = lax.axis_size("gx")
    pair_inside, pair_across = swap_pairs(count)
    brick = (nx, ny, nz)
    strip = (REACH, ny, nz)
    message = (2 * REACH * ny + 2 * TAG_ROWS, nz)
    dma = pltpu.SemaphoreType.DMA
    vec = lambda *shape: pltpu.VMEM(shape, F32)

    inside, across, coef = call(
        send_kernel,
        "strips",
        [ANY] * 3 + [SCALAR] * 3 + [VEC] * 2,
        [held(*message), held(*message), held(N_COEF, n_block, ny, nz)],
        [VEC] * 3,
        [
            vec(*brick),
            vec(2, 6, *strip),
            vec(2 * REACH, ny, nz),
            vec(2 * REACH, ny, nz),
            vec(n_block, 2, TAG_ROWS, 128),
            dma((7,)),
        ],
        (
            wave_state, layer_fields, source, frequency, start_time, speed_table, speed_index,
            pml_mask,
        ),
        2.5,
    )
    got_inside = lax.ppermute(inside, "gx", pair_inside)
    got_across = lax.ppermute(across, "gx", pair_across)

    later_inside, later_across, u0, forcing, running, state, memory, stiff = call(
        local_kernel,
        "local",
        [ANY] * 4 + [SCALAR] * 2 + [VEC],
        [
            held(*strip), held(*strip), held(*brick), held(*brick), held(*brick), held(*brick),
            held(3, *brick), held(*brick),
        ],
        [VEC] * 8,
        [vec(*brick), vec(4, *brick), vec(*brick), vec(*brick), dma((5,))],
        (
            wave_state, layer_fields, source, filtered, frequency, start_time, *in_vmem(coef),
        ),
        5,
    )
    last_inside = lax.ppermute(later_inside, "gx", pair_inside)
    last_across = lax.ppermute(later_across, "gx", pair_across)

    out_types = [
        jax.ShapeDtypeStruct(wave_state.shape, F32),
        jax.ShapeDtypeStruct(layer_fields.shape, F32),
        jax.ShapeDtypeStruct(filtered.shape, F32),
    ]
    (
        next_state, next_layer, next_filtered, edge_new, edge_memory, edge_running, ghost, partial,
    ) = call(
        joint_kernel,
        "joint",
        [SCALAR] * 3 + [VEC] * 9,
        out_types
        + [
            held(2, *strip), held(2, *strip), held(2, *strip), held(2 * REACH, ny, nz),
            held(BLK, nz),
        ],
        [ANY] * 3 + [VEC] * 5,
        [
            vec(nx + 2 * REACH, ny, nz),
            vec(2 * REACH, ny, nz),
            vec(2, *strip),
            vec(*brick),
            vec(4, *brick),
            vec(*brick),
            vec(2, 5, ny, nz),
            vec(*brick),
            vec(*brick),
            vec(2 * REACH, ny, nz),
            vec(2 * REACH, ny, nz),
            dma((5,)),
        ],
        (
            frequency, start_time, speed_table,
            *in_vmem(
                coef, got_inside, got_across, u0, forcing, running, state, memory, stiff
            ),
        ),
        5,
    )
    next_state, next_layer, next_filtered, total = call(
        finish_kernel,
        "finish",
        [SCALAR] * 2 + [VEC] * 8 + [ANY] * 3,
        out_types + [held(BLK, nz)],
        [ANY] * 3 + [VEC],
        [vec(2, *strip), vec(2, *strip), vec(2, *strip), dma((6,))],
        (
            frequency, start_time,
            *in_vmem(
                coef, last_inside, last_across, edge_new, edge_memory, edge_running, ghost, partial
            ),
            next_state, next_layer, next_filtered,
        ),
        1,
        {10: 0, 11: 1, 12: 2},
    )
    total = jnp.sum(total_over(total, "gx"))
    filter_norm = jnp.sqrt(total / (filtered.size * count) + 1e-06)
    return next_state, next_layer, next_filtered, filter_norm.reshape(1)


def solution(mesh):
    placed = (
        P("grp", "gx", None, None),
        P("grp", "gx", None, None),
        P(("grp", "gx"), None, None),
        P(("grp", "gx"), None, None),
        P("grp"),
        P("grp"),
        P(),
        P("gx", None, None),
        P("gx", None, None),
    )
    return jax.shard_map(
        body,
        mesh=mesh,
        in_specs=placed,
        out_specs=(
            P("grp", "gx", None, None),
            P("grp", "gx", None, None),
            P(("grp", "gx"), None, None),
            P("grp"),
        ),
        check_vma=False,
    )
```

time: 136 us -> 54.8 us (0.40)
  other arithmetic: 65.9 us -> 0.61 us
  blocking collectives: 35 us -> 0 us
  Pallas kernels: 0 us -> 17.2 us
  waiting for transfers between devices: 2.25 us -> 5.59 us
    psum x1 -> x0, blocking collectives: 35 us -> none  [body(): total_sum = lax.psum(local_sum, 'gx')]
    another operation x4 -> x0, other arithmetic: 27.8 us -> none  [the longest x3 25 us: body(): jnp.stack(memory + [stiff_memory])]
    reduce_sum x2 -> x1, other arithmetic: 20.5 us -> 0.6 us  [body(): total = jnp.sum(total_over(total, 'gx'))]
    pallas_call x0 -> x4, Pallas kernels: none -> 17.2 us  [call(): pl.pallas_call(kernel, name=name, in_specs=in_specs, out_shape=out_shape,...]
    div x1 -> x0, other arithmetic: 16.7 us -> none  [advance(): (2.0 * displace - (1.0 - half_damp) * previous + TIME_STEP * TIME_STEP *...]
    unnamed x29 -> x14, local copies, waits for them, and re-layouts: 2.65 us -> 6.51 us
    ppermute x6 -> x8, waiting for transfers between devices: 2.25 us -> 5.59 us  [the longest x4 5.58 us: total_over(): lax.ppermute(values, axis, [(i, i ^ hop) for i in range(count)])]
    slice x3 -> x0, local copies, waits for them, and re-layouts: 2.74 us -> none  [with_halo(): head = lax.slice_in_dim(cells, 0, width, axis=dim)]
  transfers between devices with their start and end apart: 6 -> 8, of which waited for: 2 -> 4; matrix products, arithmetic and copies ran while one was open for 4% -> 0% of each run, Pallas kernels for 0% -> 22%
where the time goes in v1:
time: 54.8 us; the launch traced here: 54.4 us
  starting transfers between devices  20.6 us (38%)
  Pallas kernels  17.2 us (31%)
  local copies, waits for them, and re-layouts  6.51 us (12%)
  waiting for transfers between devices  5.59 us (10%)
  between operations  3.86 us (7%)
  other arithmetic  0.61 us (1%)
    pallas_call x4, Pallas kernels, call(): pl.pallas_call(kernel, name=name, in_specs=in_specs, out_shape=out_shape,...  17.2 us
    ppermute x4, starting transfers between devices, total_over(): lax.ppermute(values, axis, [(i, i ^ hop) for i in range(count)])  14.8 us
    unnamed x14, local copies, waits for them, and re-layouts  6.51 us
    ppermute x4, waiting for transfers between devices, total_over(): lax.ppermute(values, axis, [(i, i ^ hop) for i in range(count)])  5.58 us
    ppermute x1, starting transfers between devices, body(): last_inside = lax.ppermute(later_inside, 'gx', pair_inside)  3.96 us
  transfers between devices with their start and end apart: 8, of which 4 were waited for; matrix products, arithmetic and copies ran while one was open for 0% of the time, Pallas kernels for 22%

profile of v1, /device:TPU:0, one launch (start us, length us, event | category | flops | bytes accessed | tf_op | source)
XLA Modules:
  0.0 54.4 jit_solution(1194785836660340195)
XLA Ops:
  1.9 0.7 %copy.16.index = s32[2,12,16]{2,1,0:T(8,128)S(1)} copy(s32[2,12,16]{2,0,1:T(2,128)} %param.16) | data formatting | bytes 3072 | tf_op args[7]
  2.6 0.7 %copy.17.mask = s32[2,12,16]{2,1,0:T(8,128)S(1)} copy(s32[2,12,16]{2,0,1:T(2,128)} %param.17) | data formatting | bytes 3072 | tf_op args[8]
  3.3 1.9 %copy-done = f32[4,16,96,128]{3,2,1,0:T(8,128)S(1)} copy-done((f32[4,16,96,128]{3,2,1,0:T(8,128)S(1)}, f32[4,16,96,128]{3,2,1,0:T(8,128)}, u32[]{:S(2)}) %copy-start) | copy-done | bytes 3145752
  5.2 1.4 %copy-done.1 = f32[2,16,96,128]{3,2,1,0:T(8,128)S(1)} copy-done((f32[2,16,96,128]{3,2,1,0:T(8,128)S(1)}, f32[2,16,96,128]{3,2,1,0:T(8,128)}, u32[]{:S(2)}) %copy-start.1) | copy-done | bytes 1572888
  6.6 1.1 %copy-done.2 = f32[16,96,128]{2,1,0:T(8,128)S(1)} copy-done((f32[16,96,128]{2,1,0:T(8,128)S(1)}, f32[16,96,128]{2,1,0:T(8,128)}, u32[]{:S(2)}) %copy-start.2) | copy-done | bytes 786456
  7.8 0.7 %copy-done.4 = f32[16]{0:T(128)S(1)} copy-done((f32[16]{0:T(128)S(1)}, f32[16]{0:T(128)}, u32[]{:S(2)}) %copy-start.4) | copy-done | bytes 88
  8.4 3.8 %strips.1 = (f32[800,128]{1,0:T(8,128)S(1)}, f32[800,128]{1,0:T(8,128)S(1)}, f32[14,2,96,128]{3,2,1,0:T(8,128)S(1)}) custom-call(f32[2,16,96,128]{3,2,1,0:T(8,128)S(1)} %copy-done.1, f32[4,16,96,128]{3,2,1,0:T(8,128)S(1)} %copy-done, f32[16,96,128]{2,1,0:T(8,128)S(1)} %copy-done.2, f32[1]{0:T(128)S(6)} %copy.21.freq, f32[1]{0:T(128)S(6)} %copy.22.start, ...), custom_call_target="tpu_custom_call" | custom-call | bytes 9000000 | tf_op jit(solution)/shard_map/strips/pallas_call | solution.py:600
  12.2 0.5 collective-permute-start.2
  12.8 0.7 %collective-permute-start.3 = (f32[800,128]{1,0:T(8,128)S(1)}, f32[800,128]{1,0:T(8,128)S(1)}, u32[]{:S(2)}, u32[]{:S(2)}) collective-permute-start(f32[800,128]{1,0:T(8,128)S(1)} %get-tuple-element.31), channel_id=1, source_target_pairs={{1,2},{2,1},{3,4},{4,3},{5,6},{6,5},{7,8},{8,7},{9,10},{10,9},{11,... | collective-permute-start | bytes 1228808 | tf_op jit(solution)/shard_map/ppermute | solution.py:669
  13.5 0.0 copy-start.5
  13.5 3.8 %local.1 = (f32[4,96,128]{2,1,0:T(8,128)S(1)}, f32[4,96,128]{2,1,0:T(8,128)S(1)}, f32[16,96,128]{2,1,0:T(8,128)S(1)}, f32[16,96,128]{2,1,0:T(8,128)S(1)}, f32[16...) custom-call(f32[2,16,96,128]{3,2,1,0:T(8,128)S(1)} %copy-done.1, ...), custom_call_target="tpu_custom_call" | custom-call | bytes 18000000 | tf_op jit(solution)/shard_map/local/pallas_call | solution.py:600
  17.2 4.0 %collective-permute-start = (f32[4,96,128]{2,1,0:T(8,128)S(1)}, f32[4,96,128]{2,1,0:T(8,128)S(1)}, u32[]{:S(2)}, u32[]{:S(2)}) collective-permute-start(f32[4,96,128]{2,1,0:T(8,128)S(1)} %get-tuple-element.28), channel_id=1, source_target_pairs={{0,1},{1,0},{2,3},{3,2},{4,5},{5,4},{6,7},{7,6},{8,9},{9,8},{10,11... | collective-permute-start | bytes 589832 | tf_op jit(solution)/shard_map/ppermute | solution.py:686
  21.2 0.7 %collective-permute-start.1 = (f32[4,96,128]{2,1,0:T(8,128)S(1)}, f32[4,96,128]{2,1,0:T(8,128)S(1)}, u32[]{:S(2)}, u32[]{:S(2)}) collective-permute-start(f32[4,96,128]{2,1,0:T(8,128)S(1)} %get-tuple-element.29), channel_id=1, source_target_pairs={{1,2},{2,1},{3,4},{4,3},{5,6},{6,5},{7,8},{8,7},{9,10},{10,9},{11,... | collective-permute-start | bytes 589832 | tf_op jit(solution)/shard_map/ppermute | solution.py:687
  21.9 8.2 %joint.1 = (f32[2,16,96,128]{3,2,1,0:T(8,128)}, f32[4,16,96,128]{3,2,1,0:T(8,128)}, f32[16,96,128]{2,1,0:T(8,128)}, f32[2,4,96,128]{3,2,1,0:T(8,128)S(1)}, f32[2...) custom-call(f32[1]{0:T(128)S(6)} %copy.21.freq, ...), custom_call_target="tpu_custom_call" | custom-call | bytes 18000000 | tf_op jit(solution)/shard_map/joint/pallas_call | solution.py:600
  30.1 1.5 %finish.1 = (f32[2,16,96,128]{3,2,1,0:T(8,128)}, f32[4,16,96,128]{3,2,1,0:T(8,128)}, f32[16,96,128]{2,1,0:T(8,128)}, f32[8,128]{1,0:T(8,128)S(1)}) custom-call(f32[1]{0:T(128)S(6)} %copy.21.freq, f32[1]{0:T(128)S(6)} %copy.22.start, f32[14,2,96,128]{3,2,1,0:T(8,128)S(1)} %get-tuple-element.27.coef, ...), custom_call_target="tpu_custom_call", output_to_operand_aliasing={{0}: (10, {}), {1}: (11, {}), {2}: (12, {})} | custom-call | bytes 3600000 | tf_op jit(solution)/shard_map/finish/pallas_call | solution.py:600
  31.6 4.7 %collective-permute-start.4 = (f32[8,128]{1,0:T(8,128)S(1)}, f32[8,128]{1,0:T(8,128)S(1)}, u32[]{:S(2)}, u32[]{:S(2)}) collective-permute-start(f32[8,128]{1,0:T(8,128)S(1)} %get-tuple-element.49), channel_id=1, source_target_pairs={{0,1},{1,0},{2,3},{3,2},{4,5},{5,4},{6,7},{7,6},{8,9},{9,8},{10,11... | collective-permute-start | bytes 12296 | tf_op jit(solution)/shard_map/ppermute | solution.py:629
  36.4 0.8 %collective-permute-done.4 = f32[8,128]{1,0:T(8,128)S(1)} collective-permute-done((f32[8,128]{1,0:T(8,128)S(1)}, f32[8,128]{1,0:T(8,128)S(1)}, u32[]{:S(2)}, u32[]{:S(2)}) %collective-permute-start.4) | collective-permute-done | bytes 4128 | tf_op jit(solution)/shard_map/ppermute | solution.py:629
  37.2 4.8 %collective-permute-start.5 = (f32[8,128]{1,0:T(8,128)S(1)}, f32[8,128]{1,0:T(8,128)S(1)}, u32[]{:S(2)}, u32[]{:S(2)}) collective-permute-start(f32[8,128]{1,0:T(8,128)S(1)} %add.15), channel_id=1, source_target_pairs={{0,2},{1,3},{2,0},{3,1},{4,6},{5,7},{6,4},{7,5},{8,10},{9,11},{10,... | collective-permute-start | bytes 12296 | tf_op jit(solution)/shard_map/ppermute | solution.py:629
  42.0 1.6 %collective-permute-done.5 = f32[8,128]{1,0:T(8,128)S(1)} collective-permute-done((f32[8,128]{1,0:T(8,128)S(1)}, f32[8,128]{1,0:T(8,128)S(1)}, u32[]{:S(2)}, u32[]{:S(2)}) %collective-permute-start.5) | collective-permute-done | bytes 4128 | tf_op jit(solution)/shard_map/ppermute | solution.py:629
  43.6 2.2 %collective-permute-start.6 = (f32[8,128]{1,0:T(8,128)S(1)}, f32[8,128]{1,0:T(8,128)S(1)}, u32[]{:S(2)}, u32[]{:S(2)}) collective-permute-start(f32[8,128]{1,0:T(8,128)S(1)} %add.16), channel_id=1, source_target_pairs={{0,4},{1,5},{2,6},{3,7},{4,0},{5,1},{6,2},{7,3},{8,12},{9,13},{10,... | collective-permute-start | bytes 12296 | tf_op jit(solution)/shard_map/ppermute | solution.py:629
  45.8 1.6 %collective-permute-done.6 = f32[8,128]{1,0:T(8,128)S(1)} collective-permute-done((f32[8,128]{1,0:T(8,128)S(1)}, f32[8,128]{1,0:T(8,128)S(1)}, u32[]{:S(2)}, u32[]{:S(2)}) %collective-permute-start.6) | collective-permute-done | bytes 4128 | tf_op jit(solution)/shard_map/ppermute | solution.py:629
  47.4 3.0 %collective-permute-start.7 = (f32[8,128]{1,0:T(8,128)S(1)}, f32[8,128]{1,0:T(8,128)S(1)}, u32[]{:S(2)}, u32[]{:S(2)}) collective-permute-start(f32[8,128]{1,0:T(8,128)S(1)} %add.17), channel_id=1, source_target_pairs={{0,8},{1,9},{2,10},{3,11},{4,12},{5,13},{6,14},{7,15},{8,0},{9,1},... | collective-permute-start | bytes 12296 | tf_op jit(solution)/shard_map/ppermute | solution.py:629
  50.4 1.6 %collective-permute-done.7 = f32[8,128]{1,0:T(8,128)S(1)} collective-permute-done((f32[8,128]{1,0:T(8,128)S(1)}, f32[8,128]{1,0:T(8,128)S(1)}, u32[]{:S(2)}, u32[]{:S(2)}) %collective-permute-start.7) | collective-permute-done | bytes 4128 | tf_op jit(solution)/shard_map/ppermute | solution.py:629
  52.0 0.6 %add_reduce_fusion = f32[]{:T(128)} fusion(f32[8,128]{1,0:T(8,128)S(1)} %add.17, f32[8,128]{1,0:T(8,128)S(1)} %collective-permute-done.7), kind=kLoop, calls=%fused_computation | loop fusion | flops 2047 | bytes 8196 | tf_op jit(solution)/shard_map/reduce_sum | solution.py:745
  (14 shorter events, 0.0 us)
Async XLA Ops:
  3.3 1.9 %copy-start = (f32[4,16,96,128]{3,2,1,0:T(8,128)S(1)}, f32[4,16,96,128]{3,2,1,0:T(8,128)}, u32[]{:S(2)}) copy-start(f32[4,16,96,128]{3,2,1,0:T(8,128)} %layer.3) | copy-start | bytes 9437188
  5.2 1.4 %copy-start.1 = (f32[2,16,96,128]{3,2,1,0:T(8,128)S(1)}, f32[2,16,96,128]{3,2,1,0:T(8,128)}, u32[]{:S(2)}) copy-start(f32[2,16,96,128]{3,2,1,0:T(8,128)} %wave.3) | copy-start | bytes 4718596
  6.6 1.1 %copy-start.2 = (f32[16,96,128]{2,1,0:T(8,128)S(1)}, f32[16,96,128]{2,1,0:T(8,128)}, u32[]{:S(2)}) copy-start(f32[16,96,128]{2,1,0:T(8,128)} %source.3) | copy-start | bytes 2359300
  7.8 0.7 %copy-start.4 = (f32[16]{0:T(128)S(1)}, f32[16]{0:T(128)}, u32[]{:S(2)}) copy-start(f32[16]{0:T(128)} %table.3) | copy-start | bytes 196
  8.4 5.0 %copy-start.3 = (f32[16,96,128]{2,1,0:T(8,128)S(1)}, f32[16,96,128]{2,1,0:T(8,128)}, u32[]{:S(2)}) copy-start(f32[16,96,128]{2,1,0:T(8,128)} %filtered.1) | copy-start | bytes 2359300
  12.2 9.6 %collective-permute-start.2 = (f32[800,128]{1,0:T(8,128)S(1)}, f32[800,128]{1,0:T(8,128)S(1)}, u32[]{:S(2)}, u32[]{:S(2)}) collective-permute-start(f32[800,128]{1,0:T(8,128)S(1)} %get-tuple-element.30), channel_id=1, source_target_pairs={{0,1},{1,0},{2,3},{3,2},{4,5},{5,4},{6,7},{7,6},{8,9},{9,8},{10,11... | collective-permute-start | bytes 1228808 | tf_op jit(solution)/shard_map/ppermute | solution.py:668
  12.8 9.1 %collective-permute-start.3 = (f32[800,128]{1,0:T(8,128)S(1)}, f32[800,128]{1,0:T(8,128)S(1)}, u32[]{:S(2)}, u32[]{:S(2)}) collective-permute-start(f32[800,128]{1,0:T(8,128)S(1)} %get-tuple-element.31), channel_id=1, source_target_pairs={{1,2},{2,1},{3,4},{4,3},{5,6},{6,5},{7,8},{8,7},{9,10},{10,9},{11,... | collective-permute-start | bytes 1228808 | tf_op jit(solution)/shard_map/ppermute | solution.py:669
  13.5 8.4 %copy-start.5 = (f32[16]{0:T(128)S(1)}, f32[16]{0:T(128)}, u32[]{:S(2)}) copy-start(f32[16]{0:T(128)} %table.3) | copy-start | bytes 196
  17.2 12.9 %collective-permute-start = (f32[4,96,128]{2,1,0:T(8,128)S(1)}, f32[4,96,128]{2,1,0:T(8,128)S(1)}, u32[]{:S(2)}, u32[]{:S(2)}) collective-permute-start(f32[4,96,128]{2,1,0:T(8,128)S(1)} %get-tuple-element.28), channel_id=1, source_target_pairs={{0,1},{1,0},{2,3},{3,2},{4,5},{5,4},{6,7},{7,6},{8,9},{9,8},{10,11... | collective-permute-start | bytes 589832 | tf_op jit(solution)/shard_map/ppermute | solution.py:686
  21.2 8.9 %collective-permute-start.1 = (f32[4,96,128]{2,1,0:T(8,128)S(1)}, f32[4,96,128]{2,1,0:T(8,128)S(1)}, u32[]{:S(2)}, u32[]{:S(2)}) collective-permute-start(f32[4,96,128]{2,1,0:T(8,128)S(1)} %get-tuple-element.29), channel_id=1, source_target_pairs={{1,2},{2,1},{3,4},{4,3},{5,6},{6,5},{7,8},{8,7},{9,10},{10,9},{11,... | collective-permute-start | bytes 589832 | tf_op jit(solution)/shard_map/ppermute | solution.py:687
  31.6 5.6 %collective-permute-start.4 = (f32[8,128]{1,0:T(8,128)S(1)}, f32[8,128]{1,0:T(8,128)S(1)}, u32[]{:S(2)}, u32[]{:S(2)}) collective-permute-start(f32[8,128]{1,0:T(8,128)S(1)} %get-tuple-element.49), channel_id=1, source_target_pairs={{0,1},{1,0},{2,3},{3,2},{4,5},{5,4},{6,7},{7,6},{8,9},{9,8},{10,11... | collective-permute-start | bytes 12296 | tf_op jit(solution)/shard_map/ppermute | solution.py:629
  37.2 6.4 %collective-permute-start.5 = (f32[8,128]{1,0:T(8,128)S(1)}, f32[8,128]{1,0:T(8,128)S(1)}, u32[]{:S(2)}, u32[]{:S(2)}) collective-permute-start(f32[8,128]{1,0:T(8,128)S(1)} %add.15), channel_id=1, source_target_pairs={{0,2},{1,3},{2,0},{3,1},{4,6},{5,7},{6,4},{7,5},{8,10},{9,11},{10,... | collective-permute-start | bytes 12296 | tf_op jit(solution)/shard_map/ppermute | solution.py:629
  43.6 3.8 %collective-permute-start.6 = (f32[8,128]{1,0:T(8,128)S(1)}, f32[8,128]{1,0:T(8,128)S(1)}, u32[]{:S(2)}, u32[]{:S(2)}) collective-permute-start(f32[8,128]{1,0:T(8,128)S(1)} %add.16), channel_id=1, source_target_pairs={{0,4},{1,5},{2,6},{3,7},{4,0},{5,1},{6,2},{7,3},{8,12},{9,13},{10,... | collective-permute-start | bytes 12296 | tf_op jit(solution)/shard_map/ppermute | solution.py:629
  47.4 4.6 %collective-permute-start.7 = (f32[8,128]{1,0:T(8,128)S(1)}, f32[8,128]{1,0:T(8,128)S(1)}, u32[]{:S(2)}, u32[]{:S(2)}) collective-permute-start(f32[8,128]{1,0:T(8,128)S(1)} %add.17), channel_id=1, source_target_pairs={{0,8},{1,9},{2,10},{3,11},{4,12},{5,13},{6,14},{7,15},{8,0},{9,1},... | collective-permute-start | bytes 12296 | tf_op jit(solution)/shard_map/ppermute | solution.py:629

commit v2 on v1

v2 whole, which is shorter than its diff:
```python
import functools
import math

import jax
import jax.numpy as jnp
from jax import lax
from jax.experimental import pallas as pl
from jax.experimental.pallas import tpu as pltpu
from jax.sharding import PartitionSpec as P

F32 = jnp.float32
BF16 = jnp.bfloat16
STEPS = 3
BLK = 8
REACH = 4
TIME_STEP = 0.25
DAMP_PEAK = 1.5
STENCIL = (-205.0 / 72.0, 8.0 / 5.0, -1.0 / 5.0, 8.0 / 315.0, -1.0 / 560.0)
SCALE = 5040.0
WHOLE = (-14336.0, 8064.0, -1008.0, 128.0, -9.0)
CENTRE_REST = 14.0 / SCALE
TAG_ROWS = 16
KAPPA, KAPPA_R, Q0, Q1, Q2, B0, B1, B2, DECAY, PAIR, AMP, BACK, STIFF, FORCE = range(14)
N_COEF = 14
VMEM_LIMIT = 30 * 1024 * 1024


def band(rows, cols, row_period, col_period):
    row = lax.broadcasted_iota(jnp.int32, (rows, cols), 0) % row_period
    col = lax.broadcasted_iota(jnp.int32, (rows, cols), 1) % col_period
    apart = jnp.abs(row - col)
    out = jnp.zeros((rows, cols), F32)
    for offset, value in enumerate(WHOLE):
        out = jnp.where(apart == offset, value, out)
    return out.astype(BF16)


def pieces(cells):
    high = cells.astype(BF16)
    return high, (cells - high.astype(F32)).astype(BF16)


def cross_diffs(planes, read, write_y, write_z, ny, nz):
    mat_y = band(ny, 2 * ny, ny, ny)
    mat_z = band(2 * nz, nz, nz, nz)
    for one, two in zip(planes[0::2], planes[1::2]):
        high_one, low_one = pieces(read(one))
        high_two, low_two = pieces(read(two))
        upper = jnp.concatenate([high_one, high_two], axis=1)
        lower = jnp.concatenate([low_one, low_two], axis=1)
        diff_y = jnp.dot(
            mat_y, jnp.concatenate([upper, lower], axis=0), preferred_element_type=F32
        )
        write_y(one, diff_y[:, :nz])
        write_y(two, diff_y[:, nz:])
        left = jnp.concatenate([high_one, low_one], axis=1)
        right = jnp.concatenate([high_two, low_two], axis=1)
        diff_z = jnp.dot(
            jnp.concatenate([left, right], axis=0), mat_z, preferred_element_type=F32
        )
        write_z(one, diff_z[:ny])
        write_z(two, diff_z[ny:])


def first_diff(cells, at):
    total = STENCIL[0] * cells[at]
    for offset in range(1, REACH + 1):
        above, below = cells.get(at + offset), cells.get(at - offset)
        if above is not None and below is not None:
            total = total + STENCIL[offset] * (above + below)
        elif above is not None:
            total = total + STENCIL[offset] * above
        elif below is not None:
            total = total + STENCIL[offset] * below
    return total


def outer_part(cells, at, positions):
    total = None
    for position in positions:
        offset = abs(position - at)
        if offset <= REACH:
            term = STENCIL[offset] * cells[position]
            total = term if total is None else total + term
    return total


def advance(cells, previous, memory, stiff, forcing, diffs, co, phase):
    rest = CENTRE_REST * cells
    diffs = [diffs[0], diffs[1] * (1.0 / SCALE) - rest, diffs[2] * (1.0 / SCALE) - rest]
    memory = [m + co(Q0 + d) * (diffs[d] - m) for d, m in enumerate(memory)]
    inner = sum(diffs[d] - co(B0 + d) * memory[d] for d in range(3))
    stiff = co(DECAY) * stiff + co(PAIR) * cells
    new = (
        co(AMP) * cells
        - co(BACK) * previous
        + co(KAPPA) * inner
        - co(STIFF) * stiff
        - (co(FORCE) * phase) * forcing
    )
    return new, memory, stiff


def coefficients(speed_square, bits):
    rates = [DAMP_PEAK * bit for bit in bits]
    damping = rates[0] + rates[1] + rates[2]
    pairing = rates[0] * rates[1] + rates[1] * rates[2] + rates[2] * rates[0]
    retention = [jnp.exp(-TIME_STEP * rate) for rate in rates]
    half = 0.5 * TIME_STEP * damping
    inverse = 1.0 / (1.0 + half)
    square = TIME_STEP * TIME_STEP
    kappa = square * speed_square * inverse
    return (
        kappa,
        kappa * retention[0],
        1.0 - retention[0],
        1.0 - retention[1],
        1.0 - retention[2],
        bits[0],
        bits[1],
        bits[2],
        jnp.exp(-TIME_STEP * damping),
        TIME_STEP * pairing,
        (2.0 - square * pairing) * inverse,
        (1.0 - half) * inverse,
        square * damping * inverse,
        square * inverse,
    )


def along_last(tiles, nz):
    row = lax.broadcasted_iota(jnp.int32, (nz, nz), 0)
    col = lax.broadcasted_iota(jnp.int32, (nz, nz), 1) // BLK
    along = (row == col).astype(F32).astype(BF16)
    return jnp.dot(tiles.astype(BF16), along, preferred_element_type=F32)


def squares(index, table):
    speed = jnp.zeros_like(index)
    for entry in range(table.shape[0]):
        speed = jnp.where(index == float(entry), table[entry], speed)
    return speed * speed


def bits_of(mask):
    mask = mask.astype(jnp.int32)
    return [((mask >> direction) & 1).astype(F32) for direction in range(3)]


def down_second(ref, lead, value, ny):
    for block in range(ny // BLK):
        rows = jnp.broadcast_to(value[block : block + 1], (BLK, value.shape[1]))
        ref[(*lead, pl.ds(block * BLK, BLK))] = rows


def fill_clock(clock, freq, start):
    steps = lax.broadcasted_iota(jnp.int32, clock.shape[1:], 0).astype(F32)
    cosine = jnp.cos(freq[0] * (start[0] + steps * TIME_STEP))
    weight = (TIME_STEP * freq[0] / math.pi) * (cosine - 0.25)
    for count in range(STEPS):
        clock[count] = jnp.broadcast_to(cosine[count : count + 1], cosine.shape)
        clock[STEPS + count] = jnp.broadcast_to(weight[count + 1 : count + 2], weight.shape)


def over_rows(ny, step):
    def one(block, carry):
        step(pl.multiple_of(block * BLK, BLK))
        return carry

    lax.fori_loop(0, ny // BLK, one, 0)


def is_even():
    return lax.axis_index("gx") % 2 == 0


def edge_planes(nx):
    return [*range(REACH), *range(nx - REACH, nx)]


def send_kernel(
    wave, layer, source, freq, start, table_in, index_in, mask_in,
    inside, across, coef, clock, edge,
    u0, strips, diff_y, diff_z, tags, index, mask, table, sems,
):
    nx, ny, nz = u0.shape
    n_block = nx // BLK
    edges = (0, nx - REACH)
    copies = [pltpu.make_async_copy(wave.at[0], u0, sems.at[0])]
    small = [
        pltpu.make_async_copy(one, to, sems.at[7 + number])
        for number, (one, to) in enumerate(
            ((index_in, index), (mask_in, mask), (table_in, table))
        )
    ]
    for side in range(2):
        at = pl.ds(edges[side], REACH)
        copies += [
            pltpu.make_async_copy(wave.at[1, at], strips.at[side, 0], sems.at[1 + 3 * side]),
            pltpu.make_async_copy(
                layer.at[:, at], strips.at[side, pl.ds(1, 4)], sems.at[2 + 3 * side]
            ),
            pltpu.make_async_copy(source.at[at], strips.at[side, 5], sems.at[3 + 3 * side]),
        ]
    for copy in small + copies:
        copy.start()
    even = is_even()
    tags[...] = jnp.zeros_like(tags)
    fill_clock(clock, freq, start)
    phase = clock[0]
    for copy in small:
        copy.wait()
    rows = n_block * TAG_ROWS
    for block in range(n_block):
        at = pl.ds(block * TAG_ROWS, index.shape[0])
        tags[0, at, : index.shape[2]] = index[:, block].astype(F32)
        tags[1, at, : mask.shape[2]] = mask[:, block].astype(F32)
    wide = along_last(tags[...].reshape(2 * rows, nz), nz)
    square = squares(wide[:rows], table)
    masks = wide[rows:]
    values = coefficients(square, bits_of(masks))
    for entry, value in enumerate(values):
        for block in range(n_block):
            down_second(coef, (entry, block), value[block * TAG_ROWS : (block + 1) * TAG_ROWS], ny)
    for part, value in enumerate((square, masks)):
        to = pl.ds(2 * REACH * ny + part * TAG_ROWS, TAG_ROWS)
        left, right = value[:TAG_ROWS], value[rows - TAG_ROWS :]
        inside[to] = jnp.where(even, right, left)
        across[to] = jnp.where(even, left, right)
    copies[0].wait()
    planes = edge_planes(nx)
    slot = {plane: number for number, plane in enumerate(planes)}

    def put_y(plane, value):
        diff_y[slot[plane]] = value

    def put_z(plane, value):
        diff_z[slot[plane]] = value

    cross_diffs(planes, lambda plane: u0[plane], put_y, put_z, ny, nz)
    for copy in copies[1:]:
        copy.wait()

    def step(rows):
        at = pl.ds(rows, BLK)
        sides = []
        for side in range(2):
            block = side * (n_block - 1)
            reach = range(2 * REACH) if side == 0 else range(nx - 2 * REACH, nx)
            cells = {plane: u0[plane, at] for plane in reach}
            values = []
            for number in range(REACH):
                plane = edges[side] + number
                new, memory, stiff = advance(
                    cells[plane],
                    strips[side, 0, number, at],
                    [strips[side, 1 + d, number, at] for d in range(3)],
                    strips[side, 4, number, at],
                    strips[side, 5, number, at],
                    [
                        first_diff(cells, plane),
                        diff_y[slot[plane], at],
                        diff_z[slot[plane], at],
                    ],
                    lambda entry, block=block: coef[entry, block, at],
                    phase,
                )
                for entry, value in enumerate((new, *memory, stiff)):
                    edge[side, entry, number, at] = value
                values.append((cells[plane], new))
            sides.append(values)
        for number in range(REACH):
            for part in range(2):
                to = pl.ds(pl.multiple_of((part * REACH + number) * ny + rows, BLK), BLK)
                left, right = sides[0][number][part], sides[1][number][part]
                inside[to] = jnp.where(even, right, left)
                across[to] = jnp.where(even, left, right)

    over_rows(ny, step)


def local_kernel(
    wave, layer, source, running, coef, clock, edge,
    inside, across, first_out, second_out, run_out,
    fields, diff_y, diff_z,
):
    _, nx, ny, nz = wave.shape
    even = is_even()

    def put_y(plane, value):
        diff_y[plane] = value

    def put_z(plane, value):
        diff_z[plane] = value

    middle = range(REACH, nx - REACH)
    cross_diffs(middle, lambda plane: wave[0, plane], put_y, put_z, ny, nz)

    def read(entry, plane, at=slice(None)):
        if plane < REACH:
            return edge[0, entry, plane, at]
        if plane >= nx - REACH:
            return edge[1, entry, plane - nx + REACH, at]
        if entry == 0:
            return first_out[plane - REACH, at]
        return fields[entry - 1, plane - REACH, at]

    def first(rows):
        at = pl.ds(rows, BLK)
        cells = {plane: wave[0, plane, at] for plane in range(nx)}
        for plane in middle:
            new, memory, stiff = advance(
                cells[plane],
                wave[1, plane, at],
                [layer[d, plane, at] for d in range(3)],
                layer[3, plane, at],
                source[plane, at],
                [first_diff(cells, plane), diff_y[plane, at], diff_z[plane, at]],
                lambda entry, block=plane // BLK: coef[entry, block, at],
                clock[0],
            )
            first_out[plane - REACH, at] = new
            for entry, value in enumerate((*memory, stiff)):
                fields[entry, plane - REACH, at] = value

    over_rows(ny, first)
    cross_diffs(range(nx), lambda plane: read(0, plane), put_y, put_z, ny, nz)

    def second(rows):
        at = pl.ds(rows, BLK)
        cells = {plane: read(0, plane, at) for plane in range(nx)}
        values = {}
        for plane in range(nx):
            new, memory, stiff = advance(
                cells[plane],
                wave[0, plane, at],
                [read(1 + d, plane, at) for d in range(3)],
                read(4, plane, at),
                source[plane, at],
                [first_diff(cells, plane), diff_y[plane, at], diff_z[plane, at]],
                lambda entry, block=plane // BLK: coef[entry, block, at],
                clock[1],
            )
            values[plane] = new
            for entry, value in enumerate((new, *memory, stiff)):
                second_out[entry, plane, at] = value
            run_out[plane, at] = (
                running[plane, at] + clock[STEPS] * cells[plane] + clock[STEPS + 1] * new
            )
        for number in range(REACH):
            left, right = values[number], values[nx - REACH + number]
            inside[number, at] = jnp.where(even, right, left)
            across[number, at] = jnp.where(even, left, right)

    over_rows(ny, second)


def joint_kernel(
    coef, clock, inside, across, wave, forcing, edge, first_in, second_in, run_in,
    out_state, out_layer, out_filtered, ghost, partial,
    ext, bump, push, ghost_coef, diff_y, diff_z, bump_y, bump_z,
):
    _, nx, ny, nz = wave.shape
    count = lax.axis_size("gx")
    place = lax.axis_index("gx")
    even = is_even()
    n_block = nx // BLK
    present = (
        jnp.where(place > 0, 1.0, 0.0).astype(F32),
        jnp.where(place < count - 1, 1.0, 0.0).astype(F32),
    )
    weights = [clock[STEPS + number] for number in range(STEPS)]
    ghosts = (range(-REACH, 0), range(nx, nx + REACH))
    owned = (range(REACH), range(nx - REACH, nx))
    nearby = (range(REACH, 2 * REACH), range(nx - 2 * REACH, nx - REACH))

    def slot(position):
        return position + REACH if position < nx // 2 else position - nx + 3 * REACH

    def received(to):
        one, two = inside[to], across[to]
        return jnp.where(even, two, one), jnp.where(even, one, two)

    tag_at = 2 * REACH * ny
    tiles = [received(pl.ds(tag_at + part * TAG_ROWS, TAG_ROWS)) for part in range(2)]
    for side in range(2):
        values = coefficients(tiles[0][side] * present[side], bits_of(tiles[1][side]))
        for entry, value in enumerate(
            (
                values[KAPPA_R],
                values[Q0],
                values[KAPPA] * (1.0 - values[Q1]),
                values[KAPPA] * (1.0 - values[Q2]),
                values[AMP] - values[STIFF] * values[PAIR],
            )
        ):
            down_second(ghost_coef, (side, entry), value, ny)

    def exchange(rows):
        at = pl.ds(rows, BLK)
        halo = {}
        sent = {}
        for number in range(REACH):
            to = pl.ds(pl.multiple_of(number * ny + rows, BLK), BLK)
            halo[-REACH + number], halo[nx + number] = received(to)
            to = pl.ds(pl.multiple_of((REACH + number) * ny + rows, BLK), BLK)
            sent[-REACH + number], sent[nx + number] = received(to)
        for side in range(2):
            mine = {plane: wave[0, plane, at] for plane in owned[side]}
            kappa_r = coef[KAPPA_R, side * (n_block - 1), at]
            for number, plane in enumerate(owned[side]):
                outer = outer_part(halo, plane, ghosts[side])
                added = kappa_r * outer
                push[slot(plane), at] = outer
                bump[slot(plane), at] = added
                ext[slot(plane), at] = edge[side, 0, number, at] + added
            kappa_r = ghost_coef[side, 0, at]
            for position in ghosts[side]:
                outer = outer_part(mine, position, owned[side])
                added = kappa_r * outer
                push[slot(position), at] = outer
                bump[slot(position), at] = added
                ext[slot(position), at] = sent[position] + added

    over_rows(ny, exchange)

    def put_bump_y(plane, value):
        bump_y[plane] = value

    def put_bump_z(plane, value):
        bump_z[plane] = value

    cross_diffs(range(4 * REACH), lambda plane: bump[plane], put_bump_y, put_bump_z, ny, nz)

    def respond(added, first, position, others, outer, q0, kappas, at):
        kappa_r, kappa_1, kappa_2, grown = kappas
        value = added[position]
        rest = CENTRE_REST * value
        along = first_diff(added, position) + outer_part(first, position, others)
        side_y = bump_y[slot(position), at] * (1.0 / SCALE) - rest
        side_z = bump_z[slot(position), at] * (1.0 / SCALE) - rest
        gain = (
            grown * value + kappa_r * (along - q0 * outer) + kappa_1 * side_y + kappa_2 * side_z
        )
        return gain, along, side_y, side_z

    def second(rows):
        at = pl.ds(rows, BLK)
        for side in range(2):
            block = side * (n_block - 1)
            first = {
                position: ext[slot(position), at] for position in (*ghosts[side], *owned[side])
            }
            added = {position: bump[slot(position), at] for position in ghosts[side]}
            kappa_r, q0, kappa_1, kappa_2, grown = [
                ghost_coef[side, entry, at] for entry in range(5)
            ]
            for number, position in enumerate(ghosts[side]):
                outer = push[slot(position), at]
                ghost[side * REACH + number, at], _, _, _ = respond(
                    added, first, position, owned[side], outer, q0,
                    (kappa_r, kappa_1, kappa_2, grown), at,
                )
            added = {position: bump[slot(position), at] for position in owned[side]}
            kappa_r, kappa = coef[KAPPA_R, block, at], coef[KAPPA, block, at]
            q0, q1, q2 = [coef[entry, block, at] for entry in (Q0, Q1, Q2)]
            pair = coef[PAIR, block, at]
            kappas = (
                kappa_r,
                kappa * (1.0 - q1),
                kappa * (1.0 - q2),
                coef[AMP, block, at] - coef[STIFF, block, at] * pair,
            )
            for plane in owned[side]:
                outer = push[slot(plane), at]
                gain, along, side_y, side_z = respond(
                    added, first, plane, ghosts[side], outer, q0, kappas, at
                )
                out_state[1, plane, at] = second_in[0, plane, at] + gain
                out_layer[0, plane, at] = second_in[1, plane, at] + q0 * (
                    along + (1.0 - q0) * outer
                )
                out_layer[1, plane, at] = second_in[2, plane, at] + q1 * side_y
                out_layer[2, plane, at] = second_in[3, plane, at] + q2 * side_z
                out_layer[3, plane, at] = second_in[4, plane, at] + pair * added[plane]
                out_filtered[plane, at] = (
                    run_in[plane, at] + weights[0] * added[plane] + weights[1] * gain
                )
            for plane in nearby[side]:
                along = outer_part(added, plane, owned[side])
                gain = kappa_r * along
                out_state[1, plane, at] = second_in[0, plane, at] + gain
                out_layer[0, plane, at] = second_in[1, plane, at] + q0 * along
                out_filtered[plane, at] = run_in[plane, at] + weights[1] * gain
        for plane in range(2 * REACH, nx - 2 * REACH):
            out_state[1, plane, at] = second_in[0, plane, at]
            out_layer[0, plane, at] = second_in[1, plane, at]
            out_filtered[plane, at] = run_in[plane, at]

    over_rows(ny, second)

    def put_y(plane, value):
        diff_y[plane] = value

    def put_z(plane, value):
        diff_z[plane] = value

    cross_diffs(range(nx), lambda plane: out_state[1, plane], put_y, put_z, ny, nz)
    partial[...] = jnp.zeros_like(partial)

    def third(rows):
        at = pl.ds(rows, BLK)
        cells = {plane: out_state[1, plane, at] for plane in range(nx)}
        total = partial[...]
        for plane in range(nx):
            at_edge = plane < REACH or plane >= nx - REACH
            if at_edge:
                previous = ext[slot(plane), at]
                fields = [out_layer[d, plane, at] for d in range(4)]
            else:
                previous = first_in[plane - REACH, at]
                fields = [out_layer[0, plane, at]]
                fields += [second_in[1 + d, plane, at] for d in range(1, 4)]
            value, memory, stiff = advance(
                cells[plane],
                previous,
                fields[:3],
                fields[3],
                forcing[plane, at],
                [first_diff(cells, plane), diff_y[plane, at], diff_z[plane, at]],
                lambda entry, block=plane // BLK: coef[entry, block, at],
                clock[2],
            )
            done = out_filtered[plane, at] + weights[2] * value
            for d in range(3):
                out_layer[d, plane, at] = memory[d]
            out_layer[3, plane, at] = stiff
            out_state[0, plane, at] = value
            out_filtered[plane, at] = done
            if not at_edge:
                total = total + done * done
        partial[...] = total

    over_rows(ny, third)


def finish_kernel(
    coef, clock, inside, across, ghost, partial, state_in, layer_in, filtered_in,
    out_state, out_layer, out_filtered, total_out,
):
    _, nx, ny, _ = state_in.shape
    n_block = nx // BLK
    even = is_even()
    weight = clock[2 * STEPS - 1]
    total_out[...] = partial[...]
    ghosts = (range(-REACH, 0), range(nx, nx + REACH))
    owned = (range(REACH), range(nx - REACH, nx))

    def step(rows):
        at = pl.ds(rows, BLK)
        halo = {}
        for number in range(REACH):
            one, two = inside[number, at], across[number, at]
            halo[-REACH + number] = jnp.where(even, two, one) + ghost[number, at]
            halo[nx + number] = jnp.where(even, one, two) + ghost[REACH + number, at]
        total = total_out[...]
        for side in range(2):
            block = side * (n_block - 1)
            kappa_r, q0 = coef[KAPPA_R, block, at], coef[Q0, block, at]
            for plane in owned[side]:
                outer = outer_part(halo, plane, ghosts[side])
                added = kappa_r * outer
                out_state[0, plane, at] = state_in[0, plane, at] + added
                out_layer[0, plane, at] = layer_in[0, plane, at] + q0 * outer
                done = filtered_in[plane, at] + weight * added
                out_filtered[plane, at] = done
                total = total + done * done
        total_out[...] = total

    over_rows(ny, step)


def store_kernel(values, held_array, out, values_out, sem):
    copy = pltpu.make_async_copy(held_array, out, sem)
    copy.start()
    values_out[...] = values[...]
    copy.wait()


SCALAR = pl.BlockSpec(memory_space=pltpu.SMEM)
HBM = pl.BlockSpec(memory_space=pltpu.HBM)
VEC = pl.BlockSpec(memory_space=pltpu.VMEM)


def held(*shape):
    return pltpu.VMEM(shape, F32)


def in_vmem(*arrays):
    return [pltpu.with_memory_space_constraint(array, pltpu.VMEM) for array in arrays]


def in_hbm(*arrays):
    return [pltpu.with_memory_space_constraint(array, pltpu.HBM) for array in arrays]


def call(kernel, name, in_specs, out_shape, out_specs, scratch, operands, micros, aliases=None):
    return pl.pallas_call(
        kernel,
        name=name,
        in_specs=in_specs,
        out_shape=out_shape,
        out_specs=out_specs,
        scratch_shapes=scratch,
        input_output_aliases=aliases or {},
        compiler_params=pltpu.CompilerParams(vmem_limit_bytes=VMEM_LIMIT),
        cost_estimate=pl.CostEstimate(
            flops=0, bytes_accessed=int(micros * 3.6e6), transcendentals=0
        ),
    )(*operands)


def swap_pairs(count):
    inside = [(i, i ^ 1) for i in range(count)]
    across = []
    for i in range(1, count - 1, 2):
        across += [(i, i + 1), (i + 1, i)]
    return inside, across


def store(values, array):
    return call(
        store_kernel,
        "store",
        [VEC] * 2,
        [jax.ShapeDtypeStruct(array.shape, F32), held(*values.shape)],
        [HBM, VEC],
        [pltpu.SemaphoreType.DMA],
        in_vmem(values, array),
        1,
    )


def total_and_stores(values, arrays, axis):
    count = lax.axis_size(axis)
    stored = []
    if count & (count - 1):
        for array in arrays:
            stored.append(store(values, array)[0])
        return lax.psum(values, axis), stored
    hop = 1
    while hop < count:
        got = lax.ppermute(values, axis, [(i, i ^ hop) for i in range(count)])
        if len(stored) < len(arrays):
            done, values = store(values, arrays[len(stored)])
            stored.append(done)
        values = values + got
        hop *= 2
    for array in arrays[len(stored) :]:
        stored.append(store(values, array)[0])
    return values, stored


def body(
    wave_state, layer_fields, source, filtered, frequency, start_time, speed_table, speed_index,
    pml_mask,
):
    _, nx, ny, nz = wave_state.shape
    n_block = nx // BLK
    count = lax.axis_size("gx")
    pair_inside, pair_across = swap_pairs(count)
    brick = (nx, ny, nz)
    strip = (REACH, ny, nz)
    message = (2 * REACH * ny + 2 * TAG_ROWS, nz)
    dma = pltpu.SemaphoreType.DMA
    vec = lambda *shape: pltpu.VMEM(shape, F32)

    blocks = (speed_index.shape[1], n_block, speed_index.shape[2])
    index, mask = in_hbm(*(jnp.transpose(one, (1, 0, 2)) for one in (speed_index, pml_mask)))

    inside, across, coef, clock, edge = call(
        send_kernel,
        "strips",
        [HBM] * 3 + [SCALAR] * 2 + [HBM] * 3,
        [
            held(*message), held(*message), held(N_COEF, n_block, ny, nz),
            held(2 * STEPS, BLK, nz), held(2, 5, *strip),
        ],
        [VEC] * 5,
        [
            vec(*brick),
            vec(2, 6, *strip),
            vec(2 * REACH, ny, nz),
            vec(2 * REACH, ny, nz),
            vec(2, n_block * TAG_ROWS, nz),
            pltpu.VMEM(blocks, jnp.int32),
            pltpu.VMEM(blocks, jnp.int32),
            pltpu.SMEM(speed_table.shape, F32),
            dma((10,)),
        ],
        (
            *in_hbm(wave_state, layer_fields, source), frequency, start_time,
            *in_hbm(speed_table), index, mask,
        ),
        2.5,
    )
    got_inside = lax.ppermute(inside, "gx", pair_inside)
    got_across = lax.ppermute(across, "gx", pair_across)
    coef, clock, edge, wave, layer, forcing, running = in_vmem(
        coef, clock, edge, wave_state, layer_fields, source, filtered
    )

    later_inside, later_across, first, second, run = call(
        local_kernel,
        "local",
        [VEC] * 7,
        [
            held(*strip), held(*strip), held(nx - 2 * REACH, ny, nz), held(5, *brick),
            held(*brick),
        ],
        [VEC] * 5,
        [vec(4, nx - 2 * REACH, ny, nz), vec(*brick), vec(*brick)],
        (wave, layer, forcing, running, coef, clock, edge),
        4,
    )
    last_inside = lax.ppermute(later_inside, "gx", pair_inside)
    last_across = lax.ppermute(later_across, "gx", pair_across)

    out_types = [
        held(*wave_state.shape), held(*layer_fields.shape), held(*filtered.shape)
    ]
    next_state, next_layer, next_filtered, ghost, partial = call(
        joint_kernel,
        "joint",
        [VEC] * 10,
        out_types + [held(2 * REACH, ny, nz), held(BLK, nz)],
        [VEC] * 5,
        [
            vec(4 * REACH, ny, nz),
            vec(4 * REACH, ny, nz),
            vec(4 * REACH, ny, nz),
            vec(2, 5, ny, nz),
            vec(*brick),
            vec(*brick),
            vec(4 * REACH, ny, nz),
            vec(4 * REACH, ny, nz),
        ],
        (
            coef, clock, *in_vmem(got_inside, got_across), wave, forcing, edge,
            *in_vmem(first, second, run),
        ),
        5,
    )
    next_state, next_layer, next_filtered, total = call(
        finish_kernel,
        "finish",
        [VEC] * 9,
        out_types + [held(BLK, nz)],
        [VEC] * 4,
        [],
        (
            coef, clock,
            *in_vmem(
                last_inside, last_across, ghost, partial, next_state, next_layer, next_filtered
            ),
        ),
        1,
        {6: 0, 7: 1, 8: 2},
    )
    total, (next_filtered, next_state, next_layer) = total_and_stores(
        total, [next_filtered, next_state, next_layer], "gx"
    )
    total = jnp.sum(total)
    filter_norm = jnp.sqrt(total / (filtered.size * count) + 1e-06)
    return next_state, next_layer, next_filtered, filter_norm.reshape(1)


def solution(mesh):
    placed = (
        P("grp", "gx", None, None),
        P("grp", "gx", None, None),
        P(("grp", "gx"), None, None),
        P(("grp", "gx"), None, None),
        P("grp"),
        P("grp"),
        P(),
        P("gx", None, None),
        P("gx", None, None),
    )
    return jax.shard_map(
        body,
        mesh=mesh,
        in_specs=placed,
        out_specs=(
            P("grp", "gx", None, None),
            P("grp", "gx", None, None),
            P(("grp", "gx"), None, None),
            P("grp"),
        ),
        check_vma=False,
    )
```

time: 54.8 us -> 42.6 us (0.78)
  local copies, waits for them, and re-layouts: 6.51 us -> 1.14 us
  waiting for transfers between devices: 5.59 us -> 2.09 us
  Pallas kernels: 17.2 us -> 14.7 us
  starting transfers between devices: 20.6 us -> 19.9 us
    unnamed x14 -> x8, local copies, waits for them, and re-layouts: 6.51 us -> 1.14 us
    ppermute x4, waiting for transfers between devices: 5.58 us -> 2.08 us  [total_and_stores(): got = lax.ppermute(values, axis, [(i, i ^ hop) for i in range(count)])]
    pallas_call x4 -> x7, Pallas kernels: 17.2 us -> 14.7 us  [call(): pl.pallas_call(kernel, name=name, in_specs=in_specs, out_shape=out_shape,...]
    ppermute x4, starting transfers between devices: 14.8 us -> 14.1 us  [total_and_stores(): got = lax.ppermute(values, axis, [(i, i ^ hop) for i in range(count)])]
  transfers between devices with their start and end apart: 8 -> 8, of which waited for: 4 -> 2; matrix products, arithmetic and copies ran while one was open for 0% -> 0% of each run, Pallas kernels for 22% -> 26%
where the time goes in v2:
time: 42.6 us; the launch traced here: 42.4 us
  starting transfers between devices  19.9 us (47%)
  Pallas kernels  14.7 us (35%)
  between operations  3.93 us (9%)
  waiting for transfers between devices  2.09 us (5%)
  local copies, waits for them, and re-layouts  1.14 us (3%)
  other arithmetic  0.61 us (1%)
    pallas_call x7, Pallas kernels, call(): pl.pallas_call(kernel, name=name, in_specs=in_specs, out_shape=out_shape,...  14.7 us
    ppermute x4, starting transfers between devices, total_and_stores(): got = lax.ppermute(values, axis, [(i, i ^ hop) for i in range(count)])  14.1 us
    ppermute x1, starting transfers between devices, body(): last_inside = lax.ppermute(later_inside, 'gx', pair_inside)  3.94 us
    ppermute x4, waiting for transfers between devices, total_and_stores(): got = lax.ppermute(values, axis, [(i, i ^ hop) for i in range(count)])  2.08 us
    unnamed x8, local copies, waits for them, and re-layouts  1.14 us
  transfers between devices with their start and end apart: 8, of which 2 were waited for; matrix products, arithmetic and copies ran while one was open for 0% of the time, Pallas kernels for 26%

profile of v2, /device:TPU:0, one launch (start us, length us, event | category | flops | bytes accessed | tf_op | source)
XLA Modules:
  0.0 42.4 jit_solution(16180016225914049362)
XLA Ops:
  2.0 2.9 %strips.1 = (f32[800,128]{1,0:T(8,128)S(1)}, f32[800,128]{1,0:T(8,128)S(1)}, f32[14,2,96,128]{3,2,1,0:T(8,128)S(1)}, f32[6,8,128]{2,1,0:T(8,128)S(1)}, f32[2,5,4,96,128]{4,3,2,1,0:T(8,128)S(1)}) custom-call(f32[2,16,96,128]{3,2,1,0:T(8,128)} %wave.5, f32[4,16,96,128]{3,2,1,0:T(8,128)} %layer.3, f32[16,96,128]{2,1,0:T(8,128)} %forcing.1, f32[1]{0:T(128)S(6)} %copy.19.freq, ...), custom_call_target="tpu_custom_call" | custom-call | bytes 9000000 | tf_op jit(solution)/shard_map/strips/pallas_call | solution.py:608
  4.9 0.5 %collective-permute-start.2 = (f32[800,128]{1,0:T(8,128)S(1)}, f32[800,128]{1,0:T(8,128)S(1)}, u32[]{:S(2)}, u32[]{:S(2)}) collective-permute-start(f32[800,128]{1,0:T(8,128)S(1)} %get-tuple-element.34), channel_id=1, source_target_pairs={{0,1},{1,0},{2,3},{3,2},{4,5},{5,4},{6,7},{7,6},{8,9},{9,8},{10,11... | collective-permute-start | bytes 1228808 | tf_op jit(solution)/shard_map/ppermute | solution.py:707
  5.4 0.7 %collective-permute-start.3 = (f32[800,128]{1,0:T(8,128)S(1)}, f32[800,128]{1,0:T(8,128)S(1)}, u32[]{:S(2)}, u32[]{:S(2)}) collective-permute-start(f32[800,128]{1,0:T(8,128)S(1)} %get-tuple-element.35), channel_id=1, source_target_pairs={{1,2},{2,1},{3,4},{4,3},{5,6},{6,5},{7,8},{8,7},{9,10},{10,9},{11,... | collective-permute-start | bytes 1228808 | tf_op jit(solution)/shard_map/ppermute | solution.py:708
  6.1 0.0 copy-start.3
  6.1 1.1 %copy-done.3 = f32[16,96,128]{2,1,0:T(8,128)S(1)} copy-done((f32[16,96,128]{2,1,0:T(8,128)S(1)}, f32[16,96,128]{2,1,0:T(8,128)}, u32[]{:S(2)}) %copy-start.3) | copy-done | bytes 786456
  7.3 3.3 %local.1 = (f32[4,96,128]{2,1,0:T(8,128)S(1)}, f32[4,96,128]{2,1,0:T(8,128)S(1)}, f32[8,96,128]{2,1,0:T(8,128)S(1)}, f32[5,16,96,128]{3,2,1,0:T(8,128)S(1)}, f32[16,96,128]{2,1,0:T(8,128)S(1)}) custom-call(f32[2,16,96,128]{3,2,1,0:T(8,128)S(1)} %copy-done, f32[4,16,96,128]{3,2,1,0:T(8,128)S(1)} %copy-done.1, f32[16,96,128]{2,1,0:T(8,128)S(1)} %copy-done.2, ...), custom_call_target="tpu_custom_call" | custom-call | bytes 14400000 | tf_op jit(solution)/shard_map/local/pallas_call | solution.py:608
  10.5 3.9 %collective-permute-start = (f32[4,96,128]{2,1,0:T(8,128)S(1)}, f32[4,96,128]{2,1,0:T(8,128)S(1)}, u32[]{:S(2)}, u32[]{:S(2)}) collective-permute-start(f32[4,96,128]{2,1,0:T(8,128)S(1)} %get-tuple-element.32), channel_id=1, source_target_pairs={{0,1},{1,0},{2,3},{3,2},{4,5},{5,4},{6,7},{7,6},{8,9},{9,8},{10,11... | collective-permute-start | bytes 589832 | tf_op jit(solution)/shard_map/ppermute | solution.py:726
  14.5 0.7 %collective-permute-start.1 = (f32[4,96,128]{2,1,0:T(8,128)S(1)}, f32[4,96,128]{2,1,0:T(8,128)S(1)}, u32[]{:S(2)}, u32[]{:S(2)}) collective-permute-start(f32[4,96,128]{2,1,0:T(8,128)S(1)} %get-tuple-element.33), channel_id=1, source_target_pairs={{1,2},{2,1},{3,4},{4,3},{5,6},{6,5},{7,8},{8,7},{9,10},{10,9},{11,... | collective-permute-start | bytes 589832 | tf_op jit(solution)/shard_map/ppermute | solution.py:727
  15.2 0.0 collective-permute-done.2.inside
  15.2 0.0 collective-permute-done.3.across
  15.2 4.2 %joint.1 = (f32[2,16,96,128]{3,2,1,0:T(8,128)S(1)}, f32[4,16,96,128]{3,2,1,0:T(8,128)S(1)}, f32[16,96,128]{2,1,0:T(8,128)S(1)}, f32[8,96,128]{2,1,0:T(8,128)S(1)}, f32[8,128]{1,0:T(8,128)S(1)}) custom-call(f32[14,2,96,128]{3,2,1,0:T(8,128)S(1)} %get-tuple-element.29.coef, f32[6,8,128]{2,1,0:T(8,128)S(1)} %get-tuple-element.30.clock, ...), custom_call_target="tpu_custom_call" | custom-call | bytes 18000000 | tf_op jit(solution)/shard_map/joint/pallas_call | solution.py:608
  19.4 0.0 collective-permute-done.inside
  19.4 0.6 %finish.1 = (f32[2,16,96,128]{3,2,1,0:T(8,128)S(1)}, f32[4,16,96,128]{3,2,1,0:T(8,128)S(1)}, f32[16,96,128]{2,1,0:T(8,128)S(1)}, f32[8,128]{1,0:T(8,128)S(1)}) custom-call(f32[14,2,96,128]{3,2,1,0:T(8,128)S(1)} %get-tuple-element.29.coef, f32[6,8,128]{2,1,0:T(8,128)S(1)} %get-tuple-element.30.clock, ...), custom_call_target="tpu_custom_call", output_to_operand_aliasing={{0}: (6, {}), {1}: (7, {}), {2}: (8, {})} | custom-call | bytes 3600000 | tf_op jit(solution)/shard_map/finish/pallas_call | solution.py:608
  20.0 4.1 %collective-permute-start.4 = (f32[8,128]{1,0:T(8,128)S(1)}, f32[8,128]{1,0:T(8,128)S(1)}, u32[]{:S(2)}, u32[]{:S(2)}) collective-permute-start(f32[8,128]{1,0:T(8,128)S(1)} %get-tuple-element.44.values), channel_id=1, source_target_pairs={{0,1},{1,0},{2,3},{3,2},{4,5},{5,4},{6,7},{7,6},{8,9},{9,8},{10,11... | collective-permute-start | bytes 12296 | tf_op jit(solution)/shard_map/ppermute | solution.py:653
  24.1 0.9 %store.3 = (f32[16,96,128]{2,1,0:T(8,128)}, f32[8,128]{1,0:T(8,128)S(1)}) custom-call(f32[8,128]{1,0:T(8,128)S(1)} %get-tuple-element.44.values, f32[16,96,128]{2,1,0:T(8,128)S(1)} %get-tuple-element.45.held_array), custom_call_target="tpu_custom_call" | custom-call | bytes 3600000 | tf_op jit(solution)/shard_map/store/pallas_call | solution.py:608
  25.0 0.0 collective-permute-done.4
  25.0 2.6 %collective-permute-start.5 = (f32[8,128]{1,0:T(8,128)S(1)}, f32[8,128]{1,0:T(8,128)S(1)}, u32[]{:S(2)}, u32[]{:S(2)}) collective-permute-start(f32[8,128]{1,0:T(8,128)S(1)} %add.15.values), channel_id=1, source_target_pairs={{0,2},{1,3},{2,0},{3,1},{4,6},{5,7},{6,4},{7,5},{8,10},{9,11},{10,... | collective-permute-start | bytes 12296 | tf_op jit(solution)/shard_map/ppermute | solution.py:653
  27.6 1.1 %store.4 = (f32[2,16,96,128]{3,2,1,0:T(8,128)}, f32[8,128]{1,0:T(8,128)S(1)}) custom-call(f32[8,128]{1,0:T(8,128)S(1)} %add.15.values, f32[2,16,96,128]{3,2,1,0:T(8,128)S(1)} %get-tuple-element.47.held_array), custom_call_target="tpu_custom_call" | custom-call | bytes 3600000 | tf_op jit(solution)/shard_map/store/pallas_call | solution.py:608
  28.8 0.4 %collective-permute-done.5 = f32[8,128]{1,0:T(8,128)S(1)} collective-permute-done((f32[8,128]{1,0:T(8,128)S(1)}, f32[8,128]{1,0:T(8,128)S(1)}, u32[]{:S(2)}, u32[]{:S(2)}) %collective-permute-start.5) | collective-permute-done | bytes 4128 | tf_op jit(solution)/shard_map/ppermute | solution.py:653
  29.2 4.5 %collective-permute-start.6 = (f32[8,128]{1,0:T(8,128)S(1)}, f32[8,128]{1,0:T(8,128)S(1)}, u32[]{:S(2)}, u32[]{:S(2)}) collective-permute-start(f32[8,128]{1,0:T(8,128)S(1)} %add.16.values), channel_id=1, source_target_pairs={{0,4},{1,5},{2,6},{3,7},{4,0},{5,1},{6,2},{7,3},{8,12},{9,13},{10,... | collective-permute-start | bytes 12296 | tf_op jit(solution)/shard_map/ppermute | solution.py:653
  33.7 1.7 %store.5 = (f32[4,16,96,128]{3,2,1,0:T(8,128)}, f32[8,128]{1,0:T(8,128)S(1)}) custom-call(f32[8,128]{1,0:T(8,128)S(1)} %add.16.values, f32[4,16,96,128]{3,2,1,0:T(8,128)S(1)} %get-tuple-element.50.held_array), custom_call_target="tpu_custom_call" | custom-call | bytes 3600000 | tf_op jit(solution)/shard_map/store/pallas_call | solution.py:608
  35.4 2.9 %collective-permute-start.7 = (f32[8,128]{1,0:T(8,128)S(1)}, f32[8,128]{1,0:T(8,128)S(1)}, u32[]{:S(2)}, u32[]{:S(2)}) collective-permute-start(f32[8,128]{1,0:T(8,128)S(1)} %add.17), channel_id=1, source_target_pairs={{0,8},{1,9},{2,10},{3,11},{4,12},{5,13},{6,14},{7,15},{8,0},{9,1},... | collective-permute-start | bytes 12296 | tf_op jit(solution)/shard_map/ppermute | solution.py:653
  38.3 1.6 %collective-permute-done.7 = f32[8,128]{1,0:T(8,128)S(1)} collective-permute-done((f32[8,128]{1,0:T(8,128)S(1)}, f32[8,128]{1,0:T(8,128)S(1)}, u32[]{:S(2)}, u32[]{:S(2)}) %collective-permute-start.7) | collective-permute-done | bytes 4128 | tf_op jit(solution)/shard_map/ppermute | solution.py:653
  40.0 0.6 %add_reduce_fusion = f32[]{:T(128)} fusion(f32[8,128]{1,0:T(8,128)S(1)} %add.17, f32[8,128]{1,0:T(8,128)S(1)} %collective-permute-done.7), kind=kLoop, calls=%fused_computation | loop fusion | flops 2047 | bytes 8196 | tf_op jit(solution)/shard_map/reduce_sum | solution.py:773
  (11 shorter events, 0.0 us)
Async XLA Ops:
  1.9 4.2 %copy-start = (f32[2,16,96,128]{3,2,1,0:T(8,128)S(1)}, f32[2,16,96,128]{3,2,1,0:T(8,128)}, u32[]{:S(2)}) copy-start(f32[2,16,96,128]{3,2,1,0:T(8,128)} %wave.5) | copy-start | bytes 4718596
  1.9 4.2 %copy-start.1 = (f32[4,16,96,128]{3,2,1,0:T(8,128)S(1)}, f32[4,16,96,128]{3,2,1,0:T(8,128)}, u32[]{:S(2)}) copy-start(f32[4,16,96,128]{3,2,1,0:T(8,128)} %layer.3) | copy-start | bytes 9437188
  1.9 4.2 %copy-start.2 = (f32[16,96,128]{2,1,0:T(8,128)S(1)}, f32[16,96,128]{2,1,0:T(8,128)}, u32[]{:S(2)}) copy-start(f32[16,96,128]{2,1,0:T(8,128)} %forcing.1) | copy-start | bytes 2359300
  4.9 10.3 %collective-permute-start.2 = (f32[800,128]{1,0:T(8,128)S(1)}, f32[800,128]{1,0:T(8,128)S(1)}, u32[]{:S(2)}, u32[]{:S(2)}) collective-permute-start(f32[800,128]{1,0:T(8,128)S(1)} %get-tuple-element.34), channel_id=1, source_target_pairs={{0,1},{1,0},{2,3},{3,2},{4,5},{5,4},{6,7},{7,6},{8,9},{9,8},{10,11... | collective-permute-start | bytes 1228808 | tf_op jit(solution)/shard_map/ppermute | solution.py:707
  5.4 9.8 %collective-permute-start.3 = (f32[800,128]{1,0:T(8,128)S(1)}, f32[800,128]{1,0:T(8,128)S(1)}, u32[]{:S(2)}, u32[]{:S(2)}) collective-permute-start(f32[800,128]{1,0:T(8,128)S(1)} %get-tuple-element.35), channel_id=1, source_target_pairs={{1,2},{2,1},{3,4},{4,3},{5,6},{6,5},{7,8},{8,7},{9,10},{10,9},{11,... | collective-permute-start | bytes 1228808 | tf_op jit(solution)/shard_map/ppermute | solution.py:708
  6.1 1.1 %copy-start.3 = (f32[16,96,128]{2,1,0:T(8,128)S(1)}, f32[16,96,128]{2,1,0:T(8,128)}, u32[]{:S(2)}) copy-start(f32[16,96,128]{2,1,0:T(8,128)} %running.1) | copy-start | bytes 2359300
  10.5 8.9 %collective-permute-start = (f32[4,96,128]{2,1,0:T(8,128)S(1)}, f32[4,96,128]{2,1,0:T(8,128)S(1)}, u32[]{:S(2)}, u32[]{:S(2)}) collective-permute-start(f32[4,96,128]{2,1,0:T(8,128)S(1)} %get-tuple-element.32), channel_id=1, source_target_pairs={{0,1},{1,0},{2,3},{3,2},{4,5},{5,4},{6,7},{7,6},{8,9},{9,8},{10,11... | collective-permute-start | bytes 589832 | tf_op jit(solution)/shard_map/ppermute | solution.py:726
  14.5 4.9 %collective-permute-start.1 = (f32[4,96,128]{2,1,0:T(8,128)S(1)}, f32[4,96,128]{2,1,0:T(8,128)S(1)}, u32[]{:S(2)}, u32[]{:S(2)}) collective-permute-start(f32[4,96,128]{2,1,0:T(8,128)S(1)} %get-tuple-element.33), channel_id=1, source_target_pairs={{1,2},{2,1},{3,4},{4,3},{5,6},{6,5},{7,8},{8,7},{9,10},{10,9},{11,... | collective-permute-start | bytes 589832 | tf_op jit(solution)/shard_map/ppermute | solution.py:727
  20.0 5.0 %collective-permute-start.4 = (f32[8,128]{1,0:T(8,128)S(1)}, f32[8,128]{1,0:T(8,128)S(1)}, u32[]{:S(2)}, u32[]{:S(2)}) collective-permute-start(f32[8,128]{1,0:T(8,128)S(1)} %get-tuple-element.44.values), channel_id=1, source_target_pairs={{0,1},{1,0},{2,3},{3,2},{4,5},{5,4},{6,7},{7,6},{8,9},{9,8},{10,11... | collective-permute-start | bytes 12296 | tf_op jit(solution)/shard_map/ppermute | solution.py:653
  25.0 4.2 %collective-permute-start.5 = (f32[8,128]{1,0:T(8,128)S(1)}, f32[8,128]{1,0:T(8,128)S(1)}, u32[]{:S(2)}, u32[]{:S(2)}) collective-permute-start(f32[8,128]{1,0:T(8,128)S(1)} %add.15.values), channel_id=1, source_target_pairs={{0,2},{1,3},{2,0},{3,1},{4,6},{5,7},{6,4},{7,5},{8,10},{9,11},{10,... | collective-permute-start | bytes 12296 | tf_op jit(solution)/shard_map/ppermute | solution.py:653
  29.2 6.2 %collective-permute-start.6 = (f32[8,128]{1,0:T(8,128)S(1)}, f32[8,128]{1,0:T(8,128)S(1)}, u32[]{:S(2)}, u32[]{:S(2)}) collective-permute-start(f32[8,128]{1,0:T(8,128)S(1)} %add.16.values), channel_id=1, source_target_pairs={{0,4},{1,5},{2,6},{3,7},{4,0},{5,1},{6,2},{7,3},{8,12},{9,13},{10,... | collective-permute-start | bytes 12296 | tf_op jit(solution)/shard_map/ppermute | solution.py:653
  35.4 4.6 %collective-permute-start.7 = (f32[8,128]{1,0:T(8,128)S(1)}, f32[8,128]{1,0:T(8,128)S(1)}, u32[]{:S(2)}, u32[]{:S(2)}) collective-permute-start(f32[8,128]{1,0:T(8,128)S(1)} %add.17), channel_id=1, source_target_pairs={{0,8},{1,9},{2,10},{3,11},{4,12},{5,13},{6,14},{7,15},{8,0},{9,1},... | collective-permute-start | bytes 12296 | tf_op jit(solution)/shard_map/ppermute | solution.py:653

commit v3 on v2

--- a/solution.py
+++ b/solution.py
@@ -179,29 +179,31 @@
 
 
 def send_kernel(
-    wave, layer, source, freq, start, table_in, index_in, mask_in,
-    inside, across, coef, clock, edge,
-    u0, strips, diff_y, diff_z, tags, index, mask, table, sems,
+    wave_in, layer_in, source_in, freq, start, table_in, index_in, mask_in,
+    inside, across, coef, clock, edge, wave, layer, source,
+    diff_y, diff_z, tags, index, mask, table, sems,
 ):
-    nx, ny, nz = u0.shape
+    _, nx, ny, nz = wave.shape
     n_block = nx // BLK
     edges = (0, nx - REACH)
-    copies = [pltpu.make_async_copy(wave.at[0], u0, sems.at[0])]
+    pieces_of = [(wave_in.at[0], wave.at[0])]
+    for first, length in ((0, REACH), (nx - REACH, REACH), (REACH, nx - 2 * REACH)):
+        at = pl.ds(first, length)
+        pieces_of += [
+            (wave_in.at[1, at], wave.at[1, at]),
+            (layer_in.at[:, at], layer.at[:, at]),
+            (source_in.at[at], source.at[at]),
+        ]
+    copies = [
+        pltpu.make_async_copy(one, to, sems.at[number])
+        for number, (one, to) in enumerate(pieces_of)
+    ]
     small = [
-        pltpu.make_async_copy(one, to, sems.at[7 + number])
+        pltpu.make_async_copy(one, to, sems.at[len(copies) + number])
         for number, (one, to) in enumerate(
             ((index_in, index), (mask_in, mask), (table_in, table))
         )
     ]
-    for side in range(2):
-        at = pl.ds(edges[side], REACH)
-        copies += [
-            pltpu.make_async_copy(wave.at[1, at], strips.at[side, 0], sems.at[1 + 3 * side]),
-            pltpu.make_async_copy(
-                layer.at[:, at], strips.at[side, pl.ds(1, 4)], sems.at[2 + 3 * side]
-            ),
-            pltpu.make_async_copy(source.at[at], strips.at[side, 5], sems.at[3 + 3 * side]),
-        ]
     for copy in small + copies:
         copy.start()
     even = is_even()
@@ -237,8 +239,8 @@
     def put_z(plane, value):
         diff_z[slot[plane]] = value
 
-    cross_diffs(planes, lambda plane: u0[plane], put_y, put_z, ny, nz)
-    for copy in copies[1:]:
+    cross_diffs(planes, lambda plane: wave[0, plane], put_y, put_z, ny, nz)
+    for copy in copies[1:7]:
         copy.wait()
 
     def step(rows):
@@ -247,16 +249,16 @@
         for side in range(2):
             block = side * (n_block - 1)
             reach = range(2 * REACH) if side == 0 else range(nx - 2 * REACH, nx)
-            cells = {plane: u0[plane, at] for plane in reach}
+            cells = {plane: wave[0, plane, at] for plane in reach}
             values = []
             for number in range(REACH):
                 plane = edges[side] + number
                 new, memory, stiff = advance(
                     cells[plane],
-                    strips[side, 0, number, at],
-                    [strips[side, 1 + d, number, at] for d in range(3)],
-                    strips[side, 4, number, at],
-                    strips[side, 5, number, at],
+                    wave[1, plane, at],
+                    [layer[d, plane, at] for d in range(3)],
+                    layer[3, plane, at],
+                    source[plane, at],
                     [
                         first_diff(cells, plane),
                         diff_y[slot[plane], at],
@@ -277,10 +279,12 @@
                 across[to] = jnp.where(even, left, right)
 
     over_rows(ny, step)
+    for copy in copies[7:]:
+        copy.wait()
 
 
 def local_kernel(
-    wave, layer, source, running, coef, clock, edge,
+    wave, layer, source, coef, clock, edge,
     inside, across, first_out, second_out, run_out,
     fields, diff_y, diff_z,
 ):
@@ -344,9 +348,7 @@
             values[plane] = new
             for entry, value in enumerate((new, *memory, stiff)):
                 second_out[entry, plane, at] = value
-            run_out[plane, at] = (
-                running[plane, at] + clock[STEPS] * cells[plane] + clock[STEPS + 1] * new
-            )
+            run_out[plane, at] = clock[STEPS] * cells[plane] + clock[STEPS + 1] * new
         for number in range(REACH):
             left, right = values[number], values[nx - REACH + number]
             inside[number, at] = jnp.where(even, right, left)
@@ -356,7 +358,7 @@
 
 
 def joint_kernel(
-    coef, clock, inside, across, wave, forcing, edge, first_in, second_in, run_in,
+    coef, clock, inside, across, wave, forcing, running, edge, first_in, second_in, run_in,
     out_state, out_layer, out_filtered, ghost, partial,
     ext, bump, push, ghost_coef, diff_y, diff_z, bump_y, bump_z,
 ):
@@ -484,18 +486,21 @@
                 out_layer[2, plane, at] = second_in[3, plane, at] + q2 * side_z
                 out_layer[3, plane, at] = second_in[4, plane, at] + pair * added[plane]
                 out_filtered[plane, at] = (
-                    run_in[plane, at] + weights[0] * added[plane] + weights[1] * gain
+                    running[plane, at]
+                    + run_in[plane, at]
+                    + weights[0] * added[plane]
+                    + weights[1] * gain
                 )
             for plane in nearby[side]:
                 along = outer_part(added, plane, owned[side])
                 gain = kappa_r * along
                 out_state[1, plane, at] = second_in[0, plane, at] + gain
                 out_layer[0, plane, at] = second_in[1, plane, at] + q0 * along
-                out_filtered[plane, at] = run_in[plane, at] + weights[1] * gain
+                out_filtered[plane, at] = running[plane, at] + run_in[plane, at] + weights[1] * gain
         for plane in range(2 * REACH, nx - 2 * REACH):
             out_state[1, plane, at] = second_in[0, plane, at]
             out_layer[0, plane, at] = second_in[1, plane, at]
-            out_filtered[plane, at] = run_in[plane, at]
+            out_filtered[plane, at] = running[plane, at] + run_in[plane, at]
 
     over_rows(ny, second)
 
@@ -545,7 +550,7 @@
 
 
 def finish_kernel(
-    coef, clock, inside, across, ghost, partial, state_in, layer_in, filtered_in,
+    coef, clock, inside, across, across_late, ghost, partial, state_in, layer_in, filtered_in,
     out_state, out_layer, out_filtered, total_out,
 ):
     _, nx, ny, _ = state_in.shape
@@ -560,7 +565,8 @@
         at = pl.ds(rows, BLK)
         halo = {}
         for number in range(REACH):
-            one, two = inside[number, at], across[number, at]
+            one = inside[number, at]
+            two = across[number, at] + across_late[number, at]
             halo[-REACH + number] = jnp.where(even, two, one) + ghost[number, at]
             halo[nx + number] = jnp.where(even, one, two) + ghost[REACH + number, at]
         total = total_out[...]
@@ -580,11 +586,20 @@
     over_rows(ny, step)
 
 
-def store_kernel(values, held_array, out, values_out, sem):
-    copy = pltpu.make_async_copy(held_array, out, sem)
-    copy.start()
+def store_kernel(parts, values, *refs):
+    n = len(parts)
+    arrays, outs, values_out, sems = refs[:n], refs[-n - 2 : -2], refs[-2], refs[-1]
+    copies = [
+        pltpu.make_async_copy(
+            *((array, out) if at is None else (array.at[at], out.at[at])), sems.at[number]
+        )
+        for number, (at, array, out) in enumerate(zip(parts, arrays, outs))
+    ]
+    for copy in copies:
+        copy.start()
     values_out[...] = values[...]
-    copy.wait()
+    for copy in copies:
+        copy.wait()
 
 
 SCALAR = pl.BlockSpec(memory_space=pltpu.SMEM)
@@ -628,37 +643,58 @@
     return inside, across
 
 
-def store(values, array):
-    return call(
-        store_kernel,
+def halves(pairs):
+    return [[pair for pair in pairs if min(pair) % 4 == first] for first in (1, 3)]
+
+
+def store(values, parts, arrays, begun=()):
+    n = len(arrays)
+    outs = [jax.ShapeDtypeStruct(array.shape, F32) for array in arrays]
+    *stored, values = call(
+        functools.partial(store_kernel, parts),
         "store",
-        [VEC] * 2,
-        [jax.ShapeDtypeStruct(array.shape, F32), held(*values.shape)],
-        [HBM, VEC],
-        [pltpu.SemaphoreType.DMA],
-        in_vmem(values, array),
+        [VEC] * (1 + n) + [HBM] * len(begun),
+        [*outs, held(*values.shape)],
+        [HBM] * n + [VEC],
+        [pltpu.SemaphoreType.DMA((n,))],
+        (*in_vmem(values, *arrays), *begun),
         1,
-    )
-
-
-def total_and_stores(values, arrays, axis):
+        {1 + n + number: n - len(begun) + number for number in range(len(begun))},
+    )
+    return values, stored
+
+
+def total_and_stores(values, state, layer, running, axis):
     count = lax.axis_size(axis)
-    stored = []
-    if count & (count - 1):
-        for array in arrays:
-            stored.append(store(values, array)[0])
-        return lax.psum(values, axis), stored
-    hop = 1
-    while hop < count:
+    half = layer.shape[0] // 2
+    stored = {}
+
+    def first(values):
+        values, (stored["state"],) = store(values, [None], [state])
+        return values
+
+    def second(values):
+        values, (stored["layer"],) = store(values, [pl.ds(0, half)], [layer])
+        return values
+
+    def third(values):
+        values, (stored["running"], stored["layer"]) = store(
+            values, [None, pl.ds(half, half)], [running, layer], [stored["layer"]]
+        )
+        return values
+
+    waiting = [first, second, third]
+    hops = [] if count & (count - 1) else [1 << k for k in range(count.bit_length() - 1)]
+    for number, hop in enumerate(hops):
         got = lax.ppermute(values, axis, [(i, i ^ hop) for i in range(count)])
-        if len(stored) < len(arrays):
-            done, values = store(values, arrays[len(stored)])
-            stored.append(done)
+        if waiting and number >= 1:
+            values = waiting.pop(0)(values)
         values = values + got
-        hop *= 2
-    for array in arrays[len(stored) :]:
-        stored.append(store(values, array)[0])
-    return values, stored
+    for step in waiting:
+        values = step(values)
+    if not hops:
+        values = lax.psum(values, axis)
+    return values, stored["state"], stored["layer"], stored["running"]
 
 
 def body(
@@ -678,25 +714,24 @@
     blocks = (speed_index.shape[1], n_block, speed_index.shape[2])
     index, mask = in_hbm(*(jnp.transpose(one, (1, 0, 2)) for one in (speed_index, pml_mask)))
 
-    inside, across, coef, clock, edge = call(
+    inside, across, coef, clock, edge, wave, layer, forcing = call(
         send_kernel,
         "strips",
         [HBM] * 3 + [SCALAR] * 2 + [HBM] * 3,
         [
             held(*message), held(*message), held(N_COEF, n_block, ny, nz),
-            held(2 * STEPS, BLK, nz), held(2, 5, *strip),
+            held(2 * STEPS, BLK, nz), held(2, 5, *strip), held(*wave_state.shape),
+            held(*layer_fields.shape), held(*brick),
         ],
-        [VEC] * 5,
+        [VEC] * 8,
         [
-            vec(*brick),
-            vec(2, 6, *strip),
             vec(2 * REACH, ny, nz),
             vec(2 * REACH, ny, nz),
             vec(2, n_block * TAG_ROWS, nz),
             pltpu.VMEM(blocks, jnp.int32),
             pltpu.VMEM(blocks, jnp.int32),
             pltpu.SMEM(speed_table.shape, F32),
-            dma((10,)),
+            dma((13,)),
         ],
         (
             *in_hbm(wave_state, layer_fields, source), frequency, start_time,
@@ -707,24 +742,27 @@
     got_inside = lax.ppermute(inside, "gx", pair_inside)
     got_across = lax.ppermute(across, "gx", pair_across)
     coef, clock, edge, wave, layer, forcing, running = in_vmem(
-        coef, clock, edge, wave_state, layer_fields, source, filtered
+        coef, clock, edge, wave, layer, forcing, filtered
     )
 
     later_inside, later_across, first, second, run = call(
         local_kernel,
         "local",
-        [VEC] * 7,
+        [VEC] * 6,
         [
             held(*strip), held(*strip), held(nx - 2 * REACH, ny, nz), held(5, *brick),
             held(*brick),
         ],
         [VEC] * 5,
         [vec(4, nx - 2 * REACH, ny, nz), vec(*brick), vec(*brick)],
-        (wave, layer, forcing, running, coef, clock, edge),
+        (wave, layer, forcing, coef, clock, edge),
         4,
     )
     last_inside = lax.ppermute(later_inside, "gx", pair_inside)
-    last_across = lax.ppermute(later_across, "gx", pair_across)
+    early_pairs, late_pairs = halves(pair_across)
+    last_across = lax.ppermute(later_across, "gx", early_pairs)
+    later_across, got_across = lax.optimization_barrier((later_across, got_across))
+    last_late = lax.ppermute(later_across, "gx", late_pairs)
 
     out_types = [
         held(*wave_state.shape), held(*layer_fields.shape), held(*filtered.shape)
@@ -732,7 +770,7 @@
     next_state, next_layer, next_filtered, ghost, partial = call(
         joint_kernel,
         "joint",
-        [VEC] * 10,
+        [VEC] * 11,
         out_types + [held(2 * REACH, ny, nz), held(BLK, nz)],
         [VEC] * 5,
         [
@@ -746,7 +784,7 @@
             vec(4 * REACH, ny, nz),
         ],
         (
-            coef, clock, *in_vmem(got_inside, got_across), wave, forcing, edge,
+            coef, clock, *in_vmem(got_inside, got_across), wave, forcing, running, edge,
             *in_vmem(first, second, run),
         ),
         5,
@@ -754,21 +792,22 @@
     next_state, next_layer, next_filtered, total = call(
         finish_kernel,
         "finish",
-        [VEC] * 9,
+        [VEC] * 10,
         out_types + [held(BLK, nz)],
         [VEC] * 4,
         [],
         (
             coef, clock,
             *in_vmem(
-                last_inside, last_across, ghost, partial, next_state, next_layer, next_filtered
+                last_inside, last_across, last_late, ghost, partial,
+                next_state, next_layer, next_filtered,
             ),
         ),
         1,
-        {6: 0, 7: 1, 8: 2},
-    )
-    total, (next_filtered, next_state, next_layer) = total_and_stores(
-        total, [next_filtered, next_state, next_layer], "gx"
+        {7: 0, 8: 1, 9: 2},
+    )
+    total, next_state, next_layer, next_filtered = total_and_stores(
+        total, next_state, next_layer, next_filtered, "gx"
     )
     total = jnp.sum(total)
     filter_norm = jnp.sqrt(total / (filtered.size * count) + 1e-06)

time: 42.6 us -> 40.6 us (0.953)
  starting transfers between devices: 19.9 us -> 18.7 us
  local copies, waits for them, and re-layouts: 1.14 us -> 0.01 us
    ppermute x1, starting transfers between devices: 0.52 us -> 4.37 us  [body(): got_inside = lax.ppermute(inside, 'gx', pair_inside)]
    ppermute x1, starting transfers between devices: 3.94 us -> 0.09 us  [body(): last_inside = lax.ppermute(later_inside, 'gx', pair_inside)]
    ppermute x4, starting transfers between devices: 14.1 us -> 12.2 us  [total_and_stores(): got = lax.ppermute(values, axis, [(i, i ^ hop) for i in range(count)])]
    unnamed x8 -> x2, local copies, waits for them, and re-layouts: 1.14 us -> 0.01 us
    ppermute x1 -> x2, starting transfers between devices: 0.66 us -> 1.33 us  [the longest x1 0.67 us: body(): last_late = lax.ppermute(later_across, 'gx', late_pairs)]
  transfers between devices with their start and end apart: 8 -> 9, of which waited for: 2 -> 4; matrix products, arithmetic and copies ran while one was open for 0% -> 0% of each run, Pallas kernels for 26% -> 28%
where the time goes in v3:
time: 40.6 us; the launch traced here: 40.3 us
  starting transfers between devices  18.7 us (46%)
  Pallas kernels  14.6 us (36%)
  between operations  3.87 us (10%)
  waiting for transfers between devices  2.5 us (6%)
  other arithmetic  0.61 us (2%)
    pallas_call x7, Pallas kernels, call(): pl.pallas_call(kernel, name=name, in_specs=in_specs, out_shape=out_shape,...  14.6 us
    ppermute x4, starting transfers between devices, total_and_stores(): got = lax.ppermute(values, axis, [(i, i ^ hop) for i in range(count)])  12.2 us
    ppermute x1, starting transfers between devices, body(): got_inside = lax.ppermute(inside, 'gx', pair_inside)  4.37 us
    ppermute x4, waiting for transfers between devices, total_and_stores(): got = lax.ppermute(values, axis, [(i, i ^ hop) for i in range(count)])  2.49 us
  transfers between devices with their start and end apart: 9, of which 4 were waited for; matrix products, arithmetic and copies ran while one was open for 0% of the time, Pallas kernels for 28%

profile of v3, /device:TPU:0, one launch (start us, length us, event | category | flops | bytes accessed | tf_op | source)
XLA Modules:
  0.0 40.3 jit_solution(17204227153904836835)
XLA Ops:
  1.9 2.8 %strips.1 = (f32[800,128]{1,0:T(8,128)S(1)}, f32[800,128]{1,0:T(8,128)S(1)}, f32[14,2,96,128]{3,2,1,0:T(8,128)S(1)}, f32[6,8,128]{2,1,0:T(8,128)S(1)}, f32[2,5,4...) custom-call(f32[2,16,96,128]{3,2,1,0:T(8,128)} %wave_in.1, ...), custom_call_target="tpu_custom_call" | custom-call | bytes 9000000 | tf_op jit(solution)/shard_map/strips/pallas_call | solution.py:623
  4.7 0.7 %collective-permute-start.2 = (f32[800,128]{1,0:T(8,128)S(1)}, f32[800,128]{1,0:T(8,128)S(1)}, u32[]{:S(2)}, u32[]{:S(2)}) collective-permute-start(f32[800,128]{1,0:T(8,128)S(1)} %get-tuple-element.43), channel_id=1, source_target_pairs={{1,2},{2,1},{3,4},{4,3},{5,6},{6,5},{7,8},{8,7},{9,10},{10,9},{11,... | collective-permute-start | bytes 1228808 | tf_op jit(solution)/shard_map/ppermute | solution.py:743
  5.4 4.4 %collective-permute-start.4 = (f32[800,128]{1,0:T(8,128)S(1)}, f32[800,128]{1,0:T(8,128)S(1)}, u32[]{:S(2)}, u32[]{:S(2)}) collective-permute-start(f32[800,128]{1,0:T(8,128)S(1)} %get-tuple-element.45), channel_id=1, source_target_pairs={{0,1},{1,0},{2,3},{3,2},{4,5},{5,4},{6,7},{7,6},{8,9},{9,8},{10,11... | collective-permute-start | bytes 1228808 | tf_op jit(solution)/shard_map/ppermute | solution.py:742
  9.8 3.2 %local.1 = (f32[4,96,128]{2,1,0:T(8,128)S(1)}, f32[4,96,128]{2,1,0:T(8,128)S(1)}, f32[8,96,128]{2,1,0:T(8,128)S(1)}, f32[5,16,96,128]{3,2,1,0:T(8,128)S(1)}, f32[16,96,128]{2,1,0:T(8,128)S(1)}) custom-call(f32[2,16,96,128]{3,2,1,0:T(8,128)S(1)} %get-tuple-element.37.wave, f32[4,16,96,128]{3,2,1,0:T(8,128)S(1)} %get-tuple-element.38.layer, ...), custom_call_target="tpu_custom_call" | custom-call | bytes 14400000 | tf_op jit(solution)/shard_map/local/pallas_call | solution.py:623
  13.0 0.1 collective-permute-start
  13.1 0.7 %collective-permute-start.1 = (f32[4,96,128]{2,1,0:T(8,128)S(1)}, f32[4,96,128]{2,1,0:T(8,128)S(1)}, u32[]{:S(2)}, u32[]{:S(2)}) collective-permute-start(f32[4,96,128]{2,1,0:T(8,128)S(1)} %get-tuple-element.44), channel_id=1, source_target_pairs={{1,2},{2,1},{5,6},{6,5},{9,10},{10,9},{13,14},{14,13},{17,18},{18,... | collective-permute-start | bytes 589832 | tf_op jit(solution)/shard_map/ppermute | solution.py:763
  13.8 0.0 collective-permute-done.2.across
  13.8 0.7 %collective-permute-start.3 = (f32[4,96,128]{2,1,0:T(8,128)S(1)}, f32[4,96,128]{2,1,0:T(8,128)S(1)}, u32[]{:S(2)}, u32[]{:S(2)}) collective-permute-start(f32[4,96,128]{2,1,0:T(8,128)S(1)} %get-tuple-element.44), channel_id=1, source_target_pairs={{3,4},{4,3},{7,8},{8,7},{11,12},{12,11},{19,20},{20,19},{23,24},{2... | collective-permute-start | bytes 589832 | tf_op jit(solution)/shard_map/ppermute | solution.py:765
  14.5 0.0 collective-permute-done.4.inside
  14.5 4.3 %joint.1 = (f32[2,16,96,128]{3,2,1,0:T(8,128)S(1)}, f32[4,16,96,128]{3,2,1,0:T(8,128)S(1)}, f32[16,96,128]{2,1,0:T(8,128)S(1)}, f32[8,96,128]{2,1,0:T(8,128)S(1)}, f32[8,128]{1,0:T(8,128)S(1)}) custom-call(f32[14,2,96,128]{3,2,1,0:T(8,128)S(1)} %get-tuple-element.35.coef, f32[6,8,128]{2,1,0:T(8,128)S(1)} %get-tuple-element.36.clock, ...), custom_call_target="tpu_custom_call" | custom-call | bytes 18000000 | tf_op jit(solution)/shard_map/joint/pallas_call | solution.py:623
  18.8 0.0 collective-permute-done.inside
  18.8 0.6 %finish.1 = (f32[2,16,96,128]{3,2,1,0:T(8,128)S(1)}, f32[4,16,96,128]{3,2,1,0:T(8,128)S(1)}, f32[16,96,128]{2,1,0:T(8,128)S(1)}, f32[8,128]{1,0:T(8,128)S(1)}) custom-call(f32[14,2,96,128]{3,2,1,0:T(8,128)S(1)} %get-tuple-element.35.coef, f32[6,8,128]{2,1,0:T(8,128)S(1)} %get-tuple-element.36.clock, ...), custom_call_target="tpu_custom_call", output_to_operand_aliasing={{0}: (7, {}), {1}: (8, {}), {2}: (9, {})} | custom-call | bytes 3600000 | tf_op jit(solution)/shard_map/finish/pallas_call | solution.py:623
  19.4 5.2 %collective-permute-start.5 = (f32[8,128]{1,0:T(8,128)S(1)}, f32[8,128]{1,0:T(8,128)S(1)}, u32[]{:S(2)}, u32[]{:S(2)}) collective-permute-start(f32[8,128]{1,0:T(8,128)S(1)} %get-tuple-element.55), channel_id=1, source_target_pairs={{0,1},{1,0},{2,3},{3,2},{4,5},{5,4},{6,7},{7,6},{8,9},{9,8},{10,11... | collective-permute-start | bytes 12296 | tf_op jit(solution)/shard_map/ppermute | solution.py:689
  24.7 0.8 %collective-permute-done.5 = f32[8,128]{1,0:T(8,128)S(1)} collective-permute-done((f32[8,128]{1,0:T(8,128)S(1)}, f32[8,128]{1,0:T(8,128)S(1)}, u32[]{:S(2)}, u32[]{:S(2)}) %collective-permute-start.5) | collective-permute-done | bytes 4128 | tf_op jit(solution)/shard_map/ppermute | solution.py:689
  25.5 2.7 %collective-permute-start.6 = (f32[8,128]{1,0:T(8,128)S(1)}, f32[8,128]{1,0:T(8,128)S(1)}, u32[]{:S(2)}, u32[]{:S(2)}) collective-permute-start(f32[8,128]{1,0:T(8,128)S(1)} %add.15.values), channel_id=1, source_target_pairs={{0,2},{1,3},{2,0},{3,1},{4,6},{5,7},{6,4},{7,5},{8,10},{9,11},{10,... | collective-permute-start | bytes 12296 | tf_op jit(solution)/shard_map/ppermute | solution.py:689
  28.2 1.1 %store.3 = (f32[2,16,96,128]{3,2,1,0:T(8,128)}, f32[8,128]{1,0:T(8,128)S(1)}) custom-call(f32[8,128]{1,0:T(8,128)S(1)} %add.15.values, f32[2,16,96,128]{3,2,1,0:T(8,128)S(1)} %get-tuple-element.56.refs_0_), custom_call_target="tpu_custom_call" | custom-call | bytes 3600000 | tf_op jit(solution)/shard_map/store/pallas_call | solution.py:623
  29.4 0.4 %collective-permute-done.6 = f32[8,128]{1,0:T(8,128)S(1)} collective-permute-done((f32[8,128]{1,0:T(8,128)S(1)}, f32[8,128]{1,0:T(8,128)S(1)}, u32[]{:S(2)}, u32[]{:S(2)}) %collective-permute-start.6) | collective-permute-done | bytes 4128 | tf_op jit(solution)/shard_map/ppermute | solution.py:689
  29.8 1.6 %collective-permute-start.7 = (f32[8,128]{1,0:T(8,128)S(1)}, f32[8,128]{1,0:T(8,128)S(1)}, u32[]{:S(2)}, u32[]{:S(2)}) collective-permute-start(f32[8,128]{1,0:T(8,128)S(1)} %add.16.values), channel_id=1, source_target_pairs={{0,4},{1,5},{2,6},{3,7},{4,0},{5,1},{6,2},{7,3},{8,12},{9,13},{10,... | collective-permute-start | bytes 12296 | tf_op jit(solution)/shard_map/ppermute | solution.py:689
  31.4 1.1 %store.4 = (f32[4,16,96,128]{3,2,1,0:T(8,128)}, f32[8,128]{1,0:T(8,128)S(1)}) custom-call(f32[8,128]{1,0:T(8,128)S(1)} %add.16.values, f32[4,16,96,128]{3,2,1,0:T(8,128)S(1)} %get-tuple-element.59.refs_0_.refs_1_), custom_call_target="tpu_custom_call" | custom-call | bytes 3600000 | tf_op jit(solution)/shard_map/store/pallas_call | solution.py:623
  32.6 0.8 %collective-permute-done.7 = f32[8,128]{1,0:T(8,128)S(1)} collective-permute-done((f32[8,128]{1,0:T(8,128)S(1)}, f32[8,128]{1,0:T(8,128)S(1)}, u32[]{:S(2)}, u32[]{:S(2)}) %collective-permute-start.7) | collective-permute-done | bytes 4128 | tf_op jit(solution)/shard_map/ppermute | solution.py:689
  33.4 2.6 %collective-permute-start.8 = (f32[8,128]{1,0:T(8,128)S(1)}, f32[8,128]{1,0:T(8,128)S(1)}, u32[]{:S(2)}, u32[]{:S(2)}) collective-permute-start(f32[8,128]{1,0:T(8,128)S(1)} %add.17.values), channel_id=1, source_target_pairs={{0,8},{1,9},{2,10},{3,11},{4,12},{5,13},{6,14},{7,15},{8,0},{9,1},... | collective-permute-start | bytes 12296 | tf_op jit(solution)/shard_map/ppermute | solution.py:689
  36.1 1.4 %store.5 = (f32[16,96,128]{2,1,0:T(8,128)}, f32[4,16,96,128]{3,2,1,0:T(8,128)}, f32[8,128]{1,0:T(8,128)S(1)}) custom-call(f32[8,128]{1,0:T(8,128)S(1)} %add.17.values, f32[16,96,128]{2,1,0:T(8,128)S(1)} %get-tuple-element.61.refs_0_, f32[4,16,96,128]{3,2,1,0:T(8,128)S(1)} %get-tuple-element.59.refs_0_.refs_1_, ...), custom_call_target="tpu_custom_call", output_to_operand_aliasing={{1}: (3, {})} | custom-call | bytes 3600000 | tf_op jit(solution)/shard_map/store/pallas_call | solution.py:623
  37.5 0.4 %collective-permute-done.8 = f32[8,128]{1,0:T(8,128)S(1)} collective-permute-done((f32[8,128]{1,0:T(8,128)S(1)}, f32[8,128]{1,0:T(8,128)S(1)}, u32[]{:S(2)}, u32[]{:S(2)}) %collective-permute-start.8) | collective-permute-done | bytes 4128 | tf_op jit(solution)/shard_map/ppermute | solution.py:689
  37.9 0.6 %add_reduce_fusion = f32[]{:T(128)} fusion(f32[8,128]{1,0:T(8,128)S(1)} %get-tuple-element.65, f32[8,128]{1,0:T(8,128)S(1)} %collective-permute-done.8), kind=kLoop, calls=%fused_computation | loop fusion | flops 2047 | bytes 8196 | tf_op jit(solution)/shard_map/reduce_sum | solution.py:812
  (7 shorter events, 0.0 us)
Async XLA Ops:
  4.7 9.1 %collective-permute-start.2 = (f32[800,128]{1,0:T(8,128)S(1)}, f32[800,128]{1,0:T(8,128)S(1)}, u32[]{:S(2)}, u32[]{:S(2)}) collective-permute-start(f32[800,128]{1,0:T(8,128)S(1)} %get-tuple-element.43), channel_id=1, source_target_pairs={{1,2},{2,1},{3,4},{4,3},{5,6},{6,5},{7,8},{8,7},{9,10},{10,9},{11,... | collective-permute-start | bytes 1228808 | tf_op jit(solution)/shard_map/ppermute | solution.py:743
  5.4 9.1 %collective-permute-start.4 = (f32[800,128]{1,0:T(8,128)S(1)}, f32[800,128]{1,0:T(8,128)S(1)}, u32[]{:S(2)}, u32[]{:S(2)}) collective-permute-start(f32[800,128]{1,0:T(8,128)S(1)} %get-tuple-element.45), channel_id=1, source_target_pairs={{0,1},{1,0},{2,3},{3,2},{4,5},{5,4},{6,7},{7,6},{8,9},{9,8},{10,11... | collective-permute-start | bytes 1228808 | tf_op jit(solution)/shard_map/ppermute | solution.py:742
  9.8 4.7 %copy-start = (f32[16,96,128]{2,1,0:T(8,128)S(1)}, f32[16,96,128]{2,1,0:T(8,128)}, u32[]{:S(2)}) copy-start(f32[16,96,128]{2,1,0:T(8,128)} %running.1) | copy-start | bytes 2359300
  13.0 5.8 %collective-permute-start = (f32[4,96,128]{2,1,0:T(8,128)S(1)}, f32[4,96,128]{2,1,0:T(8,128)S(1)}, u32[]{:S(2)}, u32[]{:S(2)}) collective-permute-start(f32[4,96,128]{2,1,0:T(8,128)S(1)} %get-tuple-element.41), channel_id=1, source_target_pairs={{0,1},{1,0},{2,3},{3,2},{4,5},{5,4},{6,7},{7,6},{8,9},{9,8},{10,11... | collective-permute-start | bytes 589832 | tf_op jit(solution)/shard_map/ppermute | solution.py:761
  13.1 5.7 %collective-permute-start.1 = (f32[4,96,128]{2,1,0:T(8,128)S(1)}, f32[4,96,128]{2,1,0:T(8,128)S(1)}, u32[]{:S(2)}, u32[]{:S(2)}) collective-permute-start(f32[4,96,128]{2,1,0:T(8,128)S(1)} %get-tuple-element.44), channel_id=1, source_target_pairs={{1,2},{2,1},{5,6},{6,5},{9,10},{10,9},{13,14},{14,13},{17,18},{18,... | collective-permute-start | bytes 589832 | tf_op jit(solution)/shard_map/ppermute | solution.py:763
  13.8 5.0 %collective-permute-start.3 = (f32[4,96,128]{2,1,0:T(8,128)S(1)}, f32[4,96,128]{2,1,0:T(8,128)S(1)}, u32[]{:S(2)}, u32[]{:S(2)}) collective-permute-start(f32[4,96,128]{2,1,0:T(8,128)S(1)} %get-tuple-element.44), channel_id=1, source_target_pairs={{3,4},{4,3},{7,8},{8,7},{11,12},{12,11},{19,20},{20,19},{23,24},{2... | collective-permute-start | bytes 589832 | tf_op jit(solution)/shard_map/ppermute | solution.py:765
  19.4 6.1 %collective-permute-start.5 = (f32[8,128]{1,0:T(8,128)S(1)}, f32[8,128]{1,0:T(8,128)S(1)}, u32[]{:S(2)}, u32[]{:S(2)}) collective-permute-start(f32[8,128]{1,0:T(8,128)S(1)} %get-tuple-element.55), channel_id=1, source_target_pairs={{0,1},{1,0},{2,3},{3,2},{4,5},{5,4},{6,7},{7,6},{8,9},{9,8},{10,11... | collective-permute-start | bytes 12296 | tf_op jit(solution)/shard_map/ppermute | solution.py:689
  25.5 4.3 %collective-permute-start.6 = (f32[8,128]{1,0:T(8,128)S(1)}, f32[8,128]{1,0:T(8,128)S(1)}, u32[]{:S(2)}, u32[]{:S(2)}) collective-permute-start(f32[8,128]{1,0:T(8,128)S(1)} %add.15.values), channel_id=1, source_target_pairs={{0,2},{1,3},{2,0},{3,1},{4,6},{5,7},{6,4},{7,5},{8,10},{9,11},{10,... | collective-permute-start | bytes 12296 | tf_op jit(solution)/shard_map/ppermute | solution.py:689
  29.8 3.6 %collective-permute-start.7 = (f32[8,128]{1,0:T(8,128)S(1)}, f32[8,128]{1,0:T(8,128)S(1)}, u32[]{:S(2)}, u32[]{:S(2)}) collective-permute-start(f32[8,128]{1,0:T(8,128)S(1)} %add.16.values), channel_id=1, source_target_pairs={{0,4},{1,5},{2,6},{3,7},{4,0},{5,1},{6,2},{7,3},{8,12},{9,13},{10,... | collective-permute-start | bytes 12296 | tf_op jit(solution)/shard_map/ppermute | solution.py:689
  33.4 4.5 %collective-permute-start.8 = (f32[8,128]{1,0:T(8,128)S(1)}, f32[8,128]{1,0:T(8,128)S(1)}, u32[]{:S(2)}, u32[]{:S(2)}) collective-permute-start(f32[8,128]{1,0:T(8,128)S(1)} %add.17.values), channel_id=1, source_target_pairs={{0,8},{1,9},{2,10},{3,11},{4,12},{5,13},{6,14},{7,15},{8,0},{9,1},... | collective-permute-start | bytes 12296 | tf_op jit(solution)/shard_map/ppermute | solution.py:689

commit v4 on v3

--- a/solution.py
+++ b/solution.py
@@ -357,152 +357,176 @@
     over_rows(ny, second)
 
 
+def side_update(
+    left, present, message, coef, clock, wave, running, edge, second_in, run_in,
+    out_state, out_layer, out_filtered, ext, ghost,
+    first, bump, push, ghost_coef, bump_y, bump_z,
+):
+    _, nx, ny, nz = wave.shape
+    n_block = nx // BLK
+    block = jnp.where(left, 0, n_block - 1)
+    side = jnp.where(left, 0, 1)
+    own = range(REACH)
+    beyond = range(-1, -1 - REACH, -1)
+    weights = [clock[STEPS + number] for number in range(2)]
+
+    def plane_of(depth):
+        return jnp.where(left, depth, nx - 1 - depth)
+
+    def slot(depth):
+        return depth if depth >= 0 else REACH - 1 - depth
+
+    tag_at = 2 * REACH * ny
+    square = message[pl.ds(tag_at, TAG_ROWS)] * present
+    values = coefficients(square, bits_of(message[pl.ds(tag_at + TAG_ROWS, TAG_ROWS)]))
+    for entry, value in enumerate(
+        (
+            values[KAPPA_R],
+            values[Q0],
+            values[KAPPA] * (1.0 - values[Q1]),
+            values[KAPPA] * (1.0 - values[Q2]),
+            values[AMP] - values[STIFF] * values[PAIR],
+        )
+    ):
+        down_second(ghost_coef, (entry,), value, ny)
+
+    def exchange(rows):
+        at = pl.ds(rows, BLK)
+        halo = {}
+        sent = {}
+        for depth in beyond:
+            number = jnp.where(left, REACH + depth, -1 - depth)
+            halo[depth] = message[pl.ds(pl.multiple_of(number * ny + rows, BLK), BLK)]
+            number = number + REACH
+            sent[depth] = message[pl.ds(pl.multiple_of(number * ny + rows, BLK), BLK)]
+        mine = {depth: wave[0, plane_of(depth), at] for depth in own}
+        kappa_r = coef[KAPPA_R, block, at]
+        for depth in own:
+            outer = outer_part(halo, depth, beyond)
+            added = kappa_r * outer
+            push[slot(depth), at] = outer
+            bump[slot(depth), at] = added
+            value = edge[side, 0, jnp.where(left, depth, REACH - 1 - depth), at] + added
+            first[slot(depth), at] = value
+            ext[jnp.where(left, depth, 2 * REACH - 1 - depth), at] = value
+        kappa_r = ghost_coef[0, at]
+        for depth in beyond:
+            outer = outer_part(mine, depth, own)
+            added = kappa_r * outer
+            push[slot(depth), at] = outer
+            bump[slot(depth), at] = added
+            first[slot(depth), at] = sent[depth] + added
+
+    over_rows(ny, exchange)
+
+    def put_bump_y(plane, value):
+        bump_y[plane] = value
+
+    def put_bump_z(plane, value):
+        bump_z[plane] = value
+
+    cross_diffs(range(2 * REACH), lambda plane: bump[plane], put_bump_y, put_bump_z, ny, nz)
+
+    def respond(added, true, depth, others, outer, q0, kappas, at):
+        kappa_r, kappa_1, kappa_2, grown = kappas
+        value = added[depth]
+        rest = CENTRE_REST * value
+        along = first_diff(added, depth) + outer_part(true, depth, others)
+        side_y = bump_y[slot(depth), at] * (1.0 / SCALE) - rest
+        side_z = bump_z[slot(depth), at] * (1.0 / SCALE) - rest
+        gain = (
+            grown * value + kappa_r * (along - q0 * outer) + kappa_1 * side_y + kappa_2 * side_z
+        )
+        return gain, along, side_y, side_z
+
+    def second(rows):
+        at = pl.ds(rows, BLK)
+        true = {depth: first[slot(depth), at] for depth in (*own, *beyond)}
+        added = {depth: bump[slot(depth), at] for depth in beyond}
+        kappa_r, q0, kappa_1, kappa_2, grown = [ghost_coef[entry, at] for entry in range(5)]
+        for depth in beyond:
+            ghost[-1 - depth, at], _, _, _ = respond(
+                added, true, depth, own, push[slot(depth), at], q0,
+                (kappa_r, kappa_1, kappa_2, grown), at,
+            )
+        added = {depth: bump[slot(depth), at] for depth in own}
+        kappa_r, kappa = coef[KAPPA_R, block, at], coef[KAPPA, block, at]
+        q0, q1, q2 = [coef[entry, block, at] for entry in (Q0, Q1, Q2)]
+        pair = coef[PAIR, block, at]
+        kappas = (
+            kappa_r,
+            kappa * (1.0 - q1),
+            kappa * (1.0 - q2),
+            coef[AMP, block, at] - coef[STIFF, block, at] * pair,
+        )
+        for depth in own:
+            plane = plane_of(depth)
+            outer = push[slot(depth), at]
+            gain, along, side_y, side_z = respond(
+                added, true, depth, beyond, outer, q0, kappas, at
+            )
+            out_state[1, plane, at] = second_in[0, plane, at] + gain
+            out_layer[0, plane, at] = second_in[1, plane, at] + q0 * (
+                along + (1.0 - q0) * outer
+            )
+            out_layer[1, plane, at] = second_in[2, plane, at] + q1 * side_y
+            out_layer[2, plane, at] = second_in[3, plane, at] + q2 * side_z
+            out_layer[3, plane, at] = second_in[4, plane, at] + pair * added[depth]
+            out_filtered[plane, at] = (
+                running[plane, at]
+                + run_in[plane, at]
+                + weights[0] * added[depth]
+                + weights[1] * gain
+            )
+        for depth in range(REACH, 2 * REACH):
+            plane = plane_of(depth)
+            along = outer_part(added, depth, own)
+            gain = kappa_r * along
+            out_state[1, plane, at] = second_in[0, plane, at] + gain
+            out_layer[0, plane, at] = second_in[1, plane, at] + q0 * along
+            out_filtered[plane, at] = running[plane, at] + run_in[plane, at] + weights[1] * gain
+
+    over_rows(ny, second)
+
+
+def inside_kernel(
+    inside, coef, clock, wave, running, edge, second_in, run_in,
+    out_state, out_layer, out_filtered, ext, ghost,
+    *scratch,
+):
+    side_update(
+        jnp.logical_not(is_even()), 1.0, inside, coef, clock, wave, running, edge, second_in,
+        run_in, out_state, out_layer, out_filtered, ext, ghost, *scratch,
+    )
+
+
 def joint_kernel(
-    coef, clock, inside, across, wave, forcing, running, edge, first_in, second_in, run_in,
-    out_state, out_layer, out_filtered, ghost, partial,
-    ext, bump, push, ghost_coef, diff_y, diff_z, bump_y, bump_z,
+    across, coef, clock, wave, forcing, running, edge, first_in, second_in, run_in,
+    state_in, layer_in, filtered_in, ext_in,
+    out_state, out_layer, out_filtered, ext, ghost, partial,
+    diff_y, diff_z, *scratch,
 ):
+    del state_in, layer_in, filtered_in, ext_in
     _, nx, ny, nz = wave.shape
     count = lax.axis_size("gx")
     place = lax.axis_index("gx")
     even = is_even()
-    n_block = nx // BLK
-    present = (
-        jnp.where(place > 0, 1.0, 0.0).astype(F32),
-        jnp.where(place < count - 1, 1.0, 0.0).astype(F32),
-    )
     weights = [clock[STEPS + number] for number in range(STEPS)]
-    ghosts = (range(-REACH, 0), range(nx, nx + REACH))
-    owned = (range(REACH), range(nx - REACH, nx))
-    nearby = (range(REACH, 2 * REACH), range(nx - 2 * REACH, nx - REACH))
-
-    def slot(position):
-        return position + REACH if position < nx // 2 else position - nx + 3 * REACH
-
-    def received(to):
-        one, two = inside[to], across[to]
-        return jnp.where(even, two, one), jnp.where(even, one, two)
-
-    tag_at = 2 * REACH * ny
-    tiles = [received(pl.ds(tag_at + part * TAG_ROWS, TAG_ROWS)) for part in range(2)]
-    for side in range(2):
-        values = coefficients(tiles[0][side] * present[side], bits_of(tiles[1][side]))
-        for entry, value in enumerate(
-            (
-                values[KAPPA_R],
-                values[Q0],
-                values[KAPPA] * (1.0 - values[Q1]),
-                values[KAPPA] * (1.0 - values[Q2]),
-                values[AMP] - values[STIFF] * values[PAIR],
-            )
-        ):
-            down_second(ghost_coef, (side, entry), value, ny)
-
-    def exchange(rows):
-        at = pl.ds(rows, BLK)
-        halo = {}
-        sent = {}
-        for number in range(REACH):
-            to = pl.ds(pl.multiple_of(number * ny + rows, BLK), BLK)
-            halo[-REACH + number], halo[nx + number] = received(to)
-            to = pl.ds(pl.multiple_of((REACH + number) * ny + rows, BLK), BLK)
-            sent[-REACH + number], sent[nx + number] = received(to)
-        for side in range(2):
-            mine = {plane: wave[0, plane, at] for plane in owned[side]}
-            kappa_r = coef[KAPPA_R, side * (n_block - 1), at]
-            for number, plane in enumerate(owned[side]):
-                outer = outer_part(halo, plane, ghosts[side])
-                added = kappa_r * outer
-                push[slot(plane), at] = outer
-                bump[slot(plane), at] = added
-                ext[slot(plane), at] = edge[side, 0, number, at] + added
-            kappa_r = ghost_coef[side, 0, at]
-            for position in ghosts[side]:
-                outer = outer_part(mine, position, owned[side])
-                added = kappa_r * outer
-                push[slot(position), at] = outer
-                bump[slot(position), at] = added
-                ext[slot(position), at] = sent[position] + added
-
-    over_rows(ny, exchange)
-
-    def put_bump_y(plane, value):
-        bump_y[plane] = value
-
-    def put_bump_z(plane, value):
-        bump_z[plane] = value
-
-    cross_diffs(range(4 * REACH), lambda plane: bump[plane], put_bump_y, put_bump_z, ny, nz)
-
-    def respond(added, first, position, others, outer, q0, kappas, at):
-        kappa_r, kappa_1, kappa_2, grown = kappas
-        value = added[position]
-        rest = CENTRE_REST * value
-        along = first_diff(added, position) + outer_part(first, position, others)
-        side_y = bump_y[slot(position), at] * (1.0 / SCALE) - rest
-        side_z = bump_z[slot(position), at] * (1.0 / SCALE) - rest
-        gain = (
-            grown * value + kappa_r * (along - q0 * outer) + kappa_1 * side_y + kappa_2 * side_z
-        )
-        return gain, along, side_y, side_z
-
-    def second(rows):
-        at = pl.ds(rows, BLK)
-        for side in range(2):
-            block = side * (n_block - 1)
-            first = {
-                position: ext[slot(position), at] for position in (*ghosts[side], *owned[side])
-            }
-            added = {position: bump[slot(position), at] for position in ghosts[side]}
-            kappa_r, q0, kappa_1, kappa_2, grown = [
-                ghost_coef[side, entry, at] for entry in range(5)
-            ]
-            for number, position in enumerate(ghosts[side]):
-                outer = push[slot(position), at]
-                ghost[side * REACH + number, at], _, _, _ = respond(
-                    added, first, position, owned[side], outer, q0,
-                    (kappa_r, kappa_1, kappa_2, grown), at,
-                )
-            added = {position: bump[slot(position), at] for position in owned[side]}
-            kappa_r, kappa = coef[KAPPA_R, block, at], coef[KAPPA, block, at]
-            q0, q1, q2 = [coef[entry, block, at] for entry in (Q0, Q1, Q2)]
-            pair = coef[PAIR, block, at]
-            kappas = (
-                kappa_r,
-                kappa * (1.0 - q1),
-                kappa * (1.0 - q2),
-                coef[AMP, block, at] - coef[STIFF, block, at] * pair,
-            )
-            for plane in owned[side]:
-                outer = push[slot(plane), at]
-                gain, along, side_y, side_z = respond(
-                    added, first, plane, ghosts[side], outer, q0, kappas, at
-                )
-                out_state[1, plane, at] = second_in[0, plane, at] + gain
-                out_layer[0, plane, at] = second_in[1, plane, at] + q0 * (
-                    along + (1.0 - q0) * outer
-                )
-                out_layer[1, plane, at] = second_in[2, plane, at] + q1 * side_y
-                out_layer[2, plane, at] = second_in[3, plane, at] + q2 * side_z
-                out_layer[3, plane, at] = second_in[4, plane, at] + pair * added[plane]
-                out_filtered[plane, at] = (
-                    running[plane, at]
-                    + run_in[plane, at]
-                    + weights[0] * added[plane]
-                    + weights[1] * gain
-                )
-            for plane in nearby[side]:
-                along = outer_part(added, plane, owned[side])
-                gain = kappa_r * along
-                out_state[1, plane, at] = second_in[0, plane, at] + gain
-                out_layer[0, plane, at] = second_in[1, plane, at] + q0 * along
-                out_filtered[plane, at] = running[plane, at] + run_in[plane, at] + weights[1] * gain
-        for plane in range(2 * REACH, nx - 2 * REACH):
-            out_state[1, plane, at] = second_in[0, plane, at]
-            out_layer[0, plane, at] = second_in[1, plane, at]
-            out_filtered[plane, at] = running[plane, at] + run_in[plane, at]
-
-    over_rows(ny, second)
+    outermost = jnp.logical_or(place == 0, place == count - 1)
+    side_update(
+        even, jnp.where(outermost, 0.0, 1.0).astype(F32), across, coef, clock, wave, running,
+        edge, second_in, run_in, out_state, out_layer, out_filtered, ext, ghost, *scratch,
+    )
+    if nx > 4 * REACH:
+
+        def between(rows):
+            at = pl.ds(rows, BLK)
+            for plane in range(2 * REACH, nx - 2 * REACH):
+                out_state[1, plane, at] = second_in[0, plane, at]
+                out_layer[0, plane, at] = second_in[1, plane, at]
+                out_filtered[plane, at] = running[plane, at] + run_in[plane, at]
+
+        over_rows(ny, between)
 
     def put_y(plane, value):
         diff_y[plane] = value
@@ -520,7 +544,7 @@
         for plane in range(nx):
             at_edge = plane < REACH or plane >= nx - REACH
             if at_edge:
-                previous = ext[slot(plane), at]
+                previous = ext[plane if plane < REACH else plane - nx + 2 * REACH, at]
                 fields = [out_layer[d, plane, at] for d in range(4)]
             else:
                 previous = first_in[plane - REACH, at]
@@ -550,7 +574,8 @@
 
 
 def finish_kernel(
-    coef, clock, inside, across, across_late, ghost, partial, state_in, layer_in, filtered_in,
+    coef, clock, inside, across, across_late, ghost_inside, ghost_across, partial,
+    state_in, layer_in, filtered_in,
     out_state, out_layer, out_filtered, total_out,
 ):
     _, nx, ny, _ = state_in.shape
@@ -567,8 +592,12 @@
         for number in range(REACH):
             one = inside[number, at]
             two = across[number, at] + across_late[number, at]
-            halo[-REACH + number] = jnp.where(even, two, one) + ghost[number, at]
-            halo[nx + number] = jnp.where(even, one, two) + ghost[REACH + number, at]
+            left = jnp.where(even, two, one)
+            right = jnp.where(even, one, two)
+            one, two = ghost_inside[REACH - 1 - number, at], ghost_across[REACH - 1 - number, at]
+            halo[-REACH + number] = left + jnp.where(even, two, one)
+            one, two = ghost_inside[number, at], ghost_across[number, at]
+            halo[nx + number] = right + jnp.where(even, one, two)
         total = total_out[...]
         for side in range(2):
             block = side * (n_block - 1)
@@ -602,6 +631,12 @@
         copy.wait()
 
 
+def norm_kernel(cells, values, got, norm):
+    total = jnp.sum(values[...] + got[...], axis=1, keepdims=True)
+    total = jnp.sum(total, axis=0, keepdims=True)
+    norm[...] = jnp.sqrt(total / cells + 1e-06)
+
+
 SCALAR = pl.BlockSpec(memory_space=pltpu.SMEM)
 HBM = pl.BlockSpec(memory_space=pltpu.HBM)
 VEC = pl.BlockSpec(memory_space=pltpu.VMEM)
@@ -664,7 +699,7 @@
     return values, stored
 
 
-def total_and_stores(values, state, layer, running, axis):
+def norm_and_stores(values, state, layer, running, axis):
     count = lax.axis_size(axis)
     half = layer.shape[0] // 2
     stored = {}
@@ -689,12 +724,23 @@
         got = lax.ppermute(values, axis, [(i, i ^ hop) for i in range(count)])
         if waiting and number >= 1:
             values = waiting.pop(0)(values)
-        values = values + got
+        if hop != hops[-1]:
+            values = values + got
     for step in waiting:
         values = step(values)
     if not hops:
-        values = lax.psum(values, axis)
-    return values, stored["state"], stored["layer"], stored["running"]
+        values, got = lax.psum(values, axis), jnp.zeros_like(values)
+    norm = call(
+        functools.partial(norm_kernel, float(running.size * count)),
+        "norm",
+        [VEC] * 2,
+        jax.ShapeDtypeStruct((1, 1), F32),
+        VEC,
+        [],
+        in_vmem(values, got),
+        1,
+    )
+    return norm.reshape(1), stored["state"], stored["layer"], stored["running"]
 
 
 def body(
@@ -761,57 +807,59 @@
     last_inside = lax.ppermute(later_inside, "gx", pair_inside)
     early_pairs, late_pairs = halves(pair_across)
     last_across = lax.ppermute(later_across, "gx", early_pairs)
-    later_across, got_across = lax.optimization_barrier((later_across, got_across))
-    last_late = lax.ppermute(later_across, "gx", late_pairs)
-
     out_types = [
         held(*wave_state.shape), held(*layer_fields.shape), held(*filtered.shape)
     ]
-    next_state, next_layer, next_filtered, ghost, partial = call(
+    edge_type = held(2 * REACH, ny, nz)
+    side_scratch = [vec(2 * REACH, ny, nz)] * 3 + [vec(5, ny, nz)] + [vec(2 * REACH, ny, nz)] * 2
+    later_across, got_inside = lax.optimization_barrier((later_across, got_inside))
+    last_late = lax.ppermute(later_across, "gx", late_pairs)
+    first, second, run = in_vmem(first, second, run)
+    next_state, next_layer, next_filtered, ext, ghost_inside = call(
+        inside_kernel,
+        "inner_half",
+        [VEC] * 8,
+        out_types + [edge_type, held(*strip)],
+        [VEC] * 5,
+        side_scratch,
+        (*in_vmem(got_inside), coef, clock, wave, running, edge, second, run),
+        1.5,
+    )
+    next_state, next_layer, next_filtered, ext, ghost_across, partial = call(
         joint_kernel,
         "joint",
-        [VEC] * 11,
-        out_types + [held(2 * REACH, ny, nz), held(BLK, nz)],
-        [VEC] * 5,
-        [
-            vec(4 * REACH, ny, nz),
-            vec(4 * REACH, ny, nz),
-            vec(4 * REACH, ny, nz),
-            vec(2, 5, ny, nz),
-            vec(*brick),
-            vec(*brick),
-            vec(4 * REACH, ny, nz),
-            vec(4 * REACH, ny, nz),
-        ],
+        [VEC] * 14,
+        out_types + [edge_type, held(*strip), held(BLK, nz)],
+        [VEC] * 6,
+        [vec(*brick), vec(*brick), *side_scratch],
         (
-            coef, clock, *in_vmem(got_inside, got_across), wave, forcing, running, edge,
-            *in_vmem(first, second, run),
+            *in_vmem(got_across), coef, clock, wave, forcing, running, edge, first, second, run,
+            *in_vmem(next_state, next_layer, next_filtered, ext),
         ),
         5,
+        {10: 0, 11: 1, 12: 2, 13: 3},
     )
     next_state, next_layer, next_filtered, total = call(
         finish_kernel,
         "finish",
-        [VEC] * 10,
+        [VEC] * 11,
         out_types + [held(BLK, nz)],
         [VEC] * 4,
         [],
         (
             coef, clock,
             *in_vmem(
-                last_inside, last_across, last_late, ghost, partial,
+                last_inside, last_across, last_late, ghost_inside, ghost_across, partial,
                 next_state, next_layer, next_filtered,
             ),
         ),
         1,
-        {7: 0, 8: 1, 9: 2},
-    )
-    total, next_state, next_layer, next_filtered = total_and_stores(
+        {8: 0, 9: 1, 10: 2},
+    )
+    filter_norm, next_state, next_layer, next_filtered = norm_and_stores(
         total, next_state, next_layer, next_filtered, "gx"
     )
-    total = jnp.sum(total)
-    filter_norm = jnp.sqrt(total / (filtered.size * count) + 1e-06)
-    return next_state, next_layer, next_filtered, filter_norm.reshape(1)
+    return next_state, next_layer, next_filtered, filter_norm
 
 
 def solution(mesh):

time: 40.6 us -> 38.4 us (0.946)
  between operations: 3.87 us -> 2.06 us
  Pallas kernels: 14.6 us -> 16 us
  waiting for transfers between devices: 2.5 us -> 1.85 us
  other arithmetic: 0.61 us -> 0.01 us
  starting transfers between devices: 18.7 us -> 18.2 us
    ppermute x1, starting transfers between devices: 0.09 us -> 5.19 us  [body(): last_inside = lax.ppermute(later_inside, 'gx', pair_inside)]
    ppermute x1, starting transfers between devices: 4.37 us -> 0.52 us  [body(): got_inside = lax.ppermute(inside, 'gx', pair_inside)]
    ppermute x4, starting transfers between devices: 12.2 us -> 10.5 us  [norm_and_stores(): got = lax.ppermute(values, axis, [(i, i ^ hop) for i in range(count)])]
    pallas_call x7 -> x9, Pallas kernels: 14.6 us -> 16 us  [call(): pl.pallas_call(kernel, name=name, in_specs=in_specs, out_shape=out_shape,...]
    ppermute x4, waiting for transfers between devices: 2.49 us -> 1.83 us  [norm_and_stores(): got = lax.ppermute(values, axis, [(i, i ^ hop) for i in range(count)])]
    reduce_sum x1 -> x0, other arithmetic: 0.6 us -> none  [body(): total = jnp.sum(total)]
  transfers between devices with their start and end apart: 9 -> 9, of which waited for: 4 -> 4; matrix products, arithmetic and copies ran while one was open for 0% -> 0% of each run, Pallas kernels for 28% -> 31%
where the time goes in v4:
time: 38.4 us; the launch traced here: 38.1 us
  starting transfers between devices  18.2 us (47%)
  Pallas kernels  16 us (42%)
  between operations  2.06 us (5%)
  waiting for transfers between devices  1.85 us (5%)
    pallas_call x9, Pallas kernels, call(): pl.pallas_call(kernel, name=name, in_specs=in_specs, out_shape=out_shape,...  16 us
    ppermute x4, starting transfers between devices, norm_and_stores(): got = lax.ppermute(values, axis, [(i, i ^ hop) for i in range(count)])  10.5 us
    ppermute x1, starting transfers between devices, body(): last_inside = lax.ppermute(later_inside, 'gx', pair_inside)  5.19 us
    ppermute x4, waiting for transfers between devices, norm_and_stores(): got = lax.ppermute(values, axis, [(i, i ^ hop) for i in range(count)])  1.83 us
  transfers between devices with their start and end apart: 9, of which 4 were waited for; matrix products, arithmetic and copies ran while one was open for 0% of the time, Pallas kernels for 31%

profile of v4, /device:TPU:0, one launch (start us, length us, event | category | flops | bytes accessed | tf_op | source)
XLA Modules:
  0.0 38.1 jit_solution(15324549157640093924)
XLA Ops:
  1.9 2.8 %strips.1 = (f32[800,128]{1,0:T(8,128)S(1)}, f32[800,128]{1,0:T(8,128)S(1)}, f32[14,2,96,128]{3,2,1,0:T(8,128)S(1)}, f32[6,8,128]{2,1,0:T(8,128)S(1)}, f32[2,5,4...) custom-call(f32[2,16,96,128]{3,2,1,0:T(8,128)} %wave_in.1, ...), custom_call_target="tpu_custom_call" | custom-call | bytes 9000000 | tf_op jit(solution)/shard_map/strips/pallas_call | solution.py:658
  4.7 0.5 %collective-permute-start.2 = (f32[800,128]{1,0:T(8,128)S(1)}, f32[800,128]{1,0:T(8,128)S(1)}, u32[]{:S(2)}, u32[]{:S(2)}) collective-permute-start(f32[800,128]{1,0:T(8,128)S(1)} %get-tuple-element.48), channel_id=1, source_target_pairs={{0,1},{1,0},{2,3},{3,2},{4,5},{5,4},{6,7},{7,6},{8,9},{9,8},{10,11... | collective-permute-start | bytes 1228808 | tf_op jit(solution)/shard_map/ppermute | solution.py:788
  5.3 0.7 %collective-permute-start.4 = (f32[800,128]{1,0:T(8,128)S(1)}, f32[800,128]{1,0:T(8,128)S(1)}, u32[]{:S(2)}, u32[]{:S(2)}) collective-permute-start(f32[800,128]{1,0:T(8,128)S(1)} %get-tuple-element.54), channel_id=1, source_target_pairs={{1,2},{2,1},{3,4},{4,3},{5,6},{6,5},{7,8},{8,7},{9,10},{10,9},{11,... | collective-permute-start | bytes 1228808 | tf_op jit(solution)/shard_map/ppermute | solution.py:789
  5.9 0.0 copy-start
  6.0 3.2 %local.1 = (f32[4,96,128]{2,1,0:T(8,128)S(1)}, f32[4,96,128]{2,1,0:T(8,128)S(1)}, f32[8,96,128]{2,1,0:T(8,128)S(1)}, f32[5,16,96,128]{3,2,1,0:T(8,128)S(1)}, f32[16,96,128]{2,1,0:T(8,128)S(1)}) custom-call(f32[2,16,96,128]{3,2,1,0:T(8,128)S(1)} %get-tuple-element.42.wave, f32[4,16,96,128]{3,2,1,0:T(8,128)S(1)} %get-tuple-element.43.layer, ...), custom_call_target="tpu_custom_call" | custom-call | bytes 14400000 | tf_op jit(solution)/shard_map/local/pallas_call | solution.py:658
  9.2 0.7 %collective-permute-start.1 = (f32[4,96,128]{2,1,0:T(8,128)S(1)}, f32[4,96,128]{2,1,0:T(8,128)S(1)}, u32[]{:S(2)}, u32[]{:S(2)}) collective-permute-start(f32[4,96,128]{2,1,0:T(8,128)S(1)} %get-tuple-element.49), channel_id=1, source_target_pairs={{1,2},{2,1},{5,6},{6,5},{9,10},{10,9},{13,14},{14,13},{17,18},{18,... | collective-permute-start | bytes 589832 | tf_op jit(solution)/shard_map/ppermute | solution.py:809
  9.9 5.2 %collective-permute-start = (f32[4,96,128]{2,1,0:T(8,128)S(1)}, f32[4,96,128]{2,1,0:T(8,128)S(1)}, u32[]{:S(2)}, u32[]{:S(2)}) collective-permute-start(f32[4,96,128]{2,1,0:T(8,128)S(1)} %get-tuple-element.46), channel_id=1, source_target_pairs={{0,1},{1,0},{2,3},{3,2},{4,5},{5,4},{6,7},{7,6},{8,9},{9,8},{10,11... | collective-permute-start | bytes 589832 | tf_op jit(solution)/shard_map/ppermute | solution.py:807
  15.1 0.7 %collective-permute-start.3 = (f32[4,96,128]{2,1,0:T(8,128)S(1)}, f32[4,96,128]{2,1,0:T(8,128)S(1)}, u32[]{:S(2)}, u32[]{:S(2)}) collective-permute-start(f32[4,96,128]{2,1,0:T(8,128)S(1)} %get-tuple-element.49), channel_id=1, source_target_pairs={{3,4},{4,3},{7,8},{8,7},{11,12},{12,11},{19,20},{20,19},{23,24},{2... | collective-permute-start | bytes 589832 | tf_op jit(solution)/shard_map/ppermute | solution.py:816
  15.7 1.5 %inner_half.1 = (f32[2,16,96,128]{3,2,1,0:T(8,128)S(1)}, f32[4,16,96,128]{3,2,1,0:T(8,128)S(1)}, f32[16,96,128]{2,1,0:T(8,128)S(1)}, f32[8,96,128]{2,1,0:T(8,128)S(1)}, f32[4,96,128]{2,1,0:T(8,128)S(1)}) custom-call(f32[800,128]{1,0:T(8,128)S(1)} %collective-permute-done.2.inside, f32[14,2,96,128]{3,2,1,0:T(8,128)S(1)} %get-tuple-element.40.coef, ...), custom_call_target="tpu_custom_call" | custom-call | bytes 5400000 | tf_op jit(solution)/shard_map/inner_half/pallas_call | solution.py:658
  17.3 3.5 %joint.1 = (f32[2,16,96,128]{3,2,1,0:T(8,128)S(1)}, f32[4,16,96,128]{3,2,1,0:T(8,128)S(1)}, f32[16,96,128]{2,1,0:T(8,128)S(1)}, f32[8,96,128]{2,1,0:T(8,128)S(1)...) custom-call(f32[800,128]{1,0:T(8,128)S(1)} %collective-permute-done., ...), custom_call_target="tpu_custom_call", output_to_operand_aliasing={{0}: (10, {}), {1}: (11, {}), {2}: (12, {}), {3}: (13, {})} | custom-call | bytes 18000000 | tf_op jit(solution)/shard_map/joint/pallas_call | solution.py:658
  20.8 0.0 collective-permute-done.1.across
  20.8 0.6 %finish.1 = (f32[2,16,96,128]{3,2,1,0:T(8,128)S(1)}, f32[4,16,96,128]{3,2,1,0:T(8,128)S(1)}, f32[16,96,128]{2,1,0:T(8,128)S(1)}, f32[8,128]{1,0:T(8,128)S(1)}) custom-call(f32[14,2,96,128]{3,2,1,0:T(8,128)S(1)} %get-tuple-element.40.coef, f32[6,8,128]{2,1,0:T(8,128)S(1)} %get-tuple-element.41.clock, ...), custom_call_target="tpu_custom_call", output_to_operand_aliasing={{0}: (8, {}), {1}: (9, {}), {2}: (10, {})} | custom-call | bytes 3600000 | tf_op jit(solution)/shard_map/finish/pallas_call | solution.py:658
  21.4 2.5 %collective-permute-start.5 = (f32[8,128]{1,0:T(8,128)S(1)}, f32[8,128]{1,0:T(8,128)S(1)}, u32[]{:S(2)}, u32[]{:S(2)}) collective-permute-start(f32[8,128]{1,0:T(8,128)S(1)} %get-tuple-element.65), channel_id=1, source_target_pairs={{0,1},{1,0},{2,3},{3,2},{4,5},{5,4},{6,7},{7,6},{8,9},{9,8},{10,11... | collective-permute-start | bytes 12296 | tf_op jit(solution)/shard_map/ppermute | solution.py:724
  24.0 0.8 %collective-permute-done.5 = f32[8,128]{1,0:T(8,128)S(1)} collective-permute-done((f32[8,128]{1,0:T(8,128)S(1)}, f32[8,128]{1,0:T(8,128)S(1)}, u32[]{:S(2)}, u32[]{:S(2)}) %collective-permute-start.5) | collective-permute-done | bytes 4128 | tf_op jit(solution)/shard_map/ppermute | solution.py:724
  24.8 2.7 %collective-permute-start.6 = (f32[8,128]{1,0:T(8,128)S(1)}, f32[8,128]{1,0:T(8,128)S(1)}, u32[]{:S(2)}, u32[]{:S(2)}) collective-permute-start(f32[8,128]{1,0:T(8,128)S(1)} %add.9.values), channel_id=1, source_target_pairs={{0,2},{1,3},{2,0},{3,1},{4,6},{5,7},{6,4},{7,5},{8,10},{9,11},{10,... | collective-permute-start | bytes 12296 | tf_op jit(solution)/shard_map/ppermute | solution.py:724
  27.5 1.1 %store.3 = (f32[2,16,96,128]{3,2,1,0:T(8,128)}, f32[8,128]{1,0:T(8,128)S(1)}) custom-call(f32[8,128]{1,0:T(8,128)S(1)} %add.9.values, f32[2,16,96,128]{3,2,1,0:T(8,128)S(1)} %get-tuple-element.66.refs_0_), custom_call_target="tpu_custom_call" | custom-call | bytes 3600000 | tf_op jit(solution)/shard_map/store/pallas_call | solution.py:658
  28.7 0.4 %collective-permute-done.6 = f32[8,128]{1,0:T(8,128)S(1)} collective-permute-done((f32[8,128]{1,0:T(8,128)S(1)}, f32[8,128]{1,0:T(8,128)S(1)}, u32[]{:S(2)}, u32[]{:S(2)}) %collective-permute-start.6) | collective-permute-done | bytes 4128 | tf_op jit(solution)/shard_map/ppermute | solution.py:724
  29.1 2.2 %collective-permute-start.7 = (f32[8,128]{1,0:T(8,128)S(1)}, f32[8,128]{1,0:T(8,128)S(1)}, u32[]{:S(2)}, u32[]{:S(2)}) collective-permute-start(f32[8,128]{1,0:T(8,128)S(1)} %add.10.values), channel_id=1, source_target_pairs={{0,4},{1,5},{2,6},{3,7},{4,0},{5,1},{6,2},{7,3},{8,12},{9,13},{10,... | collective-permute-start | bytes 12296 | tf_op jit(solution)/shard_map/ppermute | solution.py:724
  31.3 1.1 %store.4 = (f32[4,16,96,128]{3,2,1,0:T(8,128)}, f32[8,128]{1,0:T(8,128)S(1)}) custom-call(f32[8,128]{1,0:T(8,128)S(1)} %add.10.values, f32[4,16,96,128]{3,2,1,0:T(8,128)S(1)} %get-tuple-element.69.refs_0_.refs_1_), custom_call_target="tpu_custom_call" | custom-call | bytes 3600000 | tf_op jit(solution)/shard_map/store/pallas_call | solution.py:658
  32.5 0.4 %collective-permute-done.7 = f32[8,128]{1,0:T(8,128)S(1)} collective-permute-done((f32[8,128]{1,0:T(8,128)S(1)}, f32[8,128]{1,0:T(8,128)S(1)}, u32[]{:S(2)}, u32[]{:S(2)}) %collective-permute-start.7) | collective-permute-done | bytes 4128 | tf_op jit(solution)/shard_map/ppermute | solution.py:724
  32.9 3.0 %collective-permute-start.8 = (f32[8,128]{1,0:T(8,128)S(1)}, f32[8,128]{1,0:T(8,128)S(1)}, u32[]{:S(2)}, u32[]{:S(2)}) collective-permute-start(f32[8,128]{1,0:T(8,128)S(1)} %add.11.values), channel_id=1, source_target_pairs={{0,8},{1,9},{2,10},{3,11},{4,12},{5,13},{6,14},{7,15},{8,0},{9,1},... | collective-permute-start | bytes 12296 | tf_op jit(solution)/shard_map/ppermute | solution.py:724
  36.0 1.4 %store.5 = (f32[16,96,128]{2,1,0:T(8,128)}, f32[4,16,96,128]{3,2,1,0:T(8,128)}, f32[8,128]{1,0:T(8,128)S(1)}) custom-call(f32[8,128]{1,0:T(8,128)S(1)} %add.11.values, f32[16,96,128]{2,1,0:T(8,128)S(1)} %get-tuple-element.71.refs_0_, f32[4,16,96,128]{3,2,1,0:T(8,128)S(1)} %get-tuple-element.69.refs_0_.refs_1_, ...), custom_call_target="tpu_custom_call", output_to_operand_aliasing={{1}: (3, {})} | custom-call | bytes 3600000 | tf_op jit(solution)/shard_map/store/pallas_call | solution.py:658
  37.4 0.2 collective-permute-done.8.got
  37.5 0.6 %norm.1 = f32[1,1]{1,0:T(1,128)} custom-call(f32[8,128]{1,0:T(8,128)S(1)} %get-tuple-element.75.values, f32[8,128]{1,0:T(8,128)S(1)} %collective-permute-done.8.got), custom_call_target="tpu_custom_call" | custom-call | bytes 3600000 | tf_op jit(solution)/shard_map/norm/pallas_call | solution.py:658
  (8 shorter events, 0.0 us)
Async XLA Ops:
  4.7 10.3 %collective-permute-start.2 = (f32[800,128]{1,0:T(8,128)S(1)}, f32[800,128]{1,0:T(8,128)S(1)}, u32[]{:S(2)}, u32[]{:S(2)}) collective-permute-start(f32[800,128]{1,0:T(8,128)S(1)} %get-tuple-element.48), channel_id=1, source_target_pairs={{0,1},{1,0},{2,3},{3,2},{4,5},{5,4},{6,7},{7,6},{8,9},{9,8},{10,11... | collective-permute-start | bytes 1228808 | tf_op jit(solution)/shard_map/ppermute | solution.py:788
  5.3 12.0 %collective-permute-start.4 = (f32[800,128]{1,0:T(8,128)S(1)}, f32[800,128]{1,0:T(8,128)S(1)}, u32[]{:S(2)}, u32[]{:S(2)}) collective-permute-start(f32[800,128]{1,0:T(8,128)S(1)} %get-tuple-element.54), channel_id=1, source_target_pairs={{1,2},{2,1},{3,4},{4,3},{5,6},{6,5},{7,8},{8,7},{9,10},{10,9},{11,... | collective-permute-start | bytes 1228808 | tf_op jit(solution)/shard_map/ppermute | solution.py:789
  5.9 9.8 %copy-start = (f32[16,96,128]{2,1,0:T(8,128)S(1)}, f32[16,96,128]{2,1,0:T(8,128)}, u32[]{:S(2)}) copy-start(f32[16,96,128]{2,1,0:T(8,128)} %running.3) | copy-start | bytes 2359300
  9.2 11.6 %collective-permute-start.1 = (f32[4,96,128]{2,1,0:T(8,128)S(1)}, f32[4,96,128]{2,1,0:T(8,128)S(1)}, u32[]{:S(2)}, u32[]{:S(2)}) collective-permute-start(f32[4,96,128]{2,1,0:T(8,128)S(1)} %get-tuple-element.49), channel_id=1, source_target_pairs={{1,2},{2,1},{5,6},{6,5},{9,10},{10,9},{13,14},{14,13},{17,18},{18,... | collective-permute-start | bytes 589832 | tf_op jit(solution)/shard_map/ppermute | solution.py:809
  9.9 10.9 %collective-permute-start = (f32[4,96,128]{2,1,0:T(8,128)S(1)}, f32[4,96,128]{2,1,0:T(8,128)S(1)}, u32[]{:S(2)}, u32[]{:S(2)}) collective-permute-start(f32[4,96,128]{2,1,0:T(8,128)S(1)} %get-tuple-element.46), channel_id=1, source_target_pairs={{0,1},{1,0},{2,3},{3,2},{4,5},{5,4},{6,7},{7,6},{8,9},{9,8},{10,11... | collective-permute-start | bytes 589832 | tf_op jit(solution)/shard_map/ppermute | solution.py:807
  15.1 5.7 %collective-permute-start.3 = (f32[4,96,128]{2,1,0:T(8,128)S(1)}, f32[4,96,128]{2,1,0:T(8,128)S(1)}, u32[]{:S(2)}, u32[]{:S(2)}) collective-permute-start(f32[4,96,128]{2,1,0:T(8,128)S(1)} %get-tuple-element.49), channel_id=1, source_target_pairs={{3,4},{4,3},{7,8},{8,7},{11,12},{12,11},{19,20},{20,19},{23,24},{2... | collective-permute-start | bytes 589832 | tf_op jit(solution)/shard_map/ppermute | solution.py:816
  21.4 3.4 %collective-permute-start.5 = (f32[8,128]{1,0:T(8,128)S(1)}, f32[8,128]{1,0:T(8,128)S(1)}, u32[]{:S(2)}, u32[]{:S(2)}) collective-permute-start(f32[8,128]{1,0:T(8,128)S(1)} %get-tuple-element.65), channel_id=1, source_target_pairs={{0,1},{1,0},{2,3},{3,2},{4,5},{5,4},{6,7},{7,6},{8,9},{9,8},{10,11... | collective-permute-start | bytes 12296 | tf_op jit(solution)/shard_map/ppermute | solution.py:724
  24.8 4.3 %collective-permute-start.6 = (f32[8,128]{1,0:T(8,128)S(1)}, f32[8,128]{1,0:T(8,128)S(1)}, u32[]{:S(2)}, u32[]{:S(2)}) collective-permute-start(f32[8,128]{1,0:T(8,128)S(1)} %add.9.values), channel_id=1, source_target_pairs={{0,2},{1,3},{2,0},{3,1},{4,6},{5,7},{6,4},{7,5},{8,10},{9,11},{10,... | collective-permute-start | bytes 12296 | tf_op jit(solution)/shard_map/ppermute | solution.py:724
  29.1 3.8 %collective-permute-start.7 = (f32[8,128]{1,0:T(8,128)S(1)}, f32[8,128]{1,0:T(8,128)S(1)}, u32[]{:S(2)}, u32[]{:S(2)}) collective-permute-start(f32[8,128]{1,0:T(8,128)S(1)} %add.10.values), channel_id=1, source_target_pairs={{0,4},{1,5},{2,6},{3,7},{4,0},{5,1},{6,2},{7,3},{8,12},{9,13},{10,... | collective-permute-start | bytes 12296 | tf_op jit(solution)/shard_map/ppermute | solution.py:724
  32.9 4.6 %collective-permute-start.8 = (f32[8,128]{1,0:T(8,128)S(1)}, f32[8,128]{1,0:T(8,128)S(1)}, u32[]{:S(2)}, u32[]{:S(2)}) collective-permute-start(f32[8,128]{1,0:T(8,128)S(1)} %add.11.values), channel_id=1, source_target_pairs={{0,8},{1,9},{2,10},{3,11},{4,12},{5,13},{6,14},{7,15},{8,0},{9,1},... | collective-permute-start | bytes 12296 | tf_op jit(solution)/shard_map/ppermute | solution.py:724

commit v5 on v4

--- a/solution.py
+++ b/solution.py
@@ -135,6 +135,29 @@
     return jnp.dot(tiles.astype(BF16), along, preferred_element_type=F32)
 
 
+def tag_places(rows, lanes):
+    return [
+        (number * lanes, first, min(BLK, rows - first))
+        for number, first in enumerate(range(0, rows, BLK))
+    ]
+
+
+def from_tag(tile, rows, lanes, nz):
+    number = len(tag_places(rows, lanes))
+    lane = lax.broadcasted_iota(jnp.int32, (nz, 2 * number * nz), 0)
+    col = lax.broadcasted_iota(jnp.int32, (nz, 2 * number * nz), 1)
+    along = (lane == col // nz * lanes + col % nz // BLK).astype(F32).astype(BF16)
+    high = tile.astype(BF16).astype(F32)
+    middle = (tile - high).astype(BF16).astype(F32)
+    split = jnp.concatenate([high, middle, tile - high - middle, jnp.zeros_like(tile)], axis=0)
+    wide = jnp.dot(split.astype(BF16), along, preferred_element_type=F32)
+    wide = wide[:BLK] + wide[BLK : 2 * BLK] + wide[2 * BLK : 3 * BLK]
+    columns = [wide[:, at * nz : (at + 1) * nz] for at in range(2 * number)]
+    return [
+        jnp.concatenate(columns[part * number : (part + 1) * number], axis=0) for part in range(2)
+    ]
+
+
 def squares(index, table):
     speed = jnp.zeros_like(index)
     for entry in range(table.shape[0]):
@@ -181,7 +204,7 @@
 def send_kernel(
     wave_in, layer_in, source_in, freq, start, table_in, index_in, mask_in,
     inside, across, coef, clock, edge, wave, layer, source,
-    diff_y, diff_z, tags, index, mask, table, sems,
+    diff_y, diff_z, tags, tag_tiles, index, mask, table, sems,
 ):
     _, nx, ny, nz = wave.shape
     n_block = nx // BLK
@@ -224,11 +247,22 @@
     for entry, value in enumerate(values):
         for block in range(n_block):
             down_second(coef, (entry, block), value[block * TAG_ROWS : (block + 1) * TAG_ROWS], ny)
-    for part, value in enumerate((square, masks)):
-        to = pl.ds(2 * REACH * ny + part * TAG_ROWS, TAG_ROWS)
-        left, right = value[:TAG_ROWS], value[rows - TAG_ROWS :]
-        inside[to] = jnp.where(even, right, left)
-        across[to] = jnp.where(even, left, right)
+    tag_tiles[...] = jnp.zeros_like(tag_tiles)
+    places = tag_places(index.shape[0], index.shape[2])
+    for side in range(2):
+        block = side * (n_block - 1)
+        speed = jnp.zeros(index.shape[::2], F32)
+        for entry in range(table.shape[0]):
+            speed = jnp.where(index[:, block] == entry, table[entry], speed)
+        for part, value in enumerate((speed * speed, mask[:, block].astype(F32))):
+            for lane, first, length in places:
+                lane += part * len(places) * value.shape[1]
+                tag_tiles[side, :length, lane : lane + value.shape[1]] = value[
+                    first : first + length
+                ]
+    to = pl.ds(2 * REACH * ny, BLK)
+    inside[to] = jnp.where(even, tag_tiles[1], tag_tiles[0])
+    across[to] = jnp.where(even, tag_tiles[0], tag_tiles[1])
     copies[0].wait()
     planes = edge_planes(nx)
     slot = {plane: number for number, plane in enumerate(planes)}
@@ -377,8 +411,9 @@
         return depth if depth >= 0 else REACH - 1 - depth
 
     tag_at = 2 * REACH * ny
-    square = message[pl.ds(tag_at, TAG_ROWS)] * present
-    values = coefficients(square, bits_of(message[pl.ds(tag_at + TAG_ROWS, TAG_ROWS)]))
+    tile = message[pl.ds(tag_at, BLK)]
+    square, masks = from_tag(tile, ny // BLK, nz // BLK, nz)
+    values = coefficients(square * present, bits_of(masks))
     for entry, value in enumerate(
         (
             values[KAPPA_R],
@@ -753,7 +788,7 @@
     pair_inside, pair_across = swap_pairs(count)
     brick = (nx, ny, nz)
     strip = (REACH, ny, nz)
-    message = (2 * REACH * ny + 2 * TAG_ROWS, nz)
+    message = (2 * REACH * ny + BLK, nz)
     dma = pltpu.SemaphoreType.DMA
     vec = lambda *shape: pltpu.VMEM(shape, F32)
 
@@ -774,6 +809,7 @@
             vec(2 * REACH, ny, nz),
             vec(2 * REACH, ny, nz),
             vec(2, n_block * TAG_ROWS, nz),
+            vec(2, BLK, nz),
             pltpu.VMEM(blocks, jnp.int32),
             pltpu.VMEM(blocks, jnp.int32),
             pltpu.SMEM(speed_table.shape, F32),

time: 38.4 us -> 38.2 us (level)
  starting transfers between devices: 18.2 us -> 17.6 us
    ppermute x4, starting transfers between devices: 10.5 us -> 9.84 us  [norm_and_stores(): got = lax.ppermute(values, axis, [(i, i ^ hop) for i in range(count)])]
  transfers between devices with their start and end apart: 9 -> 9, of which waited for: 4 -> 4; matrix products, arithmetic and copies ran while one was open for 0% -> 0% of each run, Pallas kernels for 31% -> 32%
where the time goes in v5:
time: 38.2 us; the launch traced here: 37.9 us
  starting transfers between devices  17.6 us (46%)
  Pallas kernels  16.3 us (43%)
  between operations  2.06 us (5%)
  waiting for transfers between devices  2 us (5%)
    pallas_call x9, Pallas kernels, call(): pl.pallas_call(kernel, name=name, in_specs=in_specs, out_shape=out_shape,...  16.3 us
    ppermute x4, starting transfers between devices, norm_and_stores(): got = lax.ppermute(values, axis, [(i, i ^ hop) for i in range(count)])  9.84 us
    ppermute x1, starting transfers between devices, body(): last_inside = lax.ppermute(later_inside, 'gx', pair_inside)  5.19 us
    ppermute x4, waiting for transfers between devices, norm_and_stores(): got = lax.ppermute(values, axis, [(i, i ^ hop) for i in range(count)])  1.98 us
  transfers between devices with their start and end apart: 9, of which 4 were waited for; matrix products, arithmetic and copies ran while one was open for 0% of the time, Pallas kernels for 32%

profile of v5, /device:TPU:0, one launch (start us, length us, event | category | flops | bytes accessed | tf_op | source)
XLA Modules:
  0.0 37.9 jit_solution(4445699904214447151)
XLA Ops:
  1.9 2.8 %strips.1 = (f32[776,128]{1,0:T(8,128)S(1)}, f32[776,128]{1,0:T(8,128)S(1)}, f32[14,2,96,128]{3,2,1,0:T(8,128)S(1)}, f32[6,8,128]{2,1,0:T(8,128)S(1)}, f32[2,5,4...) custom-call(f32[2,16,96,128]{3,2,1,0:T(8,128)} %wave_in.1, ...), custom_call_target="tpu_custom_call" | custom-call | bytes 9000000 | tf_op jit(solution)/shard_map/strips/pallas_call | solution.py:693
  4.7 0.5 %collective-permute-start.2 = (f32[776,128]{1,0:T(8,128)S(1)}, f32[776,128]{1,0:T(8,128)S(1)}, u32[]{:S(2)}, u32[]{:S(2)}) collective-permute-start(f32[776,128]{1,0:T(8,128)S(1)} %get-tuple-element.48), channel_id=1, source_target_pairs={{0,1},{1,0},{2,3},{3,2},{4,5},{5,4},{6,7},{7,6},{8,9},{9,8},{10,11... | collective-permute-start | bytes 1191944 | tf_op jit(solution)/shard_map/ppermute | solution.py:824
  5.3 0.7 %collective-permute-start.4 = (f32[776,128]{1,0:T(8,128)S(1)}, f32[776,128]{1,0:T(8,128)S(1)}, u32[]{:S(2)}, u32[]{:S(2)}) collective-permute-start(f32[776,128]{1,0:T(8,128)S(1)} %get-tuple-element.54), channel_id=1, source_target_pairs={{1,2},{2,1},{3,4},{4,3},{5,6},{6,5},{7,8},{8,7},{9,10},{10,9},{11,... | collective-permute-start | bytes 1191944 | tf_op jit(solution)/shard_map/ppermute | solution.py:825
  5.9 0.0 copy-start
  6.0 3.2 %local.1 = (f32[4,96,128]{2,1,0:T(8,128)S(1)}, f32[4,96,128]{2,1,0:T(8,128)S(1)}, f32[8,96,128]{2,1,0:T(8,128)S(1)}, f32[5,16,96,128]{3,2,1,0:T(8,128)S(1)}, f32[16,96,128]{2,1,0:T(8,128)S(1)}) custom-call(f32[2,16,96,128]{3,2,1,0:T(8,128)S(1)} %get-tuple-element.42.wave, f32[4,16,96,128]{3,2,1,0:T(8,128)S(1)} %get-tuple-element.43.layer, ...), custom_call_target="tpu_custom_call" | custom-call | bytes 14400000 | tf_op jit(solution)/shard_map/local/pallas_call | solution.py:693
  9.2 0.7 %collective-permute-start.1 = (f32[4,96,128]{2,1,0:T(8,128)S(1)}, f32[4,96,128]{2,1,0:T(8,128)S(1)}, u32[]{:S(2)}, u32[]{:S(2)}) collective-permute-start(f32[4,96,128]{2,1,0:T(8,128)S(1)} %get-tuple-element.49), channel_id=1, source_target_pairs={{1,2},{2,1},{5,6},{6,5},{9,10},{10,9},{13,14},{14,13},{17,18},{18,... | collective-permute-start | bytes 589832 | tf_op jit(solution)/shard_map/ppermute | solution.py:845
  9.9 5.2 %collective-permute-start = (f32[4,96,128]{2,1,0:T(8,128)S(1)}, f32[4,96,128]{2,1,0:T(8,128)S(1)}, u32[]{:S(2)}, u32[]{:S(2)}) collective-permute-start(f32[4,96,128]{2,1,0:T(8,128)S(1)} %get-tuple-element.46), channel_id=1, source_target_pairs={{0,1},{1,0},{2,3},{3,2},{4,5},{5,4},{6,7},{7,6},{8,9},{9,8},{10,11... | collective-permute-start | bytes 589832 | tf_op jit(solution)/shard_map/ppermute | solution.py:843
  15.1 0.0 collective-permute-done.2.inside
  15.1 0.7 %collective-permute-start.3 = (f32[4,96,128]{2,1,0:T(8,128)S(1)}, f32[4,96,128]{2,1,0:T(8,128)S(1)}, u32[]{:S(2)}, u32[]{:S(2)}) collective-permute-start(f32[4,96,128]{2,1,0:T(8,128)S(1)} %get-tuple-element.49), channel_id=1, source_target_pairs={{3,4},{4,3},{7,8},{8,7},{11,12},{12,11},{19,20},{20,19},{23,24},{2... | collective-permute-start | bytes 589832 | tf_op jit(solution)/shard_map/ppermute | solution.py:852
  15.7 1.6 %inner_half.1 = (f32[2,16,96,128]{3,2,1,0:T(8,128)S(1)}, f32[4,16,96,128]{3,2,1,0:T(8,128)S(1)}, f32[16,96,128]{2,1,0:T(8,128)S(1)}, f32[8,96,128]{2,1,0:T(8,128)S(1)}, f32[4,96,128]{2,1,0:T(8,128)S(1)}) custom-call(f32[776,128]{1,0:T(8,128)S(1)} %collective-permute-done.2.inside, f32[14,2,96,128]{3,2,1,0:T(8,128)S(1)} %get-tuple-element.40.coef, ...), custom_call_target="tpu_custom_call" | custom-call | bytes 5400000 | tf_op jit(solution)/shard_map/inner_half/pallas_call | solution.py:693
  17.4 3.6 %joint.1 = (f32[2,16,96,128]{3,2,1,0:T(8,128)S(1)}, f32[4,16,96,128]{3,2,1,0:T(8,128)S(1)}, f32[16,96,128]{2,1,0:T(8,128)S(1)}, f32[8,96,128]{2,1,0:T(8,128)S(1)...) custom-call(f32[776,128]{1,0:T(8,128)S(1)} %collective-permute-done., ...), custom_call_target="tpu_custom_call", output_to_operand_aliasing={{0}: (10, {}), {1}: (11, {}), {2}: (12, {}), {3}: (13, {})} | custom-call | bytes 18000000 | tf_op jit(solution)/shard_map/joint/pallas_call | solution.py:693
  21.1 0.6 %finish.1 = (f32[2,16,96,128]{3,2,1,0:T(8,128)S(1)}, f32[4,16,96,128]{3,2,1,0:T(8,128)S(1)}, f32[16,96,128]{2,1,0:T(8,128)S(1)}, f32[8,128]{1,0:T(8,128)S(1)}) custom-call(f32[14,2,96,128]{3,2,1,0:T(8,128)S(1)} %get-tuple-element.40.coef, f32[6,8,128]{2,1,0:T(8,128)S(1)} %get-tuple-element.41.clock, ...), custom_call_target="tpu_custom_call", output_to_operand_aliasing={{0}: (8, {}), {1}: (9, {}), {2}: (10, {})} | custom-call | bytes 3600000 | tf_op jit(solution)/shard_map/finish/pallas_call | solution.py:693
  21.7 1.5 %collective-permute-start.5 = (f32[8,128]{1,0:T(8,128)S(1)}, f32[8,128]{1,0:T(8,128)S(1)}, u32[]{:S(2)}, u32[]{:S(2)}) collective-permute-start(f32[8,128]{1,0:T(8,128)S(1)} %get-tuple-element.65), channel_id=1, source_target_pairs={{0,1},{1,0},{2,3},{3,2},{4,5},{5,4},{6,7},{7,6},{8,9},{9,8},{10,11... | collective-permute-start | bytes 12296 | tf_op jit(solution)/shard_map/ppermute | solution.py:759
  23.2 0.8 %collective-permute-done.5 = f32[8,128]{1,0:T(8,128)S(1)} collective-permute-done((f32[8,128]{1,0:T(8,128)S(1)}, f32[8,128]{1,0:T(8,128)S(1)}, u32[]{:S(2)}, u32[]{:S(2)}) %collective-permute-start.5) | collective-permute-done | bytes 4128 | tf_op jit(solution)/shard_map/ppermute | solution.py:759
  24.0 3.6 %collective-permute-start.6 = (f32[8,128]{1,0:T(8,128)S(1)}, f32[8,128]{1,0:T(8,128)S(1)}, u32[]{:S(2)}, u32[]{:S(2)}) collective-permute-start(f32[8,128]{1,0:T(8,128)S(1)} %add.9.values), channel_id=1, source_target_pairs={{0,2},{1,3},{2,0},{3,1},{4,6},{5,7},{6,4},{7,5},{8,10},{9,11},{10,... | collective-permute-start | bytes 12296 | tf_op jit(solution)/shard_map/ppermute | solution.py:759
  27.6 1.1 %store.3 = (f32[2,16,96,128]{3,2,1,0:T(8,128)}, f32[8,128]{1,0:T(8,128)S(1)}) custom-call(f32[8,128]{1,0:T(8,128)S(1)} %add.9.values, f32[2,16,96,128]{3,2,1,0:T(8,128)S(1)} %get-tuple-element.66.refs_0_), custom_call_target="tpu_custom_call" | custom-call | bytes 3600000 | tf_op jit(solution)/shard_map/store/pallas_call | solution.py:693
  28.8 0.4 %collective-permute-done.6 = f32[8,128]{1,0:T(8,128)S(1)} collective-permute-done((f32[8,128]{1,0:T(8,128)S(1)}, f32[8,128]{1,0:T(8,128)S(1)}, u32[]{:S(2)}, u32[]{:S(2)}) %collective-permute-start.6) | collective-permute-done | bytes 4128 | tf_op jit(solution)/shard_map/ppermute | solution.py:759
  29.2 1.9 %collective-permute-start.7 = (f32[8,128]{1,0:T(8,128)S(1)}, f32[8,128]{1,0:T(8,128)S(1)}, u32[]{:S(2)}, u32[]{:S(2)}) collective-permute-start(f32[8,128]{1,0:T(8,128)S(1)} %add.10.values), channel_id=1, source_target_pairs={{0,4},{1,5},{2,6},{3,7},{4,0},{5,1},{6,2},{7,3},{8,12},{9,13},{10,... | collective-permute-start | bytes 12296 | tf_op jit(solution)/shard_map/ppermute | solution.py:759
  31.1 1.1 %store.4 = (f32[4,16,96,128]{3,2,1,0:T(8,128)}, f32[8,128]{1,0:T(8,128)S(1)}) custom-call(f32[8,128]{1,0:T(8,128)S(1)} %add.10.values, f32[4,16,96,128]{3,2,1,0:T(8,128)S(1)} %get-tuple-element.69.refs_0_.refs_1_), custom_call_target="tpu_custom_call" | custom-call | bytes 3600000 | tf_op jit(solution)/shard_map/store/pallas_call | solution.py:693
  32.2 0.6 %collective-permute-done.7 = f32[8,128]{1,0:T(8,128)S(1)} collective-permute-done((f32[8,128]{1,0:T(8,128)S(1)}, f32[8,128]{1,0:T(8,128)S(1)}, u32[]{:S(2)}, u32[]{:S(2)}) %collective-permute-start.7) | collective-permute-done | bytes 4128 | tf_op jit(solution)/shard_map/ppermute | solution.py:759
  32.8 2.9 %collective-permute-start.8 = (f32[8,128]{1,0:T(8,128)S(1)}, f32[8,128]{1,0:T(8,128)S(1)}, u32[]{:S(2)}, u32[]{:S(2)}) collective-permute-start(f32[8,128]{1,0:T(8,128)S(1)} %add.11.values), channel_id=1, source_target_pairs={{0,8},{1,9},{2,10},{3,11},{4,12},{5,13},{6,14},{7,15},{8,0},{9,1},... | collective-permute-start | bytes 12296 | tf_op jit(solution)/shard_map/ppermute | solution.py:759
  35.7 1.4 %store.5 = (f32[16,96,128]{2,1,0:T(8,128)}, f32[4,16,96,128]{3,2,1,0:T(8,128)}, f32[8,128]{1,0:T(8,128)S(1)}) custom-call(f32[8,128]{1,0:T(8,128)S(1)} %add.11.values, f32[16,96,128]{2,1,0:T(8,128)S(1)} %get-tuple-element.71.refs_0_, f32[4,16,96,128]{3,2,1,0:T(8,128)S(1)} %get-tuple-element.69.refs_0_.refs_1_, ...), custom_call_target="tpu_custom_call", output_to_operand_aliasing={{1}: (3, {})} | custom-call | bytes 3600000 | tf_op jit(solution)/shard_map/store/pallas_call | solution.py:693
  37.1 0.2 collective-permute-done.8.got
  37.3 0.6 %norm.1 = f32[1,1]{1,0:T(1,128)} custom-call(f32[8,128]{1,0:T(8,128)S(1)} %get-tuple-element.75.values, f32[8,128]{1,0:T(8,128)S(1)} %collective-permute-done.8.got), custom_call_target="tpu_custom_call" | custom-call | bytes 3600000 | tf_op jit(solution)/shard_map/norm/pallas_call | solution.py:693
  (8 shorter events, 0.0 us)
Async XLA Ops:
  4.7 10.3 %collective-permute-start.2 = (f32[776,128]{1,0:T(8,128)S(1)}, f32[776,128]{1,0:T(8,128)S(1)}, u32[]{:S(2)}, u32[]{:S(2)}) collective-permute-start(f32[776,128]{1,0:T(8,128)S(1)} %get-tuple-element.48), channel_id=1, source_target_pairs={{0,1},{1,0},{2,3},{3,2},{4,5},{5,4},{6,7},{7,6},{8,9},{9,8},{10,11... | collective-permute-start | bytes 1191944 | tf_op jit(solution)/shard_map/ppermute | solution.py:824
  5.3 12.1 %collective-permute-start.4 = (f32[776,128]{1,0:T(8,128)S(1)}, f32[776,128]{1,0:T(8,128)S(1)}, u32[]{:S(2)}, u32[]{:S(2)}) collective-permute-start(f32[776,128]{1,0:T(8,128)S(1)} %get-tuple-element.54), channel_id=1, source_target_pairs={{1,2},{2,1},{3,4},{4,3},{5,6},{6,5},{7,8},{8,7},{9,10},{10,9},{11,... | collective-permute-start | bytes 1191944 | tf_op jit(solution)/shard_map/ppermute | solution.py:825
  5.9 9.8 %copy-start = (f32[16,96,128]{2,1,0:T(8,128)S(1)}, f32[16,96,128]{2,1,0:T(8,128)}, u32[]{:S(2)}) copy-start(f32[16,96,128]{2,1,0:T(8,128)} %running.3) | copy-start | bytes 2359300
  9.2 11.9 %collective-permute-start.1 = (f32[4,96,128]{2,1,0:T(8,128)S(1)}, f32[4,96,128]{2,1,0:T(8,128)S(1)}, u32[]{:S(2)}, u32[]{:S(2)}) collective-permute-start(f32[4,96,128]{2,1,0:T(8,128)S(1)} %get-tuple-element.49), channel_id=1, source_target_pairs={{1,2},{2,1},{5,6},{6,5},{9,10},{10,9},{13,14},{14,13},{17,18},{18,... | collective-permute-start | bytes 589832 | tf_op jit(solution)/shard_map/ppermute | solution.py:845
  9.9 11.2 %collective-permute-start = (f32[4,96,128]{2,1,0:T(8,128)S(1)}, f32[4,96,128]{2,1,0:T(8,128)S(1)}, u32[]{:S(2)}, u32[]{:S(2)}) collective-permute-start(f32[4,96,128]{2,1,0:T(8,128)S(1)} %get-tuple-element.46), channel_id=1, source_target_pairs={{0,1},{1,0},{2,3},{3,2},{4,5},{5,4},{6,7},{7,6},{8,9},{9,8},{10,11... | collective-permute-start | bytes 589832 | tf_op jit(solution)/shard_map/ppermute | solution.py:843
  15.1 6.0 %collective-permute-start.3 = (f32[4,96,128]{2,1,0:T(8,128)S(1)}, f32[4,96,128]{2,1,0:T(8,128)S(1)}, u32[]{:S(2)}, u32[]{:S(2)}) collective-permute-start(f32[4,96,128]{2,1,0:T(8,128)S(1)} %get-tuple-element.49), channel_id=1, source_target_pairs={{3,4},{4,3},{7,8},{8,7},{11,12},{12,11},{19,20},{20,19},{23,24},{2... | collective-permute-start | bytes 589832 | tf_op jit(solution)/shard_map/ppermute | solution.py:852
  21.7 2.3 %collective-permute-start.5 = (f32[8,128]{1,0:T(8,128)S(1)}, f32[8,128]{1,0:T(8,128)S(1)}, u32[]{:S(2)}, u32[]{:S(2)}) collective-permute-start(f32[8,128]{1,0:T(8,128)S(1)} %get-tuple-element.65), channel_id=1, source_target_pairs={{0,1},{1,0},{2,3},{3,2},{4,5},{5,4},{6,7},{7,6},{8,9},{9,8},{10,11... | collective-permute-start | bytes 12296 | tf_op jit(solution)/shard_map/ppermute | solution.py:759
  24.0 5.2 %collective-permute-start.6 = (f32[8,128]{1,0:T(8,128)S(1)}, f32[8,128]{1,0:T(8,128)S(1)}, u32[]{:S(2)}, u32[]{:S(2)}) collective-permute-start(f32[8,128]{1,0:T(8,128)S(1)} %add.9.values), channel_id=1, source_target_pairs={{0,2},{1,3},{2,0},{3,1},{4,6},{5,7},{6,4},{7,5},{8,10},{9,11},{10,... | collective-permute-start | bytes 12296 | tf_op jit(solution)/shard_map/ppermute | solution.py:759
  29.2 3.6 %collective-permute-start.7 = (f32[8,128]{1,0:T(8,128)S(1)}, f32[8,128]{1,0:T(8,128)S(1)}, u32[]{:S(2)}, u32[]{:S(2)}) collective-permute-start(f32[8,128]{1,0:T(8,128)S(1)} %add.10.values), channel_id=1, source_target_pairs={{0,4},{1,5},{2,6},{3,7},{4,0},{5,1},{6,2},{7,3},{8,12},{9,13},{10,... | collective-permute-start | bytes 12296 | tf_op jit(solution)/shard_map/ppermute | solution.py:759
  32.8 4.5 %collective-permute-start.8 = (f32[8,128]{1,0:T(8,128)S(1)}, f32[8,128]{1,0:T(8,128)S(1)}, u32[]{:S(2)}, u32[]{:S(2)}) collective-permute-start(f32[8,128]{1,0:T(8,128)S(1)} %add.11.values), channel_id=1, source_target_pairs={{0,8},{1,9},{2,10},{3,11},{4,12},{5,13},{6,14},{7,15},{8,0},{9,1},... | collective-permute-start | bytes 12296 | tf_op jit(solution)/shard_map/ppermute | solution.py:759

commit v6 on v5

--- a/solution.py
+++ b/solution.py
@@ -20,7 +20,7 @@
 WHOLE = (-14336.0, 8064.0, -1008.0, 128.0, -9.0)
 CENTRE_REST = 14.0 / SCALE
 TAG_ROWS = 16
-KAPPA, KAPPA_R, Q0, Q1, Q2, B0, B1, B2, DECAY, PAIR, AMP, BACK, STIFF, FORCE = range(14)
+KAPPA, KAPPA_R, Q0, Q1, Q2, B0, B1, B2, DECAY, PAIR, AMP, BACK, STIFF, FORCE, PUSH = range(15)
 N_COEF = 14
 VMEM_LIMIT = 30 * 1024 * 1024
 
@@ -85,7 +85,7 @@
     return total
 
 
-def advance(cells, previous, memory, stiff, forcing, diffs, co, phase):
+def advance(cells, previous, memory, stiff, forcing, diffs, co):
     rest = CENTRE_REST * cells
     diffs = [diffs[0], diffs[1] * (1.0 / SCALE) - rest, diffs[2] * (1.0 / SCALE) - rest]
     memory = [m + co(Q0 + d) * (diffs[d] - m) for d, m in enumerate(memory)]
@@ -96,9 +96,23 @@
         - co(BACK) * previous
         + co(KAPPA) * inner
         - co(STIFF) * stiff
-        - (co(FORCE) * phase) * forcing
+        - co(PUSH) * forcing
     )
     return new, memory, stiff
+
+
+def loaded(coef, block, at, phase):
+    have = {}
+
+    def get(entry):
+        if entry not in have:
+            if entry == PUSH:
+                have[entry] = coef[FORCE, block, at] * phase
+            else:
+                have[entry] = coef[entry, block, at]
+        return have[entry]
+
+    return get
 
 
 def coefficients(speed_square, bits):
@@ -190,7 +204,7 @@
         step(pl.multiple_of(block * BLK, BLK))
         return carry
 
-    lax.fori_loop(0, ny // BLK, one, 0)
+    lax.fori_loop(0, ny // BLK, one, 0, unroll=2)
 
 
 def is_even():
@@ -285,6 +299,7 @@
             reach = range(2 * REACH) if side == 0 else range(nx - 2 * REACH, nx)
             cells = {plane: wave[0, plane, at] for plane in reach}
             values = []
+            co = loaded(coef, block, at, phase)
             for number in range(REACH):
                 plane = edges[side] + number
                 new, memory, stiff = advance(
@@ -298,8 +313,7 @@
                         diff_y[slot[plane], at],
                         diff_z[slot[plane], at],
                     ],
-                    lambda entry, block=block: coef[entry, block, at],
-                    phase,
+                    co,
                 )
                 for entry, value in enumerate((new, *memory, stiff)):
                     edge[side, entry, number, at] = value
@@ -345,6 +359,7 @@
 
     def first(rows):
         at = pl.ds(rows, BLK)
+        co = [loaded(coef, block, at, clock[0]) for block in range(nx // BLK)]
         cells = {plane: wave[0, plane, at] for plane in range(nx)}
         for plane in middle:
             new, memory, stiff = advance(
@@ -354,8 +369,7 @@
                 layer[3, plane, at],
                 source[plane, at],
                 [first_diff(cells, plane), diff_y[plane, at], diff_z[plane, at]],
-                lambda entry, block=plane // BLK: coef[entry, block, at],
-                clock[0],
+                co[plane // BLK],
             )
             first_out[plane - REACH, at] = new
             for entry, value in enumerate((*memory, stiff)):
@@ -366,6 +380,7 @@
 
     def second(rows):
         at = pl.ds(rows, BLK)
+        co = [loaded(coef, block, at, clock[1]) for block in range(nx // BLK)]
         cells = {plane: read(0, plane, at) for plane in range(nx)}
         values = {}
         for plane in range(nx):
@@ -376,8 +391,7 @@
                 read(4, plane, at),
                 source[plane, at],
                 [first_diff(cells, plane), diff_y[plane, at], diff_z[plane, at]],
-                lambda entry, block=plane // BLK: coef[entry, block, at],
-                clock[1],
+                co[plane // BLK],
             )
             values[plane] = new
             for entry, value in enumerate((new, *memory, stiff)):
@@ -574,6 +588,7 @@
 
     def third(rows):
         at = pl.ds(rows, BLK)
+        co = [loaded(coef, block, at, clock[2]) for block in range(nx // BLK)]
         cells = {plane: out_state[1, plane, at] for plane in range(nx)}
         total = partial[...]
         for plane in range(nx):
@@ -592,8 +607,7 @@
                 fields[3],
                 forcing[plane, at],
                 [first_diff(cells, plane), diff_y[plane, at], diff_z[plane, at]],
-                lambda entry, block=plane // BLK: coef[entry, block, at],
-                clock[2],
+                co[plane // BLK],
             )
             done = out_filtered[plane, at] + weights[2] * value
             for d in range(3):
@@ -609,7 +623,7 @@
 
 
 def finish_kernel(
-    coef, clock, inside, across, across_late, ghost_inside, ghost_across, partial,
+    coef, clock, across, inside, across_late, ghost_inside, ghost_across, partial,
     state_in, layer_in, filtered_in,
     out_state, out_layer, out_filtered, total_out,
 ):
@@ -885,7 +899,7 @@
         (
             coef, clock,
             *in_vmem(
-                last_inside, last_across, last_late, ghost_inside, ghost_across, partial,
+                last_across, last_inside, last_late, ghost_inside, ghost_across, partial,
                 next_state, next_layer, next_filtered,
             ),
         ),

time: 38.2 us -> 38 us (level)
  Pallas kernels: 16.3 us -> 15.3 us
  starting transfers between devices: 17.6 us -> 18.6 us
    pallas_call x9, Pallas kernels: 16.3 us -> 15.3 us  [call(): pl.pallas_call(kernel, name=name, in_specs=in_specs, out_shape=out_shape,...]
    ppermute x4, starting transfers between devices: 9.84 us -> 10.8 us  [norm_and_stores(): got = lax.ppermute(values, axis, [(i, i ^ hop) for i in range(count)])]
  transfers between devices with their start and end apart: 9 -> 9, of which waited for: 4 -> 4; matrix products, arithmetic and copies ran while one was open for 0% -> 0% of each run, Pallas kernels for 32% -> 30%
where the time goes in v6:
time: 38 us; the launch traced here: 37.7 us
  starting transfers between devices  18.6 us (49%)
  Pallas kernels  15.3 us (40%)
  between operations  2.06 us (5%)
  waiting for transfers between devices  1.85 us (5%)
    pallas_call x9, Pallas kernels, call(): pl.pallas_call(kernel, name=name, in_specs=in_specs, out_shape=out_shape,...  15.3 us
    ppermute x4, starting transfers between devices, norm_and_stores(): got = lax.ppermute(values, axis, [(i, i ^ hop) for i in range(count)])  10.8 us
    ppermute x1, starting transfers between devices, body(): last_inside = lax.ppermute(later_inside, 'gx', pair_inside)  5.19 us
    ppermute x4, waiting for transfers between devices, norm_and_stores(): got = lax.ppermute(values, axis, [(i, i ^ hop) for i in range(count)])  1.83 us
  transfers between devices with their start and end apart: 9, of which 4 were waited for; matrix products, arithmetic and copies ran while one was open for 0% of the time, Pallas kernels for 30%

profile of v6, /device:TPU:0, one launch (start us, length us, event | category | flops | bytes accessed | tf_op | source)
XLA Modules:
  0.0 37.7 jit_solution(7031596787164404955)
XLA Ops:
  1.9 2.8 %strips.1 = (f32[776,128]{1,0:T(8,128)S(1)}, f32[776,128]{1,0:T(8,128)S(1)}, f32[14,2,96,128]{3,2,1,0:T(8,128)S(1)}, f32[6,8,128]{2,1,0:T(8,128)S(1)}, f32[2,5,4...) custom-call(f32[2,16,96,128]{3,2,1,0:T(8,128)} %wave_in.1, ...), custom_call_target="tpu_custom_call" | custom-call | bytes 9000000 | tf_op jit(solution)/shard_map/strips/pallas_call | solution.py:707
  4.7 0.5 %collective-permute-start.2 = (f32[776,128]{1,0:T(8,128)S(1)}, f32[776,128]{1,0:T(8,128)S(1)}, u32[]{:S(2)}, u32[]{:S(2)}) collective-permute-start(f32[776,128]{1,0:T(8,128)S(1)} %get-tuple-element.48), channel_id=1, source_target_pairs={{0,1},{1,0},{2,3},{3,2},{4,5},{5,4},{6,7},{7,6},{8,9},{9,8},{10,11... | collective-permute-start | bytes 1191944 | tf_op jit(solution)/shard_map/ppermute | solution.py:838
  5.2 0.7 %collective-permute-start.4 = (f32[776,128]{1,0:T(8,128)S(1)}, f32[776,128]{1,0:T(8,128)S(1)}, u32[]{:S(2)}, u32[]{:S(2)}) collective-permute-start(f32[776,128]{1,0:T(8,128)S(1)} %get-tuple-element.54), channel_id=1, source_target_pairs={{1,2},{2,1},{3,4},{4,3},{5,6},{6,5},{7,8},{8,7},{9,10},{10,9},{11,... | collective-permute-start | bytes 1191944 | tf_op jit(solution)/shard_map/ppermute | solution.py:839
  5.9 0.0 copy-start
  5.9 3.0 %local.1 = (f32[4,96,128]{2,1,0:T(8,128)S(1)}, f32[4,96,128]{2,1,0:T(8,128)S(1)}, f32[8,96,128]{2,1,0:T(8,128)S(1)}, f32[5,16,96,128]{3,2,1,0:T(8,128)S(1)}, f32[16,96,128]{2,1,0:T(8,128)S(1)}) custom-call(f32[2,16,96,128]{3,2,1,0:T(8,128)S(1)} %get-tuple-element.42.wave, f32[4,16,96,128]{3,2,1,0:T(8,128)S(1)} %get-tuple-element.43.layer, ...), custom_call_target="tpu_custom_call" | custom-call | bytes 14400000 | tf_op jit(solution)/shard_map/local/pallas_call | solution.py:707
  8.9 0.7 %collective-permute-start = (f32[4,96,128]{2,1,0:T(8,128)S(1)}, f32[4,96,128]{2,1,0:T(8,128)S(1)}, u32[]{:S(2)}, u32[]{:S(2)}) collective-permute-start(f32[4,96,128]{2,1,0:T(8,128)S(1)} %get-tuple-element.49), channel_id=1, source_target_pairs={{1,2},{2,1},{5,6},{6,5},{9,10},{10,9},{13,14},{14,13},{17,18},{18,... | collective-permute-start | bytes 589832 | tf_op jit(solution)/shard_map/ppermute | solution.py:859
  9.5 5.2 %collective-permute-start.1 = (f32[4,96,128]{2,1,0:T(8,128)S(1)}, f32[4,96,128]{2,1,0:T(8,128)S(1)}, u32[]{:S(2)}, u32[]{:S(2)}) collective-permute-start(f32[4,96,128]{2,1,0:T(8,128)S(1)} %get-tuple-element.47), channel_id=1, source_target_pairs={{0,1},{1,0},{2,3},{3,2},{4,5},{5,4},{6,7},{7,6},{8,9},{9,8},{10,11... | collective-permute-start | bytes 589832 | tf_op jit(solution)/shard_map/ppermute | solution.py:857
  14.7 0.0 collective-permute-done.2.inside
  14.7 0.7 %collective-permute-start.3 = (f32[4,96,128]{2,1,0:T(8,128)S(1)}, f32[4,96,128]{2,1,0:T(8,128)S(1)}, u32[]{:S(2)}, u32[]{:S(2)}) collective-permute-start(f32[4,96,128]{2,1,0:T(8,128)S(1)} %get-tuple-element.49), channel_id=1, source_target_pairs={{3,4},{4,3},{7,8},{8,7},{11,12},{12,11},{19,20},{20,19},{23,24},{2... | collective-permute-start | bytes 589832 | tf_op jit(solution)/shard_map/ppermute | solution.py:866
  15.4 1.4 %inner_half.1 = (f32[2,16,96,128]{3,2,1,0:T(8,128)S(1)}, f32[4,16,96,128]{3,2,1,0:T(8,128)S(1)}, f32[16,96,128]{2,1,0:T(8,128)S(1)}, f32[8,96,128]{2,1,0:T(8,128)S(1)}, f32[4,96,128]{2,1,0:T(8,128)S(1)}) custom-call(f32[776,128]{1,0:T(8,128)S(1)} %collective-permute-done.2.inside, f32[14,2,96,128]{3,2,1,0:T(8,128)S(1)} %get-tuple-element.40.coef, ...), custom_call_target="tpu_custom_call" | custom-call | bytes 5400000 | tf_op jit(solution)/shard_map/inner_half/pallas_call | solution.py:707
  16.8 3.3 %joint.1 = (f32[2,16,96,128]{3,2,1,0:T(8,128)S(1)}, f32[4,16,96,128]{3,2,1,0:T(8,128)S(1)}, f32[16,96,128]{2,1,0:T(8,128)S(1)}, f32[8,96,128]{2,1,0:T(8,128)S(1)...) custom-call(f32[776,128]{1,0:T(8,128)S(1)} %collective-permute-done., ...), custom_call_target="tpu_custom_call", output_to_operand_aliasing={{0}: (10, {}), {1}: (11, {}), {2}: (12, {}), {3}: (13, {})} | custom-call | bytes 18000000 | tf_op jit(solution)/shard_map/joint/pallas_call | solution.py:707
  20.2 0.5 %finish.1 = (f32[2,16,96,128]{3,2,1,0:T(8,128)S(1)}, f32[4,16,96,128]{3,2,1,0:T(8,128)S(1)}, f32[16,96,128]{2,1,0:T(8,128)S(1)}, f32[8,128]{1,0:T(8,128)S(1)}) custom-call(f32[14,2,96,128]{3,2,1,0:T(8,128)S(1)} %get-tuple-element.40.coef, f32[6,8,128]{2,1,0:T(8,128)S(1)} %get-tuple-element.41.clock, ...), custom_call_target="tpu_custom_call", output_to_operand_aliasing={{0}: (8, {}), {1}: (9, {}), {2}: (10, {})} | custom-call | bytes 3600000 | tf_op jit(solution)/shard_map/finish/pallas_call | solution.py:707
  20.7 2.9 %collective-permute-start.5 = (f32[8,128]{1,0:T(8,128)S(1)}, f32[8,128]{1,0:T(8,128)S(1)}, u32[]{:S(2)}, u32[]{:S(2)}) collective-permute-start(f32[8,128]{1,0:T(8,128)S(1)} %get-tuple-element.65), channel_id=1, source_target_pairs={{0,1},{1,0},{2,3},{3,2},{4,5},{5,4},{6,7},{7,6},{8,9},{9,8},{10,11... | collective-permute-start | bytes 12296 | tf_op jit(solution)/shard_map/ppermute | solution.py:773
  23.6 0.8 %collective-permute-done.5 = f32[8,128]{1,0:T(8,128)S(1)} collective-permute-done((f32[8,128]{1,0:T(8,128)S(1)}, f32[8,128]{1,0:T(8,128)S(1)}, u32[]{:S(2)}, u32[]{:S(2)}) %collective-permute-start.5) | collective-permute-done | bytes 4128 | tf_op jit(solution)/shard_map/ppermute | solution.py:773
  24.4 2.7 %collective-permute-start.6 = (f32[8,128]{1,0:T(8,128)S(1)}, f32[8,128]{1,0:T(8,128)S(1)}, u32[]{:S(2)}, u32[]{:S(2)}) collective-permute-start(f32[8,128]{1,0:T(8,128)S(1)} %add.9.values), channel_id=1, source_target_pairs={{0,2},{1,3},{2,0},{3,1},{4,6},{5,7},{6,4},{7,5},{8,10},{9,11},{10,... | collective-permute-start | bytes 12296 | tf_op jit(solution)/shard_map/ppermute | solution.py:773
  27.1 1.1 %store.3 = (f32[2,16,96,128]{3,2,1,0:T(8,128)}, f32[8,128]{1,0:T(8,128)S(1)}) custom-call(f32[8,128]{1,0:T(8,128)S(1)} %add.9.values, f32[2,16,96,128]{3,2,1,0:T(8,128)S(1)} %get-tuple-element.66.refs_0_), custom_call_target="tpu_custom_call" | custom-call | bytes 3600000 | tf_op jit(solution)/shard_map/store/pallas_call | solution.py:707
  28.3 0.4 %collective-permute-done.6 = f32[8,128]{1,0:T(8,128)S(1)} collective-permute-done((f32[8,128]{1,0:T(8,128)S(1)}, f32[8,128]{1,0:T(8,128)S(1)}, u32[]{:S(2)}, u32[]{:S(2)}) %collective-permute-start.6) | collective-permute-done | bytes 4128 | tf_op jit(solution)/shard_map/ppermute | solution.py:773
  28.7 2.2 %collective-permute-start.7 = (f32[8,128]{1,0:T(8,128)S(1)}, f32[8,128]{1,0:T(8,128)S(1)}, u32[]{:S(2)}, u32[]{:S(2)}) collective-permute-start(f32[8,128]{1,0:T(8,128)S(1)} %add.10.values), channel_id=1, source_target_pairs={{0,4},{1,5},{2,6},{3,7},{4,0},{5,1},{6,2},{7,3},{8,12},{9,13},{10,... | collective-permute-start | bytes 12296 | tf_op jit(solution)/shard_map/ppermute | solution.py:773
  30.9 1.1 %store.4 = (f32[4,16,96,128]{3,2,1,0:T(8,128)}, f32[8,128]{1,0:T(8,128)S(1)}) custom-call(f32[8,128]{1,0:T(8,128)S(1)} %add.10.values, f32[4,16,96,128]{3,2,1,0:T(8,128)S(1)} %get-tuple-element.69.refs_0_.refs_1_), custom_call_target="tpu_custom_call" | custom-call | bytes 3600000 | tf_op jit(solution)/shard_map/store/pallas_call | solution.py:707
  32.1 0.4 %collective-permute-done.7 = f32[8,128]{1,0:T(8,128)S(1)} collective-permute-done((f32[8,128]{1,0:T(8,128)S(1)}, f32[8,128]{1,0:T(8,128)S(1)}, u32[]{:S(2)}, u32[]{:S(2)}) %collective-permute-start.7) | collective-permute-done | bytes 4128 | tf_op jit(solution)/shard_map/ppermute | solution.py:773
  32.5 3.0 %collective-permute-start.8 = (f32[8,128]{1,0:T(8,128)S(1)}, f32[8,128]{1,0:T(8,128)S(1)}, u32[]{:S(2)}, u32[]{:S(2)}) collective-permute-start(f32[8,128]{1,0:T(8,128)S(1)} %add.11.values), channel_id=1, source_target_pairs={{0,8},{1,9},{2,10},{3,11},{4,12},{5,13},{6,14},{7,15},{8,0},{9,1},... | collective-permute-start | bytes 12296 | tf_op jit(solution)/shard_map/ppermute | solution.py:773
  35.5 1.4 %store.5 = (f32[16,96,128]{2,1,0:T(8,128)}, f32[4,16,96,128]{3,2,1,0:T(8,128)}, f32[8,128]{1,0:T(8,128)S(1)}) custom-call(f32[8,128]{1,0:T(8,128)S(1)} %add.11.values, f32[16,96,128]{2,1,0:T(8,128)S(1)} %get-tuple-element.71.refs_0_, f32[4,16,96,128]{3,2,1,0:T(8,128)S(1)} %get-tuple-element.69.refs_0_.refs_1_, ...), custom_call_target="tpu_custom_call", output_to_operand_aliasing={{1}: (3, {})} | custom-call | bytes 3600000 | tf_op jit(solution)/shard_map/store/pallas_call | solution.py:707
  37.0 0.2 collective-permute-done.8.got
  37.1 0.6 %norm.1 = f32[1,1]{1,0:T(1,128)} custom-call(f32[8,128]{1,0:T(8,128)S(1)} %get-tuple-element.75.values, f32[8,128]{1,0:T(8,128)S(1)} %collective-permute-done.8.got), custom_call_target="tpu_custom_call" | custom-call | bytes 3600000 | tf_op jit(solution)/shard_map/norm/pallas_call | solution.py:707
  (8 shorter events, 0.0 us)
Async XLA Ops:
  4.7 10.0 %collective-permute-start.2 = (f32[776,128]{1,0:T(8,128)S(1)}, f32[776,128]{1,0:T(8,128)S(1)}, u32[]{:S(2)}, u32[]{:S(2)}) collective-permute-start(f32[776,128]{1,0:T(8,128)S(1)} %get-tuple-element.48), channel_id=1, source_target_pairs={{0,1},{1,0},{2,3},{3,2},{4,5},{5,4},{6,7},{7,6},{8,9},{9,8},{10,11... | collective-permute-start | bytes 1191944 | tf_op jit(solution)/shard_map/ppermute | solution.py:838
  5.2 11.6 %collective-permute-start.4 = (f32[776,128]{1,0:T(8,128)S(1)}, f32[776,128]{1,0:T(8,128)S(1)}, u32[]{:S(2)}, u32[]{:S(2)}) collective-permute-start(f32[776,128]{1,0:T(8,128)S(1)} %get-tuple-element.54), channel_id=1, source_target_pairs={{1,2},{2,1},{3,4},{4,3},{5,6},{6,5},{7,8},{8,7},{9,10},{10,9},{11,... | collective-permute-start | bytes 1191944 | tf_op jit(solution)/shard_map/ppermute | solution.py:839
  5.9 9.5 %copy-start = (f32[16,96,128]{2,1,0:T(8,128)S(1)}, f32[16,96,128]{2,1,0:T(8,128)}, u32[]{:S(2)}) copy-start(f32[16,96,128]{2,1,0:T(8,128)} %running.3) | copy-start | bytes 2359300
  8.9 11.3 %collective-permute-start = (f32[4,96,128]{2,1,0:T(8,128)S(1)}, f32[4,96,128]{2,1,0:T(8,128)S(1)}, u32[]{:S(2)}, u32[]{:S(2)}) collective-permute-start(f32[4,96,128]{2,1,0:T(8,128)S(1)} %get-tuple-element.49), channel_id=1, source_target_pairs={{1,2},{2,1},{5,6},{6,5},{9,10},{10,9},{13,14},{14,13},{17,18},{18,... | collective-permute-start | bytes 589832 | tf_op jit(solution)/shard_map/ppermute | solution.py:859
  9.5 10.6 %collective-permute-start.1 = (f32[4,96,128]{2,1,0:T(8,128)S(1)}, f32[4,96,128]{2,1,0:T(8,128)S(1)}, u32[]{:S(2)}, u32[]{:S(2)}) collective-permute-start(f32[4,96,128]{2,1,0:T(8,128)S(1)} %get-tuple-element.47), channel_id=1, source_target_pairs={{0,1},{1,0},{2,3},{3,2},{4,5},{5,4},{6,7},{7,6},{8,9},{9,8},{10,11... | collective-permute-start | bytes 589832 | tf_op jit(solution)/shard_map/ppermute | solution.py:857
  14.7 5.4 %collective-permute-start.3 = (f32[4,96,128]{2,1,0:T(8,128)S(1)}, f32[4,96,128]{2,1,0:T(8,128)S(1)}, u32[]{:S(2)}, u32[]{:S(2)}) collective-permute-start(f32[4,96,128]{2,1,0:T(8,128)S(1)} %get-tuple-element.49), channel_id=1, source_target_pairs={{3,4},{4,3},{7,8},{8,7},{11,12},{12,11},{19,20},{20,19},{23,24},{2... | collective-permute-start | bytes 589832 | tf_op jit(solution)/shard_map/ppermute | solution.py:866
  20.7 3.7 %collective-permute-start.5 = (f32[8,128]{1,0:T(8,128)S(1)}, f32[8,128]{1,0:T(8,128)S(1)}, u32[]{:S(2)}, u32[]{:S(2)}) collective-permute-start(f32[8,128]{1,0:T(8,128)S(1)} %get-tuple-element.65), channel_id=1, source_target_pairs={{0,1},{1,0},{2,3},{3,2},{4,5},{5,4},{6,7},{7,6},{8,9},{9,8},{10,11... | collective-permute-start | bytes 12296 | tf_op jit(solution)/shard_map/ppermute | solution.py:773
  24.4 4.3 %collective-permute-start.6 = (f32[8,128]{1,0:T(8,128)S(1)}, f32[8,128]{1,0:T(8,128)S(1)}, u32[]{:S(2)}, u32[]{:S(2)}) collective-permute-start(f32[8,128]{1,0:T(8,128)S(1)} %add.9.values), channel_id=1, source_target_pairs={{0,2},{1,3},{2,0},{3,1},{4,6},{5,7},{6,4},{7,5},{8,10},{9,11},{10,... | collective-permute-start | bytes 12296 | tf_op jit(solution)/shard_map/ppermute | solution.py:773
  28.7 3.8 %collective-permute-start.7 = (f32[8,128]{1,0:T(8,128)S(1)}, f32[8,128]{1,0:T(8,128)S(1)}, u32[]{:S(2)}, u32[]{:S(2)}) collective-permute-start(f32[8,128]{1,0:T(8,128)S(1)} %add.10.values), channel_id=1, source_target_pairs={{0,4},{1,5},{2,6},{3,7},{4,0},{5,1},{6,2},{7,3},{8,12},{9,13},{10,... | collective-permute-start | bytes 12296 | tf_op jit(solution)/shard_map/ppermute | solution.py:773
  32.5 4.6 %collective-permute-start.8 = (f32[8,128]{1,0:T(8,128)S(1)}, f32[8,128]{1,0:T(8,128)S(1)}, u32[]{:S(2)}, u32[]{:S(2)}) collective-permute-start(f32[8,128]{1,0:T(8,128)S(1)} %add.11.values), channel_id=1, source_target_pairs={{0,8},{1,9},{2,10},{3,11},{4,12},{5,13},{6,14},{7,15},{8,0},{9,1},... | collective-permute-start | bytes 12296 | tf_op jit(solution)/shard_map/ppermute | solution.py:773

commit v7 on v6

--- a/solution.py
+++ b/solution.py
@@ -626,12 +626,13 @@
     coef, clock, across, inside, across_late, ghost_inside, ghost_across, partial,
     state_in, layer_in, filtered_in,
     out_state, out_layer, out_filtered, total_out,
+    gathered,
 ):
     _, nx, ny, _ = state_in.shape
     n_block = nx // BLK
     even = is_even()
     weight = clock[2 * STEPS - 1]
-    total_out[...] = partial[...]
+    gathered[...] = partial[...]
     ghosts = (range(-REACH, 0), range(nx, nx + REACH))
     owned = (range(REACH), range(nx - REACH, nx))
 
@@ -647,7 +648,7 @@
             halo[-REACH + number] = left + jnp.where(even, two, one)
             one, two = ghost_inside[number, at], ghost_across[number, at]
             halo[nx + number] = right + jnp.where(even, one, two)
-        total = total_out[...]
+        total = gathered[...]
         for side in range(2):
             block = side * (n_block - 1)
             kappa_r, q0 = coef[KAPPA_R, block, at], coef[Q0, block, at]
@@ -659,9 +660,10 @@
                 done = filtered_in[plane, at] + weight * added
                 out_filtered[plane, at] = done
                 total = total + done * done
-        total_out[...] = total
+        gathered[...] = total
 
     over_rows(ny, step)
+    total_out[...] = jnp.sum(gathered[...], axis=0, keepdims=True)
 
 
 def store_kernel(parts, values, *refs):
@@ -893,9 +895,9 @@
         finish_kernel,
         "finish",
         [VEC] * 11,
-        out_types + [held(BLK, nz)],
+        out_types + [held(1, nz)],
         [VEC] * 4,
-        [],
+        [vec(BLK, nz)],
         (
             coef, clock,
             *in_vmem(

time: 38 us -> 37.8 us (level)
  no operation moved by 1% of the time
where the time goes in v7:
time: 37.8 us; the launch traced here: 37.5 us
  starting transfers between devices  18.6 us (49%)
  Pallas kernels  15.3 us (40%)
  between operations  2.05 us (5%)
  waiting for transfers between devices  1.64 us (4%)
    pallas_call x9, Pallas kernels, call(): pl.pallas_call(kernel, name=name, in_specs=in_specs, out_shape=out_shape,...  15.3 us
    ppermute x4, starting transfers between devices, norm_and_stores(): got = lax.ppermute(values, axis, [(i, i ^ hop) for i in range(count)])  10.8 us
    ppermute x1, starting transfers between devices, body(): last_inside = lax.ppermute(later_inside, 'gx', pair_inside)  5.19 us
    ppermute x4, waiting for transfers between devices, norm_and_stores(): got = lax.ppermute(values, axis, [(i, i ^ hop) for i in range(count)])  1.63 us
  transfers between devices with their start and end apart: 9, of which 4 were waited for; matrix products, arithmetic and copies ran while one was open for 0% of the time, Pallas kernels for 30%

profile of v7, /device:TPU:0, one launch (start us, length us, event | category | flops | bytes accessed | tf_op | source)
XLA Modules:
  0.0 37.5 jit_solution(2092853497140293266)
XLA Ops:
  1.9 2.8 %strips.1 = (f32[776,128]{1,0:T(8,128)S(1)}, f32[776,128]{1,0:T(8,128)S(1)}, f32[14,2,96,128]{3,2,1,0:T(8,128)S(1)}, f32[6,8,128]{2,1,0:T(8,128)S(1)}, f32[2,5,4...) custom-call(f32[2,16,96,128]{3,2,1,0:T(8,128)} %wave_in.1, ...), custom_call_target="tpu_custom_call" | custom-call | bytes 9000000 | tf_op jit(solution)/shard_map/strips/pallas_call | solution.py:709
  4.7 0.5 %collective-permute-start.2 = (f32[776,128]{1,0:T(8,128)S(1)}, f32[776,128]{1,0:T(8,128)S(1)}, u32[]{:S(2)}, u32[]{:S(2)}) collective-permute-start(f32[776,128]{1,0:T(8,128)S(1)} %get-tuple-element.48), channel_id=1, source_target_pairs={{0,1},{1,0},{2,3},{3,2},{4,5},{5,4},{6,7},{7,6},{8,9},{9,8},{10,11... | collective-permute-start | bytes 1191944 | tf_op jit(solution)/shard_map/ppermute | solution.py:840
  5.2 0.7 %collective-permute-start.4 = (f32[776,128]{1,0:T(8,128)S(1)}, f32[776,128]{1,0:T(8,128)S(1)}, u32[]{:S(2)}, u32[]{:S(2)}) collective-permute-start(f32[776,128]{1,0:T(8,128)S(1)} %get-tuple-element.54), channel_id=1, source_target_pairs={{1,2},{2,1},{3,4},{4,3},{5,6},{6,5},{7,8},{8,7},{9,10},{10,9},{11,... | collective-permute-start | bytes 1191944 | tf_op jit(solution)/shard_map/ppermute | solution.py:841
  5.9 0.0 copy-start
  5.9 3.0 %local.1 = (f32[4,96,128]{2,1,0:T(8,128)S(1)}, f32[4,96,128]{2,1,0:T(8,128)S(1)}, f32[8,96,128]{2,1,0:T(8,128)S(1)}, f32[5,16,96,128]{3,2,1,0:T(8,128)S(1)}, f32[16,96,128]{2,1,0:T(8,128)S(1)}) custom-call(f32[2,16,96,128]{3,2,1,0:T(8,128)S(1)} %get-tuple-element.42.wave, f32[4,16,96,128]{3,2,1,0:T(8,128)S(1)} %get-tuple-element.43.layer, ...), custom_call_target="tpu_custom_call" | custom-call | bytes 14400000 | tf_op jit(solution)/shard_map/local/pallas_call | solution.py:709
  8.9 0.7 %collective-permute-start = (f32[4,96,128]{2,1,0:T(8,128)S(1)}, f32[4,96,128]{2,1,0:T(8,128)S(1)}, u32[]{:S(2)}, u32[]{:S(2)}) collective-permute-start(f32[4,96,128]{2,1,0:T(8,128)S(1)} %get-tuple-element.49), channel_id=1, source_target_pairs={{1,2},{2,1},{5,6},{6,5},{9,10},{10,9},{13,14},{14,13},{17,18},{18,... | collective-permute-start | bytes 589832 | tf_op jit(solution)/shard_map/ppermute | solution.py:861
  9.5 5.2 %collective-permute-start.1 = (f32[4,96,128]{2,1,0:T(8,128)S(1)}, f32[4,96,128]{2,1,0:T(8,128)S(1)}, u32[]{:S(2)}, u32[]{:S(2)}) collective-permute-start(f32[4,96,128]{2,1,0:T(8,128)S(1)} %get-tuple-element.47), channel_id=1, source_target_pairs={{0,1},{1,0},{2,3},{3,2},{4,5},{5,4},{6,7},{7,6},{8,9},{9,8},{10,11... | collective-permute-start | bytes 589832 | tf_op jit(solution)/shard_map/ppermute | solution.py:859
  14.7 0.0 collective-permute-done.2.inside
  14.7 0.7 %collective-permute-start.3 = (f32[4,96,128]{2,1,0:T(8,128)S(1)}, f32[4,96,128]{2,1,0:T(8,128)S(1)}, u32[]{:S(2)}, u32[]{:S(2)}) collective-permute-start(f32[4,96,128]{2,1,0:T(8,128)S(1)} %get-tuple-element.49), channel_id=1, source_target_pairs={{3,4},{4,3},{7,8},{8,7},{11,12},{12,11},{19,20},{20,19},{23,24},{2... | collective-permute-start | bytes 589832 | tf_op jit(solution)/shard_map/ppermute | solution.py:868
  15.4 1.4 %inner_half.1 = (f32[2,16,96,128]{3,2,1,0:T(8,128)S(1)}, f32[4,16,96,128]{3,2,1,0:T(8,128)S(1)}, f32[16,96,128]{2,1,0:T(8,128)S(1)}, f32[8,96,128]{2,1,0:T(8,128)S(1)}, f32[4,96,128]{2,1,0:T(8,128)S(1)}) custom-call(f32[776,128]{1,0:T(8,128)S(1)} %collective-permute-done.2.inside, f32[14,2,96,128]{3,2,1,0:T(8,128)S(1)} %get-tuple-element.40.coef, ...), custom_call_target="tpu_custom_call" | custom-call | bytes 5400000 | tf_op jit(solution)/shard_map/inner_half/pallas_call | solution.py:709
  16.8 3.3 %joint.1 = (f32[2,16,96,128]{3,2,1,0:T(8,128)S(1)}, f32[4,16,96,128]{3,2,1,0:T(8,128)S(1)}, f32[16,96,128]{2,1,0:T(8,128)S(1)}, f32[8,96,128]{2,1,0:T(8,128)S(1)...) custom-call(f32[776,128]{1,0:T(8,128)S(1)} %collective-permute-done., ...), custom_call_target="tpu_custom_call", output_to_operand_aliasing={{0}: (10, {}), {1}: (11, {}), {2}: (12, {}), {3}: (13, {})} | custom-call | bytes 18000000 | tf_op jit(solution)/shard_map/joint/pallas_call | solution.py:709
  20.2 0.6 %finish.1 = (f32[2,16,96,128]{3,2,1,0:T(8,128)S(1)}, f32[4,16,96,128]{3,2,1,0:T(8,128)S(1)}, f32[16,96,128]{2,1,0:T(8,128)S(1)}, f32[1,128]{1,0:T(1,128)S(1)}) custom-call(f32[14,2,96,128]{3,2,1,0:T(8,128)S(1)} %get-tuple-element.40.coef, f32[6,8,128]{2,1,0:T(8,128)S(1)} %get-tuple-element.41.clock, ...), custom_call_target="tpu_custom_call", output_to_operand_aliasing={{0}: (8, {}), {1}: (9, {}), {2}: (10, {})} | custom-call | bytes 3600000 | tf_op jit(solution)/shard_map/finish/pallas_call | solution.py:709
  20.7 2.9 %collective-permute-start.5 = (f32[1,128]{1,0:T(1,128)S(1)}, f32[1,128]{1,0:T(1,128)S(1)}, u32[]{:S(2)}, u32[]{:S(2)}) collective-permute-start(f32[1,128]{1,0:T(1,128)S(1)} %get-tuple-element.65), channel_id=1, source_target_pairs={{0,1},{1,0},{2,3},{3,2},{4,5},{5,4},{6,7},{7,6},{8,9},{9,8},{10,11... | collective-permute-start | bytes 1544 | tf_op jit(solution)/shard_map/ppermute | solution.py:775
  23.6 0.8 %collective-permute-done.5 = f32[1,128]{1,0:T(1,128)S(1)} collective-permute-done((f32[1,128]{1,0:T(1,128)S(1)}, f32[1,128]{1,0:T(1,128)S(1)}, u32[]{:S(2)}, u32[]{:S(2)}) %collective-permute-start.5) | collective-permute-done | bytes 544 | tf_op jit(solution)/shard_map/ppermute | solution.py:775
  24.4 2.7 %collective-permute-start.6 = (f32[1,128]{1,0:T(1,128)S(1)}, f32[1,128]{1,0:T(1,128)S(1)}, u32[]{:S(2)}, u32[]{:S(2)}) collective-permute-start(f32[1,128]{1,0:T(1,128)S(1)} %add.9.values), channel_id=1, source_target_pairs={{0,2},{1,3},{2,0},{3,1},{4,6},{5,7},{6,4},{7,5},{8,10},{9,11},{10,... | collective-permute-start | bytes 1544 | tf_op jit(solution)/shard_map/ppermute | solution.py:775
  27.1 1.1 %store.3 = (f32[2,16,96,128]{3,2,1,0:T(8,128)}, f32[1,128]{1,0:T(1,128)S(1)}) custom-call(f32[1,128]{1,0:T(1,128)S(1)} %add.9.values, f32[2,16,96,128]{3,2,1,0:T(8,128)S(1)} %get-tuple-element.66.refs_0_), custom_call_target="tpu_custom_call" | custom-call | bytes 3600000 | tf_op jit(solution)/shard_map/store/pallas_call | solution.py:709
  28.2 0.4 collective-permute-done.6
  28.6 2.3 %collective-permute-start.7 = (f32[1,128]{1,0:T(1,128)S(1)}, f32[1,128]{1,0:T(1,128)S(1)}, u32[]{:S(2)}, u32[]{:S(2)}) collective-permute-start(f32[1,128]{1,0:T(1,128)S(1)} %add.10.values), channel_id=1, source_target_pairs={{0,4},{1,5},{2,6},{3,7},{4,0},{5,1},{6,2},{7,3},{8,12},{9,13},{10,... | collective-permute-start | bytes 1544 | tf_op jit(solution)/shard_map/ppermute | solution.py:775
  30.9 1.1 %store.4 = (f32[4,16,96,128]{3,2,1,0:T(8,128)}, f32[1,128]{1,0:T(1,128)S(1)}) custom-call(f32[1,128]{1,0:T(1,128)S(1)} %add.10.values, f32[4,16,96,128]{3,2,1,0:T(8,128)S(1)} %get-tuple-element.69.refs_0_.refs_1_), custom_call_target="tpu_custom_call" | custom-call | bytes 3600000 | tf_op jit(solution)/shard_map/store/pallas_call | solution.py:709
  32.0 0.4 collective-permute-done.7
  32.4 3.0 %collective-permute-start.8 = (f32[1,128]{1,0:T(1,128)S(1)}, f32[1,128]{1,0:T(1,128)S(1)}, u32[]{:S(2)}, u32[]{:S(2)}) collective-permute-start(f32[1,128]{1,0:T(1,128)S(1)} %add.11.values), channel_id=1, source_target_pairs={{0,8},{1,9},{2,10},{3,11},{4,12},{5,13},{6,14},{7,15},{8,0},{9,1},... | collective-permute-start | bytes 1544 | tf_op jit(solution)/shard_map/ppermute | solution.py:775
  35.4 1.4 %store.5 = (f32[16,96,128]{2,1,0:T(8,128)}, f32[4,16,96,128]{3,2,1,0:T(8,128)}, f32[1,128]{1,0:T(1,128)S(1)}) custom-call(f32[1,128]{1,0:T(1,128)S(1)} %add.11.values, f32[16,96,128]{2,1,0:T(8,128)S(1)} %get-tuple-element.71.refs_0_, f32[4,16,96,128]{3,2,1,0:T(8,128)S(1)} %get-tuple-element.69.refs_0_.refs_1_, ...), custom_call_target="tpu_custom_call", output_to_operand_aliasing={{1}: (3, {})} | custom-call | bytes 3600000 | tf_op jit(solution)/shard_map/store/pallas_call | solution.py:709
  36.8 0.1 collective-permute-done.8.got
  36.9 0.6 %norm.1 = f32[1,1]{1,0:T(1,128)} custom-call(f32[1,128]{1,0:T(1,128)S(1)} %get-tuple-element.75.values, f32[1,128]{1,0:T(1,128)S(1)} %collective-permute-done.8.got), custom_call_target="tpu_custom_call" | custom-call | bytes 3600000 | tf_op jit(solution)/shard_map/norm/pallas_call | solution.py:709
  (8 shorter events, 0.0 us)
Async XLA Ops:
  4.7 10.0 %collective-permute-start.2 = (f32[776,128]{1,0:T(8,128)S(1)}, f32[776,128]{1,0:T(8,128)S(1)}, u32[]{:S(2)}, u32[]{:S(2)}) collective-permute-start(f32[776,128]{1,0:T(8,128)S(1)} %get-tuple-element.48), channel_id=1, source_target_pairs={{0,1},{1,0},{2,3},{3,2},{4,5},{5,4},{6,7},{7,6},{8,9},{9,8},{10,11... | collective-permute-start | bytes 1191944 | tf_op jit(solution)/shard_map/ppermute | solution.py:840
  5.2 11.6 %collective-permute-start.4 = (f32[776,128]{1,0:T(8,128)S(1)}, f32[776,128]{1,0:T(8,128)S(1)}, u32[]{:S(2)}, u32[]{:S(2)}) collective-permute-start(f32[776,128]{1,0:T(8,128)S(1)} %get-tuple-element.54), channel_id=1, source_target_pairs={{1,2},{2,1},{3,4},{4,3},{5,6},{6,5},{7,8},{8,7},{9,10},{10,9},{11,... | collective-permute-start | bytes 1191944 | tf_op jit(solution)/shard_map/ppermute | solution.py:841
  5.9 9.5 %copy-start = (f32[16,96,128]{2,1,0:T(8,128)S(1)}, f32[16,96,128]{2,1,0:T(8,128)}, u32[]{:S(2)}) copy-start(f32[16,96,128]{2,1,0:T(8,128)} %running.3) | copy-start | bytes 2359300
  8.9 11.3 %collective-permute-start = (f32[4,96,128]{2,1,0:T(8,128)S(1)}, f32[4,96,128]{2,1,0:T(8,128)S(1)}, u32[]{:S(2)}, u32[]{:S(2)}) collective-permute-start(f32[4,96,128]{2,1,0:T(8,128)S(1)} %get-tuple-element.49), channel_id=1, source_target_pairs={{1,2},{2,1},{5,6},{6,5},{9,10},{10,9},{13,14},{14,13},{17,18},{18,... | collective-permute-start | bytes 589832 | tf_op jit(solution)/shard_map/ppermute | solution.py:861
  9.5 10.6 %collective-permute-start.1 = (f32[4,96,128]{2,1,0:T(8,128)S(1)}, f32[4,96,128]{2,1,0:T(8,128)S(1)}, u32[]{:S(2)}, u32[]{:S(2)}) collective-permute-start(f32[4,96,128]{2,1,0:T(8,128)S(1)} %get-tuple-element.47), channel_id=1, source_target_pairs={{0,1},{1,0},{2,3},{3,2},{4,5},{5,4},{6,7},{7,6},{8,9},{9,8},{10,11... | collective-permute-start | bytes 589832 | tf_op jit(solution)/shard_map/ppermute | solution.py:859
  14.7 5.4 %collective-permute-start.3 = (f32[4,96,128]{2,1,0:T(8,128)S(1)}, f32[4,96,128]{2,1,0:T(8,128)S(1)}, u32[]{:S(2)}, u32[]{:S(2)}) collective-permute-start(f32[4,96,128]{2,1,0:T(8,128)S(1)} %get-tuple-element.49), channel_id=1, source_target_pairs={{3,4},{4,3},{7,8},{8,7},{11,12},{12,11},{19,20},{20,19},{23,24},{2... | collective-permute-start | bytes 589832 | tf_op jit(solution)/shard_map/ppermute | solution.py:868
  20.7 3.7 %collective-permute-start.5 = (f32[1,128]{1,0:T(1,128)S(1)}, f32[1,128]{1,0:T(1,128)S(1)}, u32[]{:S(2)}, u32[]{:S(2)}) collective-permute-start(f32[1,128]{1,0:T(1,128)S(1)} %get-tuple-element.65), channel_id=1, source_target_pairs={{0,1},{1,0},{2,3},{3,2},{4,5},{5,4},{6,7},{7,6},{8,9},{9,8},{10,11... | collective-permute-start | bytes 1544 | tf_op jit(solution)/shard_map/ppermute | solution.py:775
  24.4 4.2 %collective-permute-start.6 = (f32[1,128]{1,0:T(1,128)S(1)}, f32[1,128]{1,0:T(1,128)S(1)}, u32[]{:S(2)}, u32[]{:S(2)}) collective-permute-start(f32[1,128]{1,0:T(1,128)S(1)} %add.9.values), channel_id=1, source_target_pairs={{0,2},{1,3},{2,0},{3,1},{4,6},{5,7},{6,4},{7,5},{8,10},{9,11},{10,... | collective-permute-start | bytes 1544 | tf_op jit(solution)/shard_map/ppermute | solution.py:775
  28.6 3.8 %collective-permute-start.7 = (f32[1,128]{1,0:T(1,128)S(1)}, f32[1,128]{1,0:T(1,128)S(1)}, u32[]{:S(2)}, u32[]{:S(2)}) collective-permute-start(f32[1,128]{1,0:T(1,128)S(1)} %add.10.values), channel_id=1, source_target_pairs={{0,4},{1,5},{2,6},{3,7},{4,0},{5,1},{6,2},{7,3},{8,12},{9,13},{10,... | collective-permute-start | bytes 1544 | tf_op jit(solution)/shard_map/ppermute | solution.py:775
  32.4 4.6 %collective-permute-start.8 = (f32[1,128]{1,0:T(1,128)S(1)}, f32[1,128]{1,0:T(1,128)S(1)}, u32[]{:S(2)}, u32[]{:S(2)}) collective-permute-start(f32[1,128]{1,0:T(1,128)S(1)} %add.11.values), channel_id=1, source_target_pairs={{0,8},{1,9},{2,10},{3,11},{4,12},{5,13},{6,14},{7,15},{8,0},{9,1},... | collective-permute-start | bytes 1544 | tf_op jit(solution)/shard_map/ppermute | solution.py:775

commit v8 on v7

--- a/solution.py
+++ b/solution.py
@@ -204,7 +204,7 @@
         step(pl.multiple_of(block * BLK, BLK))
         return carry
 
-    lax.fori_loop(0, ny // BLK, one, 0, unroll=2)
+    lax.fori_loop(0, ny // BLK, one, 0, unroll=4)
 
 
 def is_even():

time: 37.8 us -> 37.7 us (level)
  Pallas kernels: 15.3 us -> 14.9 us
where the time goes in v8:
time: 37.7 us; the launch traced here: 37.5 us
  starting transfers between devices  18.8 us (50%)
  Pallas kernels  14.9 us (40%)
  between operations  2.05 us (5%)
  waiting for transfers between devices  1.64 us (4%)
    pallas_call x9, Pallas kernels, call(): pl.pallas_call(kernel, name=name, in_specs=in_specs, out_shape=out_shape,...  14.9 us
    ppermute x4, starting transfers between devices, norm_and_stores(): got = lax.ppermute(values, axis, [(i, i ^ hop) for i in range(count)])  11.1 us
    ppermute x1, starting transfers between devices, body(): last_inside = lax.ppermute(later_inside, 'gx', pair_inside)  5.19 us
    ppermute x4, waiting for transfers between devices, norm_and_stores(): got = lax.ppermute(values, axis, [(i, i ^ hop) for i in range(count)])  1.63 us
  transfers between devices with their start and end apart: 9, of which 4 were waited for; matrix products, arithmetic and copies ran while one was open for 0% of the time, Pallas kernels for 30%

profile of v8, /device:TPU:0, one launch (start us, length us, event | category | flops | bytes accessed | tf_op | source)
XLA Modules:
  0.0 37.5 jit_solution(9636646298105474457)
XLA Ops:
  1.9 2.7 %strips.1 = (f32[776,128]{1,0:T(8,128)S(1)}, f32[776,128]{1,0:T(8,128)S(1)}, f32[14,2,96,128]{3,2,1,0:T(8,128)S(1)}, f32[6,8,128]{2,1,0:T(8,128)S(1)}, f32[2,5,4...) custom-call(f32[2,16,96,128]{3,2,1,0:T(8,128)} %wave_in.1, ...), custom_call_target="tpu_custom_call" | custom-call | bytes 9000000 | tf_op jit(solution)/shard_map/strips/pallas_call | solution.py:709
  4.6 0.5 %collective-permute-start.2 = (f32[776,128]{1,0:T(8,128)S(1)}, f32[776,128]{1,0:T(8,128)S(1)}, u32[]{:S(2)}, u32[]{:S(2)}) collective-permute-start(f32[776,128]{1,0:T(8,128)S(1)} %get-tuple-element.48), channel_id=1, source_target_pairs={{0,1},{1,0},{2,3},{3,2},{4,5},{5,4},{6,7},{7,6},{8,9},{9,8},{10,11... | collective-permute-start | bytes 1191944 | tf_op jit(solution)/shard_map/ppermute | solution.py:840
  5.1 0.7 %collective-permute-start.4 = (f32[776,128]{1,0:T(8,128)S(1)}, f32[776,128]{1,0:T(8,128)S(1)}, u32[]{:S(2)}, u32[]{:S(2)}) collective-permute-start(f32[776,128]{1,0:T(8,128)S(1)} %get-tuple-element.54), channel_id=1, source_target_pairs={{1,2},{2,1},{3,4},{4,3},{5,6},{6,5},{7,8},{8,7},{9,10},{10,9},{11,... | collective-permute-start | bytes 1191944 | tf_op jit(solution)/shard_map/ppermute | solution.py:841
  5.8 0.0 copy-start
  5.8 2.9 %local.1 = (f32[4,96,128]{2,1,0:T(8,128)S(1)}, f32[4,96,128]{2,1,0:T(8,128)S(1)}, f32[8,96,128]{2,1,0:T(8,128)S(1)}, f32[5,16,96,128]{3,2,1,0:T(8,128)S(1)}, f32[16,96,128]{2,1,0:T(8,128)S(1)}) custom-call(f32[2,16,96,128]{3,2,1,0:T(8,128)S(1)} %get-tuple-element.42.wave, f32[4,16,96,128]{3,2,1,0:T(8,128)S(1)} %get-tuple-element.43.layer, ...), custom_call_target="tpu_custom_call" | custom-call | bytes 14400000 | tf_op jit(solution)/shard_map/local/pallas_call | solution.py:709
  8.7 0.7 %collective-permute-start = (f32[4,96,128]{2,1,0:T(8,128)S(1)}, f32[4,96,128]{2,1,0:T(8,128)S(1)}, u32[]{:S(2)}, u32[]{:S(2)}) collective-permute-start(f32[4,96,128]{2,1,0:T(8,128)S(1)} %get-tuple-element.49), channel_id=1, source_target_pairs={{1,2},{2,1},{5,6},{6,5},{9,10},{10,9},{13,14},{14,13},{17,18},{18,... | collective-permute-start | bytes 589832 | tf_op jit(solution)/shard_map/ppermute | solution.py:861
  9.4 5.2 %collective-permute-start.1 = (f32[4,96,128]{2,1,0:T(8,128)S(1)}, f32[4,96,128]{2,1,0:T(8,128)S(1)}, u32[]{:S(2)}, u32[]{:S(2)}) collective-permute-start(f32[4,96,128]{2,1,0:T(8,128)S(1)} %get-tuple-element.47), channel_id=1, source_target_pairs={{0,1},{1,0},{2,3},{3,2},{4,5},{5,4},{6,7},{7,6},{8,9},{9,8},{10,11... | collective-permute-start | bytes 589832 | tf_op jit(solution)/shard_map/ppermute | solution.py:859
  14.6 0.0 collective-permute-done.2.inside
  14.6 0.7 %collective-permute-start.3 = (f32[4,96,128]{2,1,0:T(8,128)S(1)}, f32[4,96,128]{2,1,0:T(8,128)S(1)}, u32[]{:S(2)}, u32[]{:S(2)}) collective-permute-start(f32[4,96,128]{2,1,0:T(8,128)S(1)} %get-tuple-element.49), channel_id=1, source_target_pairs={{3,4},{4,3},{7,8},{8,7},{11,12},{12,11},{19,20},{20,19},{23,24},{2... | collective-permute-start | bytes 589832 | tf_op jit(solution)/shard_map/ppermute | solution.py:868
  15.3 1.3 %inner_half.1 = (f32[2,16,96,128]{3,2,1,0:T(8,128)S(1)}, f32[4,16,96,128]{3,2,1,0:T(8,128)S(1)}, f32[16,96,128]{2,1,0:T(8,128)S(1)}, f32[8,96,128]{2,1,0:T(8,128)S(1)}, f32[4,96,128]{2,1,0:T(8,128)S(1)}) custom-call(f32[776,128]{1,0:T(8,128)S(1)} %collective-permute-done.2.inside, f32[14,2,96,128]{3,2,1,0:T(8,128)S(1)} %get-tuple-element.40.coef, ...), custom_call_target="tpu_custom_call" | custom-call | bytes 5400000 | tf_op jit(solution)/shard_map/inner_half/pallas_call | solution.py:709
  16.6 3.2 %joint.1 = (f32[2,16,96,128]{3,2,1,0:T(8,128)S(1)}, f32[4,16,96,128]{3,2,1,0:T(8,128)S(1)}, f32[16,96,128]{2,1,0:T(8,128)S(1)}, f32[8,96,128]{2,1,0:T(8,128)S(1)...) custom-call(f32[776,128]{1,0:T(8,128)S(1)} %collective-permute-done., ...), custom_call_target="tpu_custom_call", output_to_operand_aliasing={{0}: (10, {}), {1}: (11, {}), {2}: (12, {}), {3}: (13, {})} | custom-call | bytes 18000000 | tf_op jit(solution)/shard_map/joint/pallas_call | solution.py:709
  19.8 0.5 %finish.1 = (f32[2,16,96,128]{3,2,1,0:T(8,128)S(1)}, f32[4,16,96,128]{3,2,1,0:T(8,128)S(1)}, f32[16,96,128]{2,1,0:T(8,128)S(1)}, f32[1,128]{1,0:T(1,128)S(1)}) custom-call(f32[14,2,96,128]{3,2,1,0:T(8,128)S(1)} %get-tuple-element.40.coef, f32[6,8,128]{2,1,0:T(8,128)S(1)} %get-tuple-element.41.clock, ...), custom_call_target="tpu_custom_call", output_to_operand_aliasing={{0}: (8, {}), {1}: (9, {}), {2}: (10, {})} | custom-call | bytes 3600000 | tf_op jit(solution)/shard_map/finish/pallas_call | solution.py:709
  20.4 3.1 %collective-permute-start.5 = (f32[1,128]{1,0:T(1,128)S(1)}, f32[1,128]{1,0:T(1,128)S(1)}, u32[]{:S(2)}, u32[]{:S(2)}) collective-permute-start(f32[1,128]{1,0:T(1,128)S(1)} %get-tuple-element.65), channel_id=1, source_target_pairs={{0,1},{1,0},{2,3},{3,2},{4,5},{5,4},{6,7},{7,6},{8,9},{9,8},{10,11... | collective-permute-start | bytes 1544 | tf_op jit(solution)/shard_map/ppermute | solution.py:775
  23.5 0.8 %collective-permute-done.5 = f32[1,128]{1,0:T(1,128)S(1)} collective-permute-done((f32[1,128]{1,0:T(1,128)S(1)}, f32[1,128]{1,0:T(1,128)S(1)}, u32[]{:S(2)}, u32[]{:S(2)}) %collective-permute-start.5) | collective-permute-done | bytes 544 | tf_op jit(solution)/shard_map/ppermute | solution.py:775
  24.3 2.7 %collective-permute-start.6 = (f32[1,128]{1,0:T(1,128)S(1)}, f32[1,128]{1,0:T(1,128)S(1)}, u32[]{:S(2)}, u32[]{:S(2)}) collective-permute-start(f32[1,128]{1,0:T(1,128)S(1)} %add.9.values), channel_id=1, source_target_pairs={{0,2},{1,3},{2,0},{3,1},{4,6},{5,7},{6,4},{7,5},{8,10},{9,11},{10,... | collective-permute-start | bytes 1544 | tf_op jit(solution)/shard_map/ppermute | solution.py:775
  27.0 1.1 %store.3 = (f32[2,16,96,128]{3,2,1,0:T(8,128)}, f32[1,128]{1,0:T(1,128)S(1)}) custom-call(f32[1,128]{1,0:T(1,128)S(1)} %add.9.values, f32[2,16,96,128]{3,2,1,0:T(8,128)S(1)} %get-tuple-element.66.refs_0_), custom_call_target="tpu_custom_call" | custom-call | bytes 3600000 | tf_op jit(solution)/shard_map/store/pallas_call | solution.py:709
  28.2 0.4 collective-permute-done.6
  28.5 2.3 %collective-permute-start.7 = (f32[1,128]{1,0:T(1,128)S(1)}, f32[1,128]{1,0:T(1,128)S(1)}, u32[]{:S(2)}, u32[]{:S(2)}) collective-permute-start(f32[1,128]{1,0:T(1,128)S(1)} %add.10.values), channel_id=1, source_target_pairs={{0,4},{1,5},{2,6},{3,7},{4,0},{5,1},{6,2},{7,3},{8,12},{9,13},{10,... | collective-permute-start | bytes 1544 | tf_op jit(solution)/shard_map/ppermute | solution.py:775
  30.8 1.1 %store.4 = (f32[4,16,96,128]{3,2,1,0:T(8,128)}, f32[1,128]{1,0:T(1,128)S(1)}) custom-call(f32[1,128]{1,0:T(1,128)S(1)} %add.10.values, f32[4,16,96,128]{3,2,1,0:T(8,128)S(1)} %get-tuple-element.69.refs_0_.refs_1_), custom_call_target="tpu_custom_call" | custom-call | bytes 3600000 | tf_op jit(solution)/shard_map/store/pallas_call | solution.py:709
  32.0 0.4 collective-permute-done.7
  32.3 3.0 %collective-permute-start.8 = (f32[1,128]{1,0:T(1,128)S(1)}, f32[1,128]{1,0:T(1,128)S(1)}, u32[]{:S(2)}, u32[]{:S(2)}) collective-permute-start(f32[1,128]{1,0:T(1,128)S(1)} %add.11.values), channel_id=1, source_target_pairs={{0,8},{1,9},{2,10},{3,11},{4,12},{5,13},{6,14},{7,15},{8,0},{9,1},... | collective-permute-start | bytes 1544 | tf_op jit(solution)/shard_map/ppermute | solution.py:775
  35.4 1.4 %store.5 = (f32[16,96,128]{2,1,0:T(8,128)}, f32[4,16,96,128]{3,2,1,0:T(8,128)}, f32[1,128]{1,0:T(1,128)S(1)}) custom-call(f32[1,128]{1,0:T(1,128)S(1)} %add.11.values, f32[16,96,128]{2,1,0:T(8,128)S(1)} %get-tuple-element.71.refs_0_, f32[4,16,96,128]{3,2,1,0:T(8,128)S(1)} %get-tuple-element.69.refs_0_.refs_1_, ...), custom_call_target="tpu_custom_call", output_to_operand_aliasing={{1}: (3, {})} | custom-call | bytes 3600000 | tf_op jit(solution)/shard_map/store/pallas_call | solution.py:709
  36.8 0.1 collective-permute-done.8.got
  36.9 0.6 %norm.1 = f32[1,1]{1,0:T(1,128)} custom-call(f32[1,128]{1,0:T(1,128)S(1)} %get-tuple-element.75.values, f32[1,128]{1,0:T(1,128)S(1)} %collective-permute-done.8.got), custom_call_target="tpu_custom_call" | custom-call | bytes 3600000 | tf_op jit(solution)/shard_map/norm/pallas_call | solution.py:709
  (8 shorter events, 0.0 us)
Async XLA Ops:
  4.6 10.0 %collective-permute-start.2 = (f32[776,128]{1,0:T(8,128)S(1)}, f32[776,128]{1,0:T(8,128)S(1)}, u32[]{:S(2)}, u32[]{:S(2)}) collective-permute-start(f32[776,128]{1,0:T(8,128)S(1)} %get-tuple-element.48), channel_id=1, source_target_pairs={{0,1},{1,0},{2,3},{3,2},{4,5},{5,4},{6,7},{7,6},{8,9},{9,8},{10,11... | collective-permute-start | bytes 1191944 | tf_op jit(solution)/shard_map/ppermute | solution.py:840
  5.1 11.5 %collective-permute-start.4 = (f32[776,128]{1,0:T(8,128)S(1)}, f32[776,128]{1,0:T(8,128)S(1)}, u32[]{:S(2)}, u32[]{:S(2)}) collective-permute-start(f32[776,128]{1,0:T(8,128)S(1)} %get-tuple-element.54), channel_id=1, source_target_pairs={{1,2},{2,1},{3,4},{4,3},{5,6},{6,5},{7,8},{8,7},{9,10},{10,9},{11,... | collective-permute-start | bytes 1191944 | tf_op jit(solution)/shard_map/ppermute | solution.py:841
  5.8 9.4 %copy-start = (f32[16,96,128]{2,1,0:T(8,128)S(1)}, f32[16,96,128]{2,1,0:T(8,128)}, u32[]{:S(2)}) copy-start(f32[16,96,128]{2,1,0:T(8,128)} %running.3) | copy-start | bytes 2359300
  8.7 11.1 %collective-permute-start = (f32[4,96,128]{2,1,0:T(8,128)S(1)}, f32[4,96,128]{2,1,0:T(8,128)S(1)}, u32[]{:S(2)}, u32[]{:S(2)}) collective-permute-start(f32[4,96,128]{2,1,0:T(8,128)S(1)} %get-tuple-element.49), channel_id=1, source_target_pairs={{1,2},{2,1},{5,6},{6,5},{9,10},{10,9},{13,14},{14,13},{17,18},{18,... | collective-permute-start | bytes 589832 | tf_op jit(solution)/shard_map/ppermute | solution.py:861
  9.4 10.4 %collective-permute-start.1 = (f32[4,96,128]{2,1,0:T(8,128)S(1)}, f32[4,96,128]{2,1,0:T(8,128)S(1)}, u32[]{:S(2)}, u32[]{:S(2)}) collective-permute-start(f32[4,96,128]{2,1,0:T(8,128)S(1)} %get-tuple-element.47), channel_id=1, source_target_pairs={{0,1},{1,0},{2,3},{3,2},{4,5},{5,4},{6,7},{7,6},{8,9},{9,8},{10,11... | collective-permute-start | bytes 589832 | tf_op jit(solution)/shard_map/ppermute | solution.py:859
  14.6 5.2 %collective-permute-start.3 = (f32[4,96,128]{2,1,0:T(8,128)S(1)}, f32[4,96,128]{2,1,0:T(8,128)S(1)}, u32[]{:S(2)}, u32[]{:S(2)}) collective-permute-start(f32[4,96,128]{2,1,0:T(8,128)S(1)} %get-tuple-element.49), channel_id=1, source_target_pairs={{3,4},{4,3},{7,8},{8,7},{11,12},{12,11},{19,20},{20,19},{23,24},{2... | collective-permute-start | bytes 589832 | tf_op jit(solution)/shard_map/ppermute | solution.py:868
  20.4 4.0 %collective-permute-start.5 = (f32[1,128]{1,0:T(1,128)S(1)}, f32[1,128]{1,0:T(1,128)S(1)}, u32[]{:S(2)}, u32[]{:S(2)}) collective-permute-start(f32[1,128]{1,0:T(1,128)S(1)} %get-tuple-element.65), channel_id=1, source_target_pairs={{0,1},{1,0},{2,3},{3,2},{4,5},{5,4},{6,7},{7,6},{8,9},{9,8},{10,11... | collective-permute-start | bytes 1544 | tf_op jit(solution)/shard_map/ppermute | solution.py:775
  24.3 4.2 %collective-permute-start.6 = (f32[1,128]{1,0:T(1,128)S(1)}, f32[1,128]{1,0:T(1,128)S(1)}, u32[]{:S(2)}, u32[]{:S(2)}) collective-permute-start(f32[1,128]{1,0:T(1,128)S(1)} %add.9.values), channel_id=1, source_target_pairs={{0,2},{1,3},{2,0},{3,1},{4,6},{5,7},{6,4},{7,5},{8,10},{9,11},{10,... | collective-permute-start | bytes 1544 | tf_op jit(solution)/shard_map/ppermute | solution.py:775
  28.5 3.8 %collective-permute-start.7 = (f32[1,128]{1,0:T(1,128)S(1)}, f32[1,128]{1,0:T(1,128)S(1)}, u32[]{:S(2)}, u32[]{:S(2)}) collective-permute-start(f32[1,128]{1,0:T(1,128)S(1)} %add.10.values), channel_id=1, source_target_pairs={{0,4},{1,5},{2,6},{3,7},{4,0},{5,1},{6,2},{7,3},{8,12},{9,13},{10,... | collective-permute-start | bytes 1544 | tf_op jit(solution)/shard_map/ppermute | solution.py:775
  32.3 4.6 %collective-permute-start.8 = (f32[1,128]{1,0:T(1,128)S(1)}, f32[1,128]{1,0:T(1,128)S(1)}, u32[]{:S(2)}, u32[]{:S(2)}) collective-permute-start(f32[1,128]{1,0:T(1,128)S(1)} %add.11.values), channel_id=1, source_target_pairs={{0,8},{1,9},{2,10},{3,11},{4,12},{5,13},{6,14},{7,15},{8,0},{9,1},... | collective-permute-start | bytes 1544 | tf_op jit(solution)/shard_map/ppermute | solution.py:775
